TPU v7x, 32 devices: a whole 2x2x4 slice. The times are simulated.
32 devices in a mesh: groups: 2 (over y), row: 4 (over x, core), col: 4 (over z).
Axes of the slice: x: 2, y: 2, z: 4, core: 2. Of those that a mesh axis runs over, the one named last changes fastest.
Arguments:
- a_blocks: float32 [8, 4, 2, 384, 384], P(('groups', 'col'), 'row'), parts along dimension 0, may hold values from -0.3125 to 0.3125
- first_factor_cell_index: int32 [8, 4, 2], P(('groups', 'col'), 'row'), parts along dimension 0, may hold values from 0 to 48, as said below
- b_blocks: float32 [8, 4, 2, 384, 384], P(('groups', 'col'), 'row'), parts along dimension 0, may hold values from -6 to 6
- second_factor_cell_index: int32 [8, 4, 2], P(('groups', 'col'), 'row'), parts along dimension 0, may hold values from 0 to 48, as said below
- c_where: int32 [8, 4, 2], P(('groups', 'col'), 'row'), parts along dimension 0, may hold values from 0 to 48, as said below
Outputs:
- c_blocks: float32 [8, 4, 2, 384, 384], P(('groups', 'col'), 'row'), parts along dimension 0
There are 2 independent parts, one for each index of `groups`. A program takes and returns all parts, laid end to end along the dimension named above; each array names one. Nothing has to cross between parts.
Inputs may be any that keep to these rules, and one draw needn't show every extreme that they name: `first_factor_cell_index`: each value is a cell r * 7 + c of a 7 x 7 tile; the 2 cells of one tile are distinct. `second_factor_cell_index`: each value is a cell r * 7 + c of a 7 x 7 tile; the 2 cells of one tile are distinct. `c_where`: each value is a cell r * 7 + c of a 7 x 7 tile; the 2 cells of one tile are distinct.
All inputs are finite; a program needn't handle non-finite values.
Results may differ from a plain program's by a relative error of at most 0.0003.
Values sent between devices are 32-bit elements; how exact they have to be, the bound alone decides.
No kernel may reach another device: no remote copies, remote signals or barrier semaphores. Data moves between devices by JAX's collectives and lax.ppermute only.
A program may use at most 64 MiB of HBM per device.

v0:
```python
import jax
import jax.numpy as jnp
from jax import lax
from jax.sharding import PartitionSpec as P

TILE = 7
STEPS = 3


def from_behind(block, axis, distance):
    devices = range(lax.axis_size(axis))
    route = [((i - distance) % len(devices), i) for i in devices]
    return lax.ppermute(block, axis, route)


def choose(flag, shifted, current):
    return tuple(
        (jnp.where(flag, moved_part, kept_part) for moved_part, kept_part in zip(shifted, current))
    )


def multiply_add(accumulated, a_tile, a_cells, b_tile, b_cells, kept_cells):
    a_blockrow = a_cells // TILE
    a_inner = a_cells % TILE
    b_inner = b_cells // TILE
    b_blockcol = b_cells % TILE
    matching = a_inner[:, None] == b_inner[None, :]
    product_cell = a_blockrow[:, None] * TILE + b_blockcol[None, :]
    weights = (
        matching[:, :, None] & (product_cell[:, :, None] == kept_cells[None, None, :])
    ).astype(jnp.float32)
    products = jnp.einsum("axy,byz->abxz", a_tile, b_tile, precision=lax.Precision.HIGHEST)
    return accumulated + jnp.einsum(
        "abc,abxz->cxz", weights, products, precision=lax.Precision.HIGHEST
    )


def on_device(a_blocks, first_factor_cell_index, b_blocks, second_factor_cell_index, c_where):
    extent = lax.axis_size("row")
    row_place = lax.axis_index("row")
    col_place = lax.axis_index("col")
    kept_cells = c_where[0, 0]
    accumulated = jnp.zeros(a_blocks.shape[2:], jnp.float32)
    first_pair = (a_blocks, first_factor_cell_index)
    second_pair = (b_blocks, second_factor_cell_index)
    lag_first = (extent - col_place) % extent
    lag_second = (extent - row_place) % extent
    for bit_index in range((extent - 1).bit_length()):
        shifted = from_behind(first_pair, "row", 1 << bit_index)
        first_pair = choose(lag_first >> bit_index & 1 == 1, shifted, first_pair)
    for bit_index in range((extent - 1).bit_length()):
        shifted = from_behind(second_pair, "col", 1 << bit_index)
        second_pair = choose(lag_second >> bit_index & 1 == 1, shifted, second_pair)
    for turn_index in range(STEPS):
        accumulated = multiply_add(
            accumulated,
            first_pair[0][0, 0],
            first_pair[1][0, 0],
            second_pair[0][0, 0],
            second_pair[1][0, 0],
            kept_cells,
        )
        if turn_index + 1 < STEPS:
            first_pair = from_behind(first_pair, "row", -1)
            second_pair = from_behind(second_pair, "col", -1)
    return accumulated[None, None]


def solution(mesh):
    return jax.shard_map(
        on_device,
        mesh=mesh,
        in_specs=(
            P(("groups", "col"), "row", None, None, None),
            P(("groups", "col"), "row", None),
            P(("groups", "col"), "row", None, None, None),
            P(("groups", "col"), "row", None),
            P(("groups", "col"), "row", None),
        ),
        out_specs=P(("groups", "col"), "row", None, None, None),
        check_vma=False,
    )
```

profile of v0, /device:TPU:0, one launch (start us, length us, event | category | flops | bytes accessed | tf_op | source)
XLA Modules:
  0.0 179.2 jit_solution(17820772859960535709)
XLA Ops:
  0.5 2.6 %collective-permute-start.4 = (f32[1,1,2,384,384]{4,3,2,1,0:T(8,128)}, f32[1,1,2,384,384]{4,3,2,1,0:T(8,128)S(1)}, u32[]{:S(2)}, u32[]{:S(2)}) collective-permute-start(f32[1,1,2,384,384]{4,3,2,1,0:T(8,128)} %param.7), channel_id=1, source_target_pairs={{3,0},{0,1},{1,2},{2,3},{7,4},{4,5},{5,6},{6,7},{11,8},{8,9},{9,10... | collective-permute-start | bytes 3538952 | tf_op jit(solution)/shard_map/ppermute | solution.py:13
  3.0 1.6 collective-permute-start.2
  4.6 1.0 collective-permute-start
  5.6 25.6 %collective-permute-done.2 = s32[1,1,2]{2,1,0:T(1,128)S(1)} collective-permute-done((s32[1,1,2]{2,1,0:T(1,128)}, s32[1,1,2]{2,1,0:T(1,128)S(1)}, u32[]{:S(2)}, u32[]{:S(2)}) %collective-permute-start.2) | collective-permute-done | bytes 40 | tf_op jit(solution)/shard_map/ppermute | solution.py:13
  31.3 0.7 broadcast_select_fusion.4
  31.9 1.3 collective-permute-start.3
  33.2 0.7 broadcast_select_fusion.6
  33.9 1.8 collective-permute-start.1
  35.7 0.7 collective-permute-done.3
  36.4 2.4 %collective-permute-start.9 = (s32[1,1,2]{2,1,0:T(1,128)S(1)}, s32[1,1,2]{2,1,0:T(1,128)S(1)}, u32[]{:S(2)}, u32[]{:S(2)}) collective-permute-start(s32[1,1,2]{2,1,0:T(1,128)S(1)} %get-tuple-element.8), channel_id=1, source_target_pairs={{1,0},{2,1},{3,2},{0,3},{5,4},{6,5},{7,6},{4,7},{9,8},{10,9},{11,1... | collective-permute-start | bytes 32 | tf_op jit(solution)/shard_map/ppermute | solution.py:13
  38.9 1.5 broadcast_select_fusion
  40.4 1.8 %collective-permute-start.7 = (f32[1,1,2,384,384]{4,3,2,1,0:T(8,128)S(1)}, f32[1,1,2,384,384]{4,3,2,1,0:T(8,128)S(1)}, u32[]{:S(2)}, u32[]{:S(2)}) collective-permute-start(f32[1,1,2,384,384]{4,3,2,1,0:T(8,128)S(1)} %broadcast_select_fusion), channel_id=1, source_target_pairs={{8,0},{12,4},{0,8},{4,12},{9,1},{13,5},{1,9},{5,13},{10,2},{14,6},... | collective-permute-start | bytes 3538952 | tf_op jit(solution)/shard_map/ppermute | solution.py:13
  42.5 0.9 collective-permute-start.5
  43.4 0.6 broadcast_compare_fusion.2
  44.1 24.8 %collective-permute-done.7 = f32[1,1,2,384,384]{4,3,2,1,0:T(8,128)S(1)} collective-permute-done((f32[1,1,2,384,384]{4,3,2,1,0:T(8,128)S(1)}, f32[1,1,2,384,384]{4,3,2,1,0:T(8,128)S(1)}, u32[]{:S(2)}, u32[]{:S(2)}) %collective-permute-start.7) | collective-permute-done | bytes 1179680 | tf_op jit(solution)/shard_map/ppermute | solution.py:13
  69.0 1.1 collective-permute-start.11
  70.1 25.1 %collective-permute-done.5 = f32[1,1,2,384,384]{4,3,2,1,0:T(8,128)S(1)} collective-permute-done((f32[1,1,2,384,384]{4,3,2,1,0:T(8,128)S(1)}, f32[1,1,2,384,384]{4,3,2,1,0:T(8,128)S(1)}, u32[]{:S(2)}, u32[]{:S(2)}) %collective-permute-start.5) | collective-permute-done | bytes 1179680 | tf_op jit(solution)/shard_map/ppermute | solution.py:13
  95.2 0.8 collective-permute-start.10
  96.0 0.6 broadcast_compare_fusion.1
  97.4 25.9 %collective-permute-done.13 = s32[1,1,2]{2,1,0:T(1,128)S(1)} collective-permute-done((s32[1,1,2]{2,1,0:T(1,128)S(1)}, s32[1,1,2]{2,1,0:T(1,128)S(1)}, u32[]{:S(2)}, u32[]{:S(2)}) %collective-permute-start.13) | collective-permute-done | bytes 40 | tf_op jit(solution)/shard_map/ppermute | solution.py:13
  123.4 0.6 broadcast_compare_fusion
  124.2 2.0 %collective-permute-start.14 = (f32[1,1,2,384,384]{4,3,2,1,0:T(8,128)}, f32[1,1,2,384,384]{4,3,2,1,0:T(8,128)}, u32[]{:S(2)}, u32[]{:S(2)}) collective-permute-start(f32[1,1,2,384,384]{4,3,2,1,0:T(8,128)} %collective-permute-done.10), channel_id=1, source_target_pairs={{1,0},{2,1},{3,2},{0,3},{5,4},{6,5},{7,6},{4,7},{9,8},{10,9},{11,1... | collective-permute-start | bytes 3538952 | tf_op jit(solution)/shard_map/ppermute | solution.py:13
  126.2 6.0 %fusion.21 = f32[2,384,2,384]{3,1,2,0:T(8,128)S(1)} fusion(f32[1,1,2,384,384]{4,3,2,1,0:T(8,128)S(1)} %broadcast_select_fusion.1, f32[1,1,2,384,384]{4,3,2,1,0:T(8,128)S(1)} %broadcast_select_fusion.3), kind=kOutput, calls=%fused_computation.15 | convolution fusion | flops 2717908992 | bytes 4718592 | tf_op jit(solution)/shard_map/axy,byz->abxz/dot_general | solution.py:32
  132.2 3.4 %copy.8 = f32[2,384,2,384]{1,0,2,3:T(2,128)} copy(f32[2,384,2,384]{3,1,2,0:T(8,128)S(1)} %fusion.21) | data formatting | bytes 4718592 | tf_op jit(solution)/shard_map/axy,byz->abxz/dot_general | solution.py:32
  135.6 7.3 %fusion.6 = f32[2,384,384]{2,0,1:T(2,128)} fusion(f32[2,384,2,384]{1,0,2,3:T(2,128)} %copy.8, pred[2,2]{1,0:T(4,128)(4,1)} %broadcast_compare_fusion.2, s32[2,2]{1,0:T(2,128)S(1)} %broadcast_add_fusion.2, s32[2]{0:T(128)S(1)} %bitcast.148), kind=kOutput, calls=%fused_computation.6 | convolution fusion | flops 14155792 | bytes 3538972 | tf_op jit(solution)/shard_map/abc,abxz->cxz/dot_general | solution.py:33
  142.8 7.0 %fusion.18 = f32[2,384,2,384]{3,1,2,0:T(8,128)S(1)} fusion(f32[1,1,2,384,384]{4,3,2,1,0:T(8,128)S(1)} %collective-permute-done.11, f32[1,1,2,384,384]{4,3,2,1,0:T(8,128)} %collective-permute-done.10), kind=kOutput, calls=%fused_computation.12 | convolution fusion | flops 2717908992 | bytes 4718592 | tf_op jit(solution)/shard_map/axy,byz->abxz/dot_general | solution.py:32
  149.8 3.2 %copy.11 = f32[2,384,2,384]{1,0,2,3:T(2,128)} copy(f32[2,384,2,384]{3,1,2,0:T(8,128)S(1)} %fusion.18) | data formatting | bytes 4718592 | tf_op jit(solution)/shard_map/axy,byz->abxz/dot_general | solution.py:32
  153.1 7.3 %fusion.9 = f32[2,384,384]{2,0,1:T(2,128)} fusion(f32[2,384,2,384]{1,0,2,3:T(2,128)} %copy.11, pred[2,2]{1,0:T(4,128)(4,1)S(1)} %copy-done.2, s32[2,2]{1,0:T(2,128)S(1)} %broadcast_add_fusion.1, s32[2]{0:T(128)S(1)} %bitcast.149), kind=kOutput, calls=%fused_computation.7 | convolution fusion | flops 14155792 | bytes 3538972 | tf_op jit(solution)/shard_map/abc,abxz->cxz/dot_general | solution.py:33
  160.3 7.3 %fusion.15 = f32[2,384,2,384]{3,1,2,0:T(8,128)S(1)} fusion(f32[1,1,2,384,384]{4,3,2,1,0:T(8,128)} %collective-permute-done.15, f32[1,1,2,384,384]{4,3,2,1,0:T(8,128)} %collective-permute-done.14), kind=kOutput, calls=%fused_computation.9 | convolution fusion | flops 2717908992 | bytes 4718592 | tf_op jit(solution)/shard_map/axy,byz->abxz/dot_general | solution.py:32
  167.7 3.2 %copy.14 = f32[2,384,2,384]{1,0,2,3:T(2,128)} copy(f32[2,384,2,384]{3,1,2,0:T(8,128)S(1)} %fusion.15) | data formatting | bytes 4718592 | tf_op jit(solution)/shard_map/axy,byz->abxz/dot_general | solution.py:32
  170.9 7.2 %add_bitcast_fusion = f32[1,1,2,384,384]{4,2,3,1,0:T(2,128)S(1)} fusion(f32[2,384,384]{2,0,1:T(2,128)S(1)} %copy-done.4, f32[2,384,384]{2,0,1:T(2,128)} %fusion.9, f32[2,384,2,384]{1,0,2,3:T(2,128)} %copy.14, pred[2,2]{1,0:T(4,128)(4,1)S(1)} %copy-done.3, s32[2,2]{1,0:T(2,128)S(1)} %broadcast_add_fusion, s32[2]{0:T(128)S(1)} %bitcast.150), kind=kOutput, calls=%fused_computation.18 | convolution fusion | flops 14745616 | bytes 5898268 | tf_op jit(solution)/shard_map/abc,abxz->cxz/dot_general | solution.py:33
  178.1 1.1 copy.6
  (40 shorter events, 2.2 us)
Async XLA Ops:
  0.0 38.9 %collective-permute-start.6 = (f32[1,1,2,384,384]{4,3,2,1,0:T(8,128)}, f32[1,1,2,384,384]{4,3,2,1,0:T(8,128)S(1)}, u32[]{:S(2)}, u32[]{:S(2)}) collective-permute-start(f32[1,1,2,384,384]{4,3,2,1,0:T(8,128)} %param.5), channel_id=1, source_target_pairs={{12,0},{0,4},{4,8},{8,12},{13,1},{1,5},{5,9},{9,13},{14,2},{2,6},{... | collective-permute-start | bytes 3538952 | tf_op jit(solution)/shard_map/ppermute | solution.py:13
  0.5 41.8 %collective-permute-start.4 = (f32[1,1,2,384,384]{4,3,2,1,0:T(8,128)}, f32[1,1,2,384,384]{4,3,2,1,0:T(8,128)S(1)}, u32[]{:S(2)}, u32[]{:S(2)}) collective-permute-start(f32[1,1,2,384,384]{4,3,2,1,0:T(8,128)} %param.7), channel_id=1, source_target_pairs={{3,0},{0,1},{1,2},{2,3},{7,4},{4,5},{5,6},{6,7},{11,8},{8,9},{9,10... | collective-permute-start | bytes 3538952 | tf_op jit(solution)/shard_map/ppermute | solution.py:13
  3.0 28.2 %collective-permute-start.2 = (s32[1,1,2]{2,1,0:T(1,128)}, s32[1,1,2]{2,1,0:T(1,128)S(1)}, u32[]{:S(2)}, u32[]{:S(2)}) collective-permute-start(s32[1,1,2]{2,1,0:T(1,128)} %param.8), channel_id=1, source_target_pairs={{3,0},{0,1},{1,2},{2,3},{7,4},{4,5},{5,6},{6,7},{11,8},{8,9},{9,10... | collective-permute-start | bytes 32 | tf_op jit(solution)/shard_map/ppermute | solution.py:13
  4.6 28.6 %collective-permute-start = (s32[1,1,2]{2,1,0:T(1,128)}, s32[1,1,2]{2,1,0:T(1,128)S(1)}, u32[]{:S(2)}, u32[]{:S(2)}) collective-permute-start(s32[1,1,2]{2,1,0:T(1,128)} %param.6), channel_id=1, source_target_pairs={{12,0},{0,4},{4,8},{8,12},{13,1},{1,5},{5,9},{9,13},{14,2},{2,6},{... | collective-permute-start | bytes 32 | tf_op jit(solution)/shard_map/ppermute | solution.py:13
  31.9 4.4 %collective-permute-start.3 = (s32[1,1,2]{2,1,0:T(1,128)S(1)}, s32[1,1,2]{2,1,0:T(1,128)S(1)}, u32[]{:S(2)}, u32[]{:S(2)}) collective-permute-start(s32[1,1,2]{2,1,0:T(1,128)S(1)} %broadcast_select_fusion.4), channel_id=1, source_target_pairs={{2,0},{3,1},{0,2},{1,3},{6,4},{7,5},{4,6},{5,7},{10,8},{11,9},{8,1... | collective-permute-start | bytes 32 | tf_op jit(solution)/shard_map/ppermute | solution.py:13
  33.9 4.9 %collective-permute-start.1 = (s32[1,1,2]{2,1,0:T(1,128)S(1)}, s32[1,1,2]{2,1,0:T(1,128)S(1)}, u32[]{:S(2)}, u32[]{:S(2)}) collective-permute-start(s32[1,1,2]{2,1,0:T(1,128)S(1)} %broadcast_select_fusion.6), channel_id=1, source_target_pairs={{8,0},{12,4},{0,8},{4,12},{9,1},{13,5},{1,9},{5,13},{10,2},{14,6},... | collective-permute-start | bytes 32 | tf_op jit(solution)/shard_map/ppermute | solution.py:13
  36.4 7.7 %collective-permute-start.9 = (s32[1,1,2]{2,1,0:T(1,128)S(1)}, s32[1,1,2]{2,1,0:T(1,128)S(1)}, u32[]{:S(2)}, u32[]{:S(2)}) collective-permute-start(s32[1,1,2]{2,1,0:T(1,128)S(1)} %get-tuple-element.8), channel_id=1, source_target_pairs={{1,0},{2,1},{3,2},{0,3},{5,4},{6,5},{7,6},{4,7},{9,8},{10,9},{11,1... | collective-permute-start | bytes 32 | tf_op jit(solution)/shard_map/ppermute | solution.py:13
  38.8 5.3 %collective-permute-start.8 = (s32[1,1,2]{2,1,0:T(1,128)S(1)}, s32[1,1,2]{2,1,0:T(1,128)S(1)}, u32[]{:S(2)}, u32[]{:S(2)}) collective-permute-start(s32[1,1,2]{2,1,0:T(1,128)S(1)} %get-tuple-element.6), channel_id=1, source_target_pairs={{4,0},{8,4},{12,8},{0,12},{5,1},{9,5},{13,9},{1,13},{6,2},{10,6},{... | collective-permute-start | bytes 32 | tf_op jit(solution)/shard_map/ppermute | solution.py:13
  38.9 3.4 %copy-start = (f32[1,1,2,384,384]{4,3,2,1,0:T(8,128)S(1)}, f32[1,1,2,384,384]{4,3,2,1,0:T(8,128)}, u32[]{:S(2)}) copy-start(f32[1,1,2,384,384]{4,3,2,1,0:T(8,128)} %param.7) | copy-start | bytes 3538948
  40.4 28.5 %collective-permute-start.7 = (f32[1,1,2,384,384]{4,3,2,1,0:T(8,128)S(1)}, f32[1,1,2,384,384]{4,3,2,1,0:T(8,128)S(1)}, u32[]{:S(2)}, u32[]{:S(2)}) collective-permute-start(f32[1,1,2,384,384]{4,3,2,1,0:T(8,128)S(1)} %broadcast_select_fusion), channel_id=1, source_target_pairs={{8,0},{12,4},{0,8},{4,12},{9,1},{13,5},{1,9},{5,13},{10,2},{14,6},... | collective-permute-start | bytes 3538952 | tf_op jit(solution)/shard_map/ppermute | solution.py:13
  42.5 52.7 %collective-permute-start.5 = (f32[1,1,2,384,384]{4,3,2,1,0:T(8,128)S(1)}, f32[1,1,2,384,384]{4,3,2,1,0:T(8,128)S(1)}, u32[]{:S(2)}, u32[]{:S(2)}) collective-permute-start(f32[1,1,2,384,384]{4,3,2,1,0:T(8,128)S(1)} %broadcast_select_fusion.2), channel_id=1, source_target_pairs={{2,0},{3,1},{0,2},{1,3},{6,4},{7,5},{4,6},{5,7},{10,8},{11,9},{8,1... | collective-permute-start | bytes 3538952 | tf_op jit(solution)/shard_map/ppermute | solution.py:13
  69.0 55.1 %collective-permute-start.11 = (f32[1,1,2,384,384]{4,3,2,1,0:T(8,128)S(1)}, f32[1,1,2,384,384]{4,3,2,1,0:T(8,128)S(1)}, u32[]{:S(2)}, u32[]{:S(2)}) collective-permute-start(f32[1,1,2,384,384]{4,3,2,1,0:T(8,128)S(1)} %broadcast_select_fusion.1), channel_id=1, source_target_pairs={{4,0},{8,4},{12,8},{0,12},{5,1},{9,5},{13,9},{1,13},{6,2},{10,6},{... | collective-permute-start | bytes 3538952 | tf_op jit(solution)/shard_map/ppermute | solution.py:13
  95.2 29.0 %collective-permute-start.10 = (f32[1,1,2,384,384]{4,3,2,1,0:T(8,128)S(1)}, f32[1,1,2,384,384]{4,3,2,1,0:T(8,128)}, u32[]{:S(2)}, u32[]{:S(2)}) collective-permute-start(f32[1,1,2,384,384]{4,3,2,1,0:T(8,128)S(1)} %broadcast_select_fusion.3), channel_id=1, source_target_pairs={{1,0},{2,1},{3,2},{0,3},{5,4},{6,5},{7,6},{4,7},{9,8},{10,9},{11,1... | collective-permute-start | bytes 3538952 | tf_op jit(solution)/shard_map/ppermute | solution.py:13
  96.6 26.7 %collective-permute-start.13 = (s32[1,1,2]{2,1,0:T(1,128)S(1)}, s32[1,1,2]{2,1,0:T(1,128)S(1)}, u32[]{:S(2)}, u32[]{:S(2)}) collective-permute-start(s32[1,1,2]{2,1,0:T(1,128)S(1)} %collective-permute-done.9), channel_id=1, source_target_pairs={{1,0},{2,1},{3,2},{0,3},{5,4},{6,5},{7,6},{4,7},{9,8},{10,9},{11,1... | collective-permute-start | bytes 32 | tf_op jit(solution)/shard_map/ppermute | solution.py:13
  96.9 26.4 %collective-permute-start.12 = (s32[1,1,2]{2,1,0:T(1,128)S(1)}, s32[1,1,2]{2,1,0:T(1,128)S(1)}, u32[]{:S(2)}, u32[]{:S(2)}) collective-permute-start(s32[1,1,2]{2,1,0:T(1,128)S(1)} %collective-permute-done.8), channel_id=1, source_target_pairs={{4,0},{8,4},{12,8},{0,12},{5,1},{9,5},{13,9},{1,13},{6,2},{10,6},{... | collective-permute-start | bytes 32 | tf_op jit(solution)/shard_map/ppermute | solution.py:13
  124.1 36.3 %collective-permute-start.15 = (f32[1,1,2,384,384]{4,3,2,1,0:T(8,128)S(1)}, f32[1,1,2,384,384]{4,3,2,1,0:T(8,128)}, u32[]{:S(2)}, u32[]{:S(2)}) collective-permute-start(f32[1,1,2,384,384]{4,3,2,1,0:T(8,128)S(1)} %collective-permute-done.11), channel_id=1, source_target_pairs={{4,0},{8,4},{12,8},{0,12},{5,1},{9,5},{13,9},{1,13},{6,2},{10,6},{... | collective-permute-start | bytes 3538952 | tf_op jit(solution)/shard_map/ppermute | solution.py:13
  124.2 36.1 %collective-permute-start.14 = (f32[1,1,2,384,384]{4,3,2,1,0:T(8,128)}, f32[1,1,2,384,384]{4,3,2,1,0:T(8,128)}, u32[]{:S(2)}, u32[]{:S(2)}) collective-permute-start(f32[1,1,2,384,384]{4,3,2,1,0:T(8,128)} %collective-permute-done.10), channel_id=1, source_target_pairs={{1,0},{2,1},{3,2},{0,3},{5,4},{6,5},{7,6},{4,7},{9,8},{10,9},{11,1... | collective-permute-start | bytes 3538952 | tf_op jit(solution)/shard_map/ppermute | solution.py:13
  132.2 3.4 %copy-start.1 = (s32[1,1,2]{2,1,0:T(1,128)S(1)}, s32[1,1,2]{2,1,0:T(1,128)}, u32[]{:S(2)}) copy-start(s32[1,1,2]{2,1,0:T(1,128)} %param.9) | copy-start | bytes 28
  149.8 3.2 %copy-start.2 = (pred[2,2]{1,0:T(4,128)(4,1)S(1)}, pred[2,2]{1,0:T(4,128)(4,1)}, u32[]{:S(2)}) copy-start(pred[2,2]{1,0:T(4,128)(4,1)} %broadcast_compare_fusion.1) | copy-start | bytes 16
  167.7 3.2 %copy-start.3 = (pred[2,2]{1,0:T(4,128)(4,1)S(1)}, pred[2,2]{1,0:T(4,128)(4,1)}, u32[]{:S(2)}) copy-start(pred[2,2]{1,0:T(4,128)(4,1)} %broadcast_compare_fusion) | copy-start | bytes 16
  167.7 3.2 %copy-start.4 = (f32[2,384,384]{2,0,1:T(2,128)S(1)}, f32[2,384,384]{2,0,1:T(2,128)}, u32[]{:S(2)}) copy-start(f32[2,384,384]{2,0,1:T(2,128)} %fusion.6) | copy-start | bytes 3538948
where the time goes:
time: 179 us
  waiting for transfers between devices  102 us (57%)
  matrix products  42 us (23%)
  starting transfers between devices  18.6 us (10%)
  local copies, waits for them, and re-layouts  10.9 us (6%)
  other arithmetic  5.39 us (3%)
    ppermute x16, waiting for transfers between devices, from_behind(): return lax.ppermute(block, axis, route)  102 us
    dot_general x3, matrix products, multiply_add(): jnp.einsum('abc,abxz->cxz', weights, products, precision=lax.Precision.HI...  21.7 us
    dot_general x3, matrix products, multiply_add(): jnp.einsum('axy,byz->abxz', a_tile, b_tile, precision=lax.Precision.HIGHEST)  20.3 us
    ppermute x16, starting transfers between devices, from_behind(): return lax.ppermute(block, axis, route)  18.6 us
    dot_general x3, local copies, waits for them, and re-layouts, multiply_add(): jnp.einsum('axy,byz->abxz', a_tile, b_tile, precision=lax.Precision.HIGHEST)  9.82 us
  transfers between devices with their start and end apart: 16, of which 5 were waited for; matrix products, arithmetic and copies ran while one was open for 22% of the time, Pallas kernels for 0%

commit v1 on v0

v1 whole, which is shorter than its diff:
```python
import functools

import jax
import jax.numpy as jnp
import numpy as np
from jax import lax
from jax.experimental import pallas as pl
from jax.experimental.pallas import tpu as pltpu
from jax.sharding import PartitionSpec as P

TILE = 7
STEPS = 3
AXES = ("row", "col")

DOWN = (
    [(j, s, s - 1) for j in (0, 1, 3) for s in (1, 2, 3)] + [(2, 2, 0), (2, 3, 2)],
    [(0, 1, 0), (0, 2, 1), (1, 1, 0), (1, 2, 1), (2, 2, 1), (3, 2, 0)],
    [(1, 1, 0), (2, 1, 0)],
)
UP = (
    [(0, 0, 1), (0, 1, 3)] + [(j, s, s + 1) for j in (1, 2, 3) for s in (0, 1, 2)],
    [(0, 1, 2), (1, 1, 2), (1, 2, 3), (2, 1, 2), (2, 2, 3), (3, 1, 3)],
    [(0, 2, 3), (1, 2, 3)],
)


def origins(stages, n):
    held = np.tile(np.arange(n), (n, 1))
    out = []
    for flows in stages:
        got = np.full((n, n), -1)
        for j, source, target in flows:
            got[j, target] = held[j, source]
        held = got
        out.append(got)
    return out


def move(block, flows, n):
    return lax.ppermute(block, AXES, [(j * n + s, j * n + t) for j, s, t in flows])


def multiply(n_first, widths, tile, cells_ref, plan_ref, where_ref, *refs):
    firsts, seconds = refs[:n_first], refs[n_first : n_first + len(widths)]
    out_ref, a_vmem, b_vmem, sems = refs[n_first + len(widths) :]
    out_ref[...] = jnp.zeros_like(out_ref)
    slots = out_ref.shape[0]

    entry = 0
    for second, width in zip(seconds, widths):
        for part in range(width):
            which, a_at, b_at = plan_ref[3 * entry], plan_ref[3 * entry + 1], plan_ref[3 * entry + 2]
            entry += 1

            def one_entry(second=second, part=part, which=which, a_at=a_at, b_at=b_at):
                b_cell = cells_ref[b_at]

                def one_pair(first_slot, carry):
                    a_cell = cells_ref[a_at + first_slot]
                    product = (a_cell // tile) * tile + b_cell % tile
                    matching = a_cell % tile == b_cell // tile
                    kept = [matching & (product == where_ref[c]) for c in range(slots)]

                    @pl.when(functools.reduce(jnp.logical_or, kept))
                    def _():
                        b_copy = pltpu.make_async_copy(second.at[part], b_vmem, sems.at[1])
                        b_copy.start()
                        for m, first in enumerate(firsts):

                            @pl.when(which == m)
                            def _():
                                a_copy = pltpu.make_async_copy(first.at[first_slot], a_vmem, sems.at[0])
                                a_copy.start()
                                a_copy.wait()

                        b_copy.wait()
                        a, b = a_vmem[...], b_vmem[...]
                        a_high = a.astype(jnp.bfloat16)
                        b_high = b.astype(jnp.bfloat16)
                        a_low = (a - a_high.astype(jnp.float32)).astype(jnp.bfloat16)
                        b_low = (b - b_high.astype(jnp.float32)).astype(jnp.bfloat16)
                        dot = functools.partial(jnp.dot, preferred_element_type=jnp.float32)
                        value = dot(a_high, b_high) + (dot(a_high, b_low) + dot(a_low, b_high))
                        for c in range(slots):

                            @pl.when(kept[c])
                            def _():
                                out_ref[c] += value

                    return carry

                lax.fori_loop(0, slots, one_pair, 0)

            pl.when(which >= 0)(one_entry)


def product(cells, plan, where, firsts, seconds):
    slots, rows, columns = firsts[0].shape
    widths = [x.shape[0] for x in seconds]
    smem = pl.BlockSpec(memory_space=pltpu.SMEM)
    return pl.pallas_call(
        functools.partial(multiply, len(firsts), widths, TILE),
        out_shape=jax.ShapeDtypeStruct((slots, rows, columns), jnp.float32),
        in_specs=[smem] * 3 + [pl.BlockSpec(memory_space=pl.ANY)] * (len(firsts) + len(seconds)),
        out_specs=pl.BlockSpec(memory_space=pltpu.VMEM),
        scratch_shapes=[
            pltpu.VMEM((rows, columns), jnp.float32),
            pltpu.VMEM((rows, columns), jnp.float32),
            pltpu.SemaphoreType.DMA((2,)),
        ],
        compiler_params=pltpu.CompilerParams(vmem_limit_bytes=24 * 1024 * 1024),
    )(cells, plan, where, *firsts, *seconds)


def gathered_four(a, b, n):
    a_core = lax.ppermute(a, "row", [(j, j ^ 1) for j in range(n)])
    a_chip = lax.ppermute(a, "row", [(j, j ^ 2) for j in range(n)])
    a_far = lax.ppermute(a_chip, "row", [(j, j ^ 1) for j in range(n)])
    firsts = [a, a_core, a_chip, a_far]
    seconds, tiles = [b], [np.tile(np.arange(n), (n, 1))]
    parts = [b[s : s + 1] for s in range(b.shape[0])]
    down, up = list(parts), list(parts)
    down_tiles, up_tiles = origins(DOWN, n), origins(UP, n)
    got = []
    for stage in range(len(DOWN)):
        for s in range(len(parts)):
            down[s] = move(down[s], DOWN[stage], n)
            up[s] = move(up[s], UP[stage], n)
            got += [(down[s], s, down_tiles[stage]), (up[s], s, up_tiles[stage])]
    entries = [(b, list(range(b.shape[0])), tiles[0])] + [(x, [s], t) for x, s, t in got]
    j, i = np.meshgrid(np.arange(n), np.arange(n), indexing="ij")
    plan = []
    for _, slots, tile in entries:
        inside = (tile >= 0) & ((tile - i - j) % n < STEPS)
        for s in slots:
            plan.append(np.where(inside, tile ^ j, -1))
            plan.append((tile * n + i) * 2 * b.shape[0])
            plan.append((j * n + tile) * 2 * b.shape[0] + b.shape[0] + s)
    return firsts, [x for x, _, _ in entries], np.stack(plan, -1)


def gathered_any(a, b, n):
    firsts, seconds, plan = [], [], []
    j, i = np.meshgrid(np.arange(n), np.arange(n), indexing="ij")
    for step in range(STEPS):
        tile = (i + j + step) % n
        here = (j * n + i).reshape(-1)
        firsts.append(lax.ppermute(a, AXES, list(zip((tile * n + i).reshape(-1).tolist(), here.tolist()))))
        seconds.append(lax.ppermute(b, AXES, list(zip((j * n + tile).reshape(-1).tolist(), here.tolist()))))
        for s in range(b.shape[0]):
            plan.append(np.full((n, n), step))
            plan.append((tile * n + i) * 2 * b.shape[0])
            plan.append((j * n + tile) * 2 * b.shape[0] + b.shape[0] + s)
    return firsts, seconds, np.stack(plan, -1)


def on_device(a_blocks, first_factor_cell_index, b_blocks, second_factor_cell_index, c_where):
    n = lax.axis_size("row")
    own_cells = jnp.concatenate([first_factor_cell_index[0, 0], second_factor_cell_index[0, 0]])
    cells = lax.all_gather(own_cells, AXES).reshape(-1)
    gathered = gathered_four if n == 4 else gathered_any
    firsts, seconds, plan = gathered(a_blocks[0, 0], b_blocks[0, 0], n)
    plan = jnp.asarray(plan, jnp.int32)[lax.axis_index("row"), lax.axis_index("col")]
    return product(cells, plan, c_where[0, 0], firsts, seconds)[None, None]


def solution(mesh):
    return jax.shard_map(
        on_device,
        mesh=mesh,
        in_specs=(
            P(("groups", "col"), "row", None, None, None),
            P(("groups", "col"), "row", None),
            P(("groups", "col"), "row", None, None, None),
            P(("groups", "col"), "row", None),
            P(("groups", "col"), "row", None),
        ),
        out_specs=P(("groups", "col"), "row", None, None, None),
        check_vma=False,
    )
```

time: 179 us -> 97.3 us (0.54)
  the two profiles are of different devices: /device:TPU:0 before, /device:TPU:10 now
where the time goes in v1:
time: 97.3 us; the launch traced here: 96 us
  starting transfers between devices  31.8 us (33%)
  waiting for transfers between devices  26.5 us (27%)
  blocking collectives  18.4 us (19%)
  local copies, waits for them, and re-layouts  12.7 us (13%)
  Pallas kernels  5.3 us (5%)
  between operations  1.04 us (1%)
    ppermute x12, starting transfers between devices, move(): lax.ppermute(block, AXES, [(j * n + s, j * n + t) for j, s, t in flows])  29 us
    ppermute x12, waiting for transfers between devices, move(): lax.ppermute(block, AXES, [(j * n + s, j * n + t) for j, s, t in flows])  26.5 us
    unnamed x1, blocking collectives  18.4 us
    unnamed x34, local copies, waits for them, and re-layouts  10.5 us
    pallas_call x1, Pallas kernels, product(): pl.pallas_call(functools.partial(multiply, len(firsts), widths, TILE), ou...  5.3 us
    ppermute x1, starting transfers between devices, gathered_four(): a_chip = lax.ppermute(a, 'row', [(j, j ^ 2) for j in range(n)])  2.83 us
  transfers between devices with their start and end apart: 15, of which 6 were waited for; matrix products, arithmetic and copies ran while one was open for 2% of the time, Pallas kernels for 0%

profile of v1, /device:TPU:10, one launch (start us, length us, event | category | flops | bytes accessed | tf_op | source)
XLA Modules:
  0.0 96.0 jit_solution(7350778264612450151)
XLA Ops:
  0.0 1.5 %slice_bitcast_fusion = (f32[1,384,384]{2,1,0:T(8,128)S(1)}, f32[1,384,384]{2,1,0:T(8,128)S(1)}) fusion(f32[1,1,2,384,384]{4,3,2,1,0:T(8,128)} %param.8), kind=kLoop, calls=%fused_computation | loop fusion | bytes 2359296 | tf_op jit(solution)/shard_map/slice | solution.py:121
  1.5 3.5 %collective-permute-start.6 = (f32[1,384,384]{2,1,0:T(8,128)S(1)}, f32[1,384,384]{2,1,0:T(8,128)S(1)}, u32[]{:S(2)}, u32[]{:S(2)}) collective-permute-start(f32[1,384,384]{2,1,0:T(8,128)S(1)} %get-tuple-element.5), channel_id=1, source_target_pairs={{0,1},{1,3},{4,5},{5,6},{6,7},{8,9},{9,10},{10,11},{12,13},{13,14}... | collective-permute-start | bytes 1769480 | tf_op jit(solution)/shard_map/ppermute | solution.py:40
  5.0 0.7 collective-permute-start.5
  5.7 2.8 %collective-permute-start.1 = (f32[2,384,384]{2,1,0:T(8,128)S(1)}, f32[2,384,384]{2,1,0:T(8,128)S(1)}, u32[]{:S(2)}, u32[]{:S(2)}) collective-permute-start(f32[2,384,384]{2,1,0:T(8,128)S(1)} %bitcast.14), channel_id=1, source_target_pairs={{0,8},{4,12},{8,0},{12,4},{1,9},{5,13},{9,1},{13,5},{2,10},{6,14},... | collective-permute-start | bytes 3538952 | tf_op jit(solution)/shard_map/ppermute | solution.py:117
  8.6 3.9 %collective-permute-start.4 = (f32[1,384,384]{2,1,0:T(8,128)S(1)}, f32[1,384,384]{2,1,0:T(8,128)S(1)}, u32[]{:S(2)}, u32[]{:S(2)}) collective-permute-start(f32[1,384,384]{2,1,0:T(8,128)S(1)} %get-tuple-element.6), channel_id=1, source_target_pairs={{0,1},{1,3},{4,5},{5,6},{6,7},{8,9},{9,10},{10,11},{12,13},{13,14}... | collective-permute-start | bytes 1769480 | tf_op jit(solution)/shard_map/ppermute | solution.py:40
  12.5 0.7 collective-permute-start.3
  13.2 6.4 %collective-permute-done.6.refs_8_ = f32[1,384,384]{2,1,0:T(8,128)S(1)} collective-permute-done((f32[1,384,384]{2,1,0:T(8,128)S(1)}, f32[1,384,384]{2,1,0:T(8,128)S(1)}, u32[]{:S(2)}, u32[]{:S(2)}) %collective-permute-start.6) | collective-permute-done | bytes 589856 | tf_op jit(solution)/shard_map/ppermute | solution.py:40
  19.6 4.3 %collective-permute-start.10 = (f32[1,384,384]{2,1,0:T(8,128)S(1)}, f32[1,384,384]{2,1,0:T(8,128)}, u32[]{:S(2)}, u32[]{:S(2)}) collective-permute-start(f32[1,384,384]{2,1,0:T(8,128)S(1)} %collective-permute-done.6.refs_8_), channel_id=1, source_target_pairs={{1,2},{5,6},{6,7},{9,10},{10,11},{13,15},{17,18},{21,22},{22,23},{... | collective-permute-start | bytes 1769480 | tf_op jit(solution)/shard_map/ppermute | solution.py:40
  23.9 0.8 copy-done.4
  24.8 6.6 %collective-permute-done.4.refs_6_ = f32[1,384,384]{2,1,0:T(8,128)S(1)} collective-permute-done((f32[1,384,384]{2,1,0:T(8,128)S(1)}, f32[1,384,384]{2,1,0:T(8,128)S(1)}, u32[]{:S(2)}, u32[]{:S(2)}) %collective-permute-start.4) | collective-permute-done | bytes 589856 | tf_op jit(solution)/shard_map/ppermute | solution.py:40
  31.4 1.3 %collective-permute-start.9 = (f32[1,384,384]{2,1,0:T(8,128)S(1)}, f32[1,384,384]{2,1,0:T(8,128)}, u32[]{:S(2)}, u32[]{:S(2)}) collective-permute-start(f32[1,384,384]{2,1,0:T(8,128)S(1)} %collective-permute-done.5.refs_7_), channel_id=1, source_target_pairs={{1,0},{2,1},{5,4},{6,5},{10,9},{14,12},{17,16},{18,17},{21,20},{22... | collective-permute-start | bytes 1769480 | tf_op jit(solution)/shard_map/ppermute | solution.py:40
  32.7 0.8 copy-done.6
  33.5 6.2 %collective-permute-start.8 = (f32[1,384,384]{2,1,0:T(8,128)S(1)}, f32[1,384,384]{2,1,0:T(8,128)}, u32[]{:S(2)}, u32[]{:S(2)}) collective-permute-start(f32[1,384,384]{2,1,0:T(8,128)S(1)} %collective-permute-done.4.refs_6_), channel_id=1, source_target_pairs={{1,2},{5,6},{6,7},{9,10},{10,11},{13,15},{17,18},{21,22},{22,23},{... | collective-permute-start | bytes 1769480 | tf_op jit(solution)/shard_map/ppermute | solution.py:40
  39.7 0.8 copy-done.8
  40.5 3.5 %collective-permute-done.10.refs_12_ = f32[1,384,384]{2,1,0:T(8,128)} collective-permute-done((f32[1,384,384]{2,1,0:T(8,128)S(1)}, f32[1,384,384]{2,1,0:T(8,128)}, u32[]{:S(2)}, u32[]{:S(2)}) %collective-permute-start.10) | collective-permute-done | bytes 589856 | tf_op jit(solution)/shard_map/ppermute | solution.py:40
  44.0 1.3 %collective-permute-start.7 = (f32[1,384,384]{2,1,0:T(8,128)S(1)}, f32[1,384,384]{2,1,0:T(8,128)}, u32[]{:S(2)}, u32[]{:S(2)}) collective-permute-start(f32[1,384,384]{2,1,0:T(8,128)S(1)} %collective-permute-done.3.refs_5_), channel_id=1, source_target_pairs={{1,0},{2,1},{5,4},{6,5},{10,9},{14,12},{17,16},{18,17},{21,20},{22... | collective-permute-start | bytes 1769480 | tf_op jit(solution)/shard_map/ppermute | solution.py:40
  45.3 0.9 copy-done.10
  46.2 3.4 %collective-permute-done.9.refs_11_ = f32[1,384,384]{2,1,0:T(8,128)} collective-permute-done((f32[1,384,384]{2,1,0:T(8,128)S(1)}, f32[1,384,384]{2,1,0:T(8,128)}, u32[]{:S(2)}, u32[]{:S(2)}) %collective-permute-start.9) | collective-permute-done | bytes 589856 | tf_op jit(solution)/shard_map/ppermute | solution.py:40
  49.6 1.5 %collective-permute-start.14 = (f32[1,384,384]{2,1,0:T(8,128)}, f32[1,384,384]{2,1,0:T(8,128)}, u32[]{:S(2)}, u32[]{:S(2)}) collective-permute-start(f32[1,384,384]{2,1,0:T(8,128)} %collective-permute-done.10.refs_12_), channel_id=1, source_target_pairs={{2,3},{6,7},{18,19},{22,23}} | collective-permute-start | bytes 1769480 | tf_op jit(solution)/shard_map/ppermute | solution.py:40
  51.1 4.4 %collective-permute-done.8.refs_10_ = f32[1,384,384]{2,1,0:T(8,128)} collective-permute-done((f32[1,384,384]{2,1,0:T(8,128)S(1)}, f32[1,384,384]{2,1,0:T(8,128)}, u32[]{:S(2)}, u32[]{:S(2)}) %collective-permute-start.8) | collective-permute-done | bytes 589856 | tf_op jit(solution)/shard_map/ppermute | solution.py:40
  55.5 2.1 %collective-permute-start.13 = (f32[1,384,384]{2,1,0:T(8,128)}, f32[1,384,384]{2,1,0:T(8,128)}, u32[]{:S(2)}, u32[]{:S(2)}) collective-permute-start(f32[1,384,384]{2,1,0:T(8,128)} %collective-permute-done.9.refs_11_), channel_id=1, source_target_pairs={{5,4},{9,8},{21,20},{25,24}} | collective-permute-start | bytes 1769480 | tf_op jit(solution)/shard_map/ppermute | solution.py:40
  57.6 2.1 %collective-permute-done.7.refs_9_ = f32[1,384,384]{2,1,0:T(8,128)} collective-permute-done((f32[1,384,384]{2,1,0:T(8,128)S(1)}, f32[1,384,384]{2,1,0:T(8,128)}, u32[]{:S(2)}, u32[]{:S(2)}) %collective-permute-start.7) | collective-permute-done | bytes 589856 | tf_op jit(solution)/shard_map/ppermute | solution.py:40
  59.7 1.5 %collective-permute-start.12 = (f32[1,384,384]{2,1,0:T(8,128)}, f32[1,384,384]{2,1,0:T(8,128)}, u32[]{:S(2)}, u32[]{:S(2)}) collective-permute-start(f32[1,384,384]{2,1,0:T(8,128)} %collective-permute-done.8.refs_10_), channel_id=1, source_target_pairs={{2,3},{6,7},{18,19},{22,23}} | collective-permute-start | bytes 1769480 | tf_op jit(solution)/shard_map/ppermute | solution.py:40
  61.2 1.0 %copy-done.2 = f32[2,384,384]{2,1,0:T(8,128)} copy-done((f32[2,384,384]{2,1,0:T(8,128)}, f32[2,384,384]{2,1,0:T(8,128)S(1)}, u32[]{:S(2)}) %copy-start.2) | copy-done | bytes 1179672
  62.2 2.1 %collective-permute-start.11 = (f32[1,384,384]{2,1,0:T(8,128)}, f32[1,384,384]{2,1,0:T(8,128)}, u32[]{:S(2)}, u32[]{:S(2)}) collective-permute-start(f32[1,384,384]{2,1,0:T(8,128)} %collective-permute-done.7.refs_9_), channel_id=1, source_target_pairs={{5,4},{9,8},{21,20},{25,24}} | collective-permute-start | bytes 1769480 | tf_op jit(solution)/shard_map/ppermute | solution.py:40
  65.8 18.4 %all-reduce.cells_ref = s32[64]{0:T(128)S(1)} all-reduce(s32[64]{0:T(128)S(1)} %add_dynamic-update-slice_fusion), channel_id=2, replica_groups=mesh['groups'=2,'row'=4,'col'=4] {'row','col'}, use_global_device_ids=true, to_apply=%add | all-reduce | flops 64 | bytes 512
  85.0 1.3 %copy-done.3 = f32[2,384,384]{2,1,0:T(8,128)S(1)} copy-done((f32[2,384,384]{2,1,0:T(8,128)S(1)}, f32[2,384,384]{2,1,0:T(8,128)}, u32[]{:S(2)}) %copy-start.3) | copy-done | bytes 1179672
  86.3 1.1 %copy-done.5 = f32[1,384,384]{2,1,0:T(8,128)S(1)} copy-done((f32[1,384,384]{2,1,0:T(8,128)S(1)}, f32[1,384,384]{2,1,0:T(8,128)}, u32[]{:S(2)}) %copy-start.5) | copy-done | bytes 589848
  87.3 1.1 %copy-done.7 = f32[1,384,384]{2,1,0:T(8,128)S(1)} copy-done((f32[1,384,384]{2,1,0:T(8,128)S(1)}, f32[1,384,384]{2,1,0:T(8,128)}, u32[]{:S(2)}) %copy-start.7) | copy-done | bytes 589848
  88.4 1.1 %copy-done.9 = f32[1,384,384]{2,1,0:T(8,128)S(1)} copy-done((f32[1,384,384]{2,1,0:T(8,128)S(1)}, f32[1,384,384]{2,1,0:T(8,128)}, u32[]{:S(2)}) %copy-start.9) | copy-done | bytes 589848
  89.5 1.1 %copy-done.11 = f32[1,384,384]{2,1,0:T(8,128)S(1)} copy-done((f32[1,384,384]{2,1,0:T(8,128)S(1)}, f32[1,384,384]{2,1,0:T(8,128)}, u32[]{:S(2)}) %copy-start.11) | copy-done | bytes 589848
  90.5 5.3 %shard_map.64 = f32[2,384,384]{2,1,0:T(8,128)} custom-call(s32[64]{0:T(128)S(1)} %all-reduce.cells_ref, s32[42]{0:T(128)S(1)} %dynamic-slice_bitcast_fusion.plan_ref, s32[2]{0:T(128)S(1)} %bitcast.17, f32[2,384,384]{2,1,0:T(8,128)S(1)} %bitcast.16, f32[2,384,384]{2,1,0:T(8,128)S(1)} %copy-done.3, f32[2,384,384]{2,1,0:T(8,128)S(1)} %collective-permute-done.1.refs_2_, ...), custom_call_target="tpu_custom_call" | custom-call | tf_op jit(solution)/shard_map/pallas_call | solution.py:101
  (37 shorter events, 1.6 us)
Async XLA Ops:
  0.0 64.3 %copy-start.15 = (u32[32]{0:T(128)S(1)}, u32[32]{0:T(128)}, u32[]{:S(2)}) copy-start(u32[32]{0:T(128)} %constant.21) | copy-start | bytes 388
  0.0 85.0 %copy-start = (f32[1,1,2,384,384]{4,3,2,1,0:T(8,128)S(1)}, f32[1,1,2,384,384]{4,3,2,1,0:T(8,128)}, u32[]{:S(2)}) copy-start(f32[1,1,2,384,384]{4,3,2,1,0:T(8,128)} %param.8) | copy-start | bytes 3538948
  0.0 5.7 %copy-start.1 = (f32[1,1,2,384,384]{4,3,2,1,0:T(8,128)S(1)}, f32[1,1,2,384,384]{4,3,2,1,0:T(8,128)}, u32[]{:S(2)}) copy-start(f32[1,1,2,384,384]{4,3,2,1,0:T(8,128)} %param.6) | copy-start | bytes 3538948
  0.0 65.6 %copy-start.13 = (s32[1,1,2]{2,1,0:T(1,128)S(1)}, s32[1,1,2]{2,1,0:T(1,128)}, u32[]{:S(2)}) copy-start(s32[1,1,2]{2,1,0:T(1,128)} %param.9) | copy-start | bytes 28
  0.0 65.6 %copy-start.14 = (s32[1,1,2]{2,1,0:T(1,128)S(1)}, s32[1,1,2]{2,1,0:T(1,128)}, u32[]{:S(2)}) copy-start(s32[1,1,2]{2,1,0:T(1,128)} %param.7) | copy-start | bytes 28
  0.0 84.9 %copy-start.12 = (s32[1,1,2]{2,1,0:T(1,128)S(1)}, s32[1,1,2]{2,1,0:T(1,128)}, u32[]{:S(2)}) copy-start(s32[1,1,2]{2,1,0:T(1,128)} %param.10) | copy-start | bytes 28
  1.5 18.1 %collective-permute-start.6 = (f32[1,384,384]{2,1,0:T(8,128)S(1)}, f32[1,384,384]{2,1,0:T(8,128)S(1)}, u32[]{:S(2)}, u32[]{:S(2)}) collective-permute-start(f32[1,384,384]{2,1,0:T(8,128)S(1)} %get-tuple-element.5), channel_id=1, source_target_pairs={{0,1},{1,3},{4,5},{5,6},{6,7},{8,9},{9,10},{10,11},{12,13},{13,14}... | collective-permute-start | bytes 1769480 | tf_op jit(solution)/shard_map/ppermute | solution.py:40
  5.0 19.8 %collective-permute-start.5 = (f32[1,384,384]{2,1,0:T(8,128)S(1)}, f32[1,384,384]{2,1,0:T(8,128)S(1)}, u32[]{:S(2)}, u32[]{:S(2)}) collective-permute-start(f32[1,384,384]{2,1,0:T(8,128)S(1)} %get-tuple-element.5), channel_id=1, source_target_pairs={{1,0},{2,1},{3,2},{5,4},{6,5},{7,6},{13,12},{14,13},{15,14},{10,8}... | collective-permute-start | bytes 1769480 | tf_op jit(solution)/shard_map/ppermute | solution.py:40
  5.7 40.4 %collective-permute-start.1 = (f32[2,384,384]{2,1,0:T(8,128)S(1)}, f32[2,384,384]{2,1,0:T(8,128)S(1)}, u32[]{:S(2)}, u32[]{:S(2)}) collective-permute-start(f32[2,384,384]{2,1,0:T(8,128)S(1)} %bitcast.14), channel_id=1, source_target_pairs={{0,8},{4,12},{8,0},{12,4},{1,9},{5,13},{9,1},{13,5},{2,10},{6,14},... | collective-permute-start | bytes 3538952 | tf_op jit(solution)/shard_map/ppermute | solution.py:117
  8.6 22.8 %collective-permute-start.4 = (f32[1,384,384]{2,1,0:T(8,128)S(1)}, f32[1,384,384]{2,1,0:T(8,128)S(1)}, u32[]{:S(2)}, u32[]{:S(2)}) collective-permute-start(f32[1,384,384]{2,1,0:T(8,128)S(1)} %get-tuple-element.6), channel_id=1, source_target_pairs={{0,1},{1,3},{4,5},{5,6},{6,7},{8,9},{9,10},{10,11},{12,13},{13,14}... | collective-permute-start | bytes 1769480 | tf_op jit(solution)/shard_map/ppermute | solution.py:40
  12.5 21.0 %collective-permute-start.3 = (f32[1,384,384]{2,1,0:T(8,128)S(1)}, f32[1,384,384]{2,1,0:T(8,128)S(1)}, u32[]{:S(2)}, u32[]{:S(2)}) collective-permute-start(f32[1,384,384]{2,1,0:T(8,128)S(1)} %get-tuple-element.6), channel_id=1, source_target_pairs={{1,0},{2,1},{3,2},{5,4},{6,5},{7,6},{13,12},{14,13},{15,14},{10,8}... | collective-permute-start | bytes 1769480 | tf_op jit(solution)/shard_map/ppermute | solution.py:40
  19.6 24.4 %collective-permute-start.10 = (f32[1,384,384]{2,1,0:T(8,128)S(1)}, f32[1,384,384]{2,1,0:T(8,128)}, u32[]{:S(2)}, u32[]{:S(2)}) collective-permute-start(f32[1,384,384]{2,1,0:T(8,128)S(1)} %collective-permute-done.6.refs_8_), channel_id=1, source_target_pairs={{1,2},{5,6},{6,7},{9,10},{10,11},{13,15},{17,18},{21,22},{22,23},{... | collective-permute-start | bytes 1769480 | tf_op jit(solution)/shard_map/ppermute | solution.py:40
  23.9 0.8 copy-start.4
  24.8 36.4 %collective-permute-start = (f32[2,384,384]{2,1,0:T(8,128)S(1)}, f32[2,384,384]{2,1,0:T(8,128)S(1)}, u32[]{:S(2)}, u32[]{:S(2)}) collective-permute-start(f32[2,384,384]{2,1,0:T(8,128)S(1)} %bitcast.15), channel_id=1, source_target_pairs={{0,4},{4,0},{8,12},{12,8},{1,5},{5,1},{9,13},{13,9},{2,6},{6,2},{1... | collective-permute-start | bytes 3538952 | tf_op jit(solution)/shard_map/ppermute | solution.py:116
  31.4 18.3 %collective-permute-start.9 = (f32[1,384,384]{2,1,0:T(8,128)S(1)}, f32[1,384,384]{2,1,0:T(8,128)}, u32[]{:S(2)}, u32[]{:S(2)}) collective-permute-start(f32[1,384,384]{2,1,0:T(8,128)S(1)} %collective-permute-done.5.refs_7_), channel_id=1, source_target_pairs={{1,0},{2,1},{5,4},{6,5},{10,9},{14,12},{17,16},{18,17},{21,20},{22... | collective-permute-start | bytes 1769480 | tf_op jit(solution)/shard_map/ppermute | solution.py:40
  32.6 0.8 copy-start.6
  33.5 22.0 %collective-permute-start.8 = (f32[1,384,384]{2,1,0:T(8,128)S(1)}, f32[1,384,384]{2,1,0:T(8,128)}, u32[]{:S(2)}, u32[]{:S(2)}) collective-permute-start(f32[1,384,384]{2,1,0:T(8,128)S(1)} %collective-permute-done.4.refs_6_), channel_id=1, source_target_pairs={{1,2},{5,6},{6,7},{9,10},{10,11},{13,15},{17,18},{21,22},{22,23},{... | collective-permute-start | bytes 1769480 | tf_op jit(solution)/shard_map/ppermute | solution.py:40
  39.7 0.8 copy-start.8
  44.0 15.7 %collective-permute-start.7 = (f32[1,384,384]{2,1,0:T(8,128)S(1)}, f32[1,384,384]{2,1,0:T(8,128)}, u32[]{:S(2)}, u32[]{:S(2)}) collective-permute-start(f32[1,384,384]{2,1,0:T(8,128)S(1)} %collective-permute-done.3.refs_5_), channel_id=1, source_target_pairs={{1,0},{2,1},{5,4},{6,5},{10,9},{14,12},{17,16},{18,17},{21,20},{22... | collective-permute-start | bytes 1769480 | tf_op jit(solution)/shard_map/ppermute | solution.py:40
  45.3 0.9 copy-start.10
  46.2 38.8 %collective-permute-start.2 = (f32[2,384,384]{2,1,0:T(8,128)S(1)}, f32[2,384,384]{2,1,0:T(8,128)}, u32[]{:S(2)}, u32[]{:S(2)}) collective-permute-start(f32[2,384,384]{2,1,0:T(8,128)S(1)} %collective-permute-done.1.refs_2_), channel_id=1, source_target_pairs={{0,4},{4,0},{8,12},{12,8},{1,5},{5,1},{9,13},{13,9},{2,6},{6,2},{1... | collective-permute-start | bytes 3538952 | tf_op jit(solution)/shard_map/ppermute | solution.py:118
  49.6 35.3 %collective-permute-start.14 = (f32[1,384,384]{2,1,0:T(8,128)}, f32[1,384,384]{2,1,0:T(8,128)}, u32[]{:S(2)}, u32[]{:S(2)}) collective-permute-start(f32[1,384,384]{2,1,0:T(8,128)} %collective-permute-done.10.refs_12_), channel_id=1, source_target_pairs={{2,3},{6,7},{18,19},{22,23}} | collective-permute-start | bytes 1769480 | tf_op jit(solution)/shard_map/ppermute | solution.py:40
  55.5 29.4 %collective-permute-start.13 = (f32[1,384,384]{2,1,0:T(8,128)}, f32[1,384,384]{2,1,0:T(8,128)}, u32[]{:S(2)}, u32[]{:S(2)}) collective-permute-start(f32[1,384,384]{2,1,0:T(8,128)} %collective-permute-done.9.refs_11_), channel_id=1, source_target_pairs={{5,4},{9,8},{21,20},{25,24}} | collective-permute-start | bytes 1769480 | tf_op jit(solution)/shard_map/ppermute | solution.py:40
  59.7 25.2 %collective-permute-start.12 = (f32[1,384,384]{2,1,0:T(8,128)}, f32[1,384,384]{2,1,0:T(8,128)}, u32[]{:S(2)}, u32[]{:S(2)}) collective-permute-start(f32[1,384,384]{2,1,0:T(8,128)} %collective-permute-done.8.refs_10_), channel_id=1, source_target_pairs={{2,3},{6,7},{18,19},{22,23}} | collective-permute-start | bytes 1769480 | tf_op jit(solution)/shard_map/ppermute | solution.py:40
  61.2 1.0 %copy-start.2 = (f32[2,384,384]{2,1,0:T(8,128)}, f32[2,384,384]{2,1,0:T(8,128)S(1)}, u32[]{:S(2)}) copy-start(f32[2,384,384]{2,1,0:T(8,128)S(1)} %collective-permute-done.refs_1_) | copy-start | bytes 3538948
  62.2 22.7 %collective-permute-start.11 = (f32[1,384,384]{2,1,0:T(8,128)}, f32[1,384,384]{2,1,0:T(8,128)}, u32[]{:S(2)}, u32[]{:S(2)}) collective-permute-start(f32[1,384,384]{2,1,0:T(8,128)} %collective-permute-done.7.refs_9_), channel_id=1, source_target_pairs={{5,4},{9,8},{21,20},{25,24}} | collective-permute-start | bytes 1769480 | tf_op jit(solution)/shard_map/ppermute | solution.py:40
  85.0 1.3 %copy-start.3 = (f32[2,384,384]{2,1,0:T(8,128)S(1)}, f32[2,384,384]{2,1,0:T(8,128)}, u32[]{:S(2)}) copy-start(f32[2,384,384]{2,1,0:T(8,128)} %copy-done.2) | copy-start | bytes 3538948
  86.3 1.1 %copy-start.5 = (f32[1,384,384]{2,1,0:T(8,128)S(1)}, f32[1,384,384]{2,1,0:T(8,128)}, u32[]{:S(2)}) copy-start(f32[1,384,384]{2,1,0:T(8,128)} %copy-done.4) | copy-start | bytes 1769476
  87.3 1.1 %copy-start.7 = (f32[1,384,384]{2,1,0:T(8,128)S(1)}, f32[1,384,384]{2,1,0:T(8,128)}, u32[]{:S(2)}) copy-start(f32[1,384,384]{2,1,0:T(8,128)} %copy-done.6) | copy-start | bytes 1769476
  88.4 1.1 %copy-start.9 = (f32[1,384,384]{2,1,0:T(8,128)S(1)}, f32[1,384,384]{2,1,0:T(8,128)}, u32[]{:S(2)}) copy-start(f32[1,384,384]{2,1,0:T(8,128)} %copy-done.8) | copy-start | bytes 1769476
  89.4 1.1 %copy-start.11 = (f32[1,384,384]{2,1,0:T(8,128)S(1)}, f32[1,384,384]{2,1,0:T(8,128)}, u32[]{:S(2)}) copy-start(f32[1,384,384]{2,1,0:T(8,128)} %copy-done.10) | copy-start | bytes 1769476

commit v2 on v0

v2 whole, which is shorter than its diff:
```python
import functools

import jax
import jax.numpy as jnp
import numpy as np
from jax import lax
from jax.experimental import pallas as pl
from jax.experimental.pallas import tpu as pltpu
from jax.sharding import PartitionSpec as P

TILE = 7
STEPS = 3
PAD = 8
AXES = ("row", "col")

DOWN = (
    [(j, s, s - 1) for j in (0, 1, 3) for s in (1, 2, 3)] + [(2, 2, 0), (2, 3, 2)],
    [(0, 1, 0), (0, 2, 1), (1, 1, 0), (1, 2, 1), (2, 2, 1), (3, 2, 0)],
    [(1, 1, 0), (2, 1, 0)],
)
UP = (
    [(0, 0, 1), (0, 1, 3)] + [(j, s, s + 1) for j in (1, 2, 3) for s in (0, 1, 2)],
    [(0, 1, 2), (1, 1, 2), (1, 2, 3), (2, 1, 2), (2, 2, 3), (3, 1, 3)],
    [(0, 2, 3), (1, 2, 3)],
)


def origins(stages, n):
    held = np.tile(np.arange(n), (n, 1))
    out = []
    for flows in stages:
        got = np.full((n, n), -1)
        for j, source, target in flows:
            got[j, target] = held[j, source]
        held = got
        out.append(got)
    return out


def move(block, flows, n):
    return lax.ppermute(block, AXES, [(j * n + s, j * n + t) for j, s, t in flows])


def tag_kernel(cell_ref, in_ref, *rest):
    slots, rows, columns = in_ref.shape
    outs, sems = rest[:slots], rest[slots]
    copies = [pltpu.make_async_copy(in_ref.at[s], outs[s].at[pl.ds(0, rows)], sems.at[s]) for s in range(slots)]
    for copy in copies:
        copy.start()
    for s in range(slots):
        outs[s][pl.ds(rows, PAD)] = jnp.full((PAD, columns), cell_ref[s].astype(jnp.float32))
    for copy in copies:
        copy.wait()


def tagged(blocks, cells):
    slots, rows, columns = blocks.shape
    return pl.pallas_call(
        tag_kernel,
        out_shape=[jax.ShapeDtypeStruct((rows + PAD, columns), blocks.dtype)] * slots,
        in_specs=[pl.BlockSpec(memory_space=pltpu.SMEM), pl.BlockSpec(memory_space=pltpu.HBM)],
        out_specs=[pl.BlockSpec(memory_space=pltpu.VMEM)] * slots,
        scratch_shapes=[pltpu.SemaphoreType.DMA((slots,))],
        compiler_params=pltpu.CompilerParams(vmem_limit_bytes=62 * 1024 * 1024),
    )(cells, blocks)


def tag_all_kernel(cell_ref, in_ref, out_ref, sems):
    slots, rows, columns = in_ref.shape
    copy = pltpu.make_async_copy(in_ref, out_ref.at[:, pl.ds(0, rows)], sems.at[0])
    copy.start()
    for s in range(slots):
        out_ref[s, pl.ds(rows, PAD)] = jnp.full((PAD, columns), cell_ref[s].astype(jnp.float32))
    copy.wait()


def tagged_together(blocks, cells):
    slots, rows, columns = blocks.shape
    return pl.pallas_call(
        tag_all_kernel,
        out_shape=jax.ShapeDtypeStruct((slots, rows + PAD, columns), blocks.dtype),
        in_specs=[pl.BlockSpec(memory_space=pltpu.SMEM), pl.BlockSpec(memory_space=pltpu.HBM)],
        out_specs=pl.BlockSpec(memory_space=pltpu.VMEM),
        scratch_shapes=[pltpu.SemaphoreType.DMA((1,))],
        compiler_params=pltpu.CompilerParams(vmem_limit_bytes=62 * 1024 * 1024),
    )(cells, blocks)


def dot_split(a, b):
    a_high, b_high = a.astype(jnp.bfloat16), b.astype(jnp.bfloat16)
    a_low = (a - a_high.astype(jnp.float32)).astype(jnp.bfloat16)
    b_low = (b - b_high.astype(jnp.float32)).astype(jnp.bfloat16)
    dot = functools.partial(jnp.dot, preferred_element_type=jnp.float32)
    return dot(a_high, b_high) + (dot(a_high, b_low) + dot(a_low, b_high))


def kept_cells(a_cell, b_cell, where_ref, slots):
    product = (a_cell // TILE) * TILE + b_cell % TILE
    matching = a_cell % TILE == b_cell // TILE
    return [matching & (product == where_ref[c]) for c in range(slots)]


def multiply(plan_ref, where_ref, *refs, firsts_at, n_arrays, n_second):
    arrays, seconds = refs[:n_arrays], refs[n_arrays : n_arrays + n_second]
    out_ref, a_vmem, b_vmem, a_cells, b_cells, cell_sems, sems = refs[-7:]
    slots, rows, columns = out_ref.shape
    tag = (pl.ds(rows, PAD), pl.ds(0, 128))

    copies = []
    for m, (k, offset) in enumerate(firsts_at):
        for s in range(slots):
            copies.append(pltpu.make_async_copy(arrays[k].at[offset + s, *tag], a_cells.at[m, s], cell_sems.at[0]))
    for e in range(n_second):
        copies.append(pltpu.make_async_copy(seconds[e].at[*tag], b_cells.at[e], cell_sems.at[0]))
    for copy in copies:
        copy.start()
    out_ref[...] = jnp.zeros_like(out_ref)
    for copy in copies:
        copy.wait()

    for entry, second in enumerate(seconds):
        which = plan_ref[entry]

        def one_entry(entry=entry, second=second, which=which):
            b_cell = b_cells[entry, 0, 0].astype(jnp.int32)

            def one_pair(first_slot, carry):
                a_cell = a_cells[which, first_slot, 0, 0].astype(jnp.int32)
                kept = kept_cells(a_cell, b_cell, where_ref, slots)

                @pl.when(functools.reduce(jnp.logical_or, kept))
                def _():
                    b_copy = pltpu.make_async_copy(second.at[pl.ds(0, rows)], b_vmem, sems.at[1])
                    b_copy.start()
                    for m, (k, offset) in enumerate(firsts_at):

                        @pl.when(which == m)
                        def _():
                            source = arrays[k].at[offset + first_slot, pl.ds(0, rows)]
                            a_copy = pltpu.make_async_copy(source, a_vmem, sems.at[0])
                            a_copy.start()
                            a_copy.wait()

                    b_copy.wait()
                    value = dot_split(a_vmem[...], b_vmem[...])
                    for c in range(slots):

                        @pl.when(kept[c])
                        def _():
                            out_ref[c] += value

                return carry

            lax.fori_loop(0, slots, one_pair, 0)

        pl.when(which >= 0)(one_entry)


def multiply_last(plan_ref, where_ref, *refs, firsts_at, n_arrays, n_second):
    for entry in range(n_second):
        last_entry(entry, plan_ref, where_ref, *refs, firsts_at=firsts_at, n_arrays=n_arrays)


def last_entry(entry, plan_ref, where_ref, *refs, firsts_at, n_arrays):
    arrays, second = refs[:n_arrays], refs[n_arrays + entry]
    sums, a_vmem, b_vmem, c_vmem, a_cells, b_cells, cell_sems, sems = refs[-8:]
    slots, rows, columns = sums.shape
    body, tag = pl.ds(0, rows), (pl.ds(rows, PAD), pl.ds(0, 128))
    which = plan_ref[entry]

    @pl.when(which >= 0)
    def _():
        tags = [pltpu.make_async_copy(second.at[*tag], b_cells, cell_sems.at[0])]
        blocks = [pltpu.make_async_copy(second.at[body], b_vmem, sems.at[0])]
        for s in range(slots):
            tags.append(pltpu.make_async_copy(arrays[0].at[s, *tag], a_cells.at[s], cell_sems.at[0]))
            blocks.append(pltpu.make_async_copy(arrays[0].at[s, body], a_vmem.at[s], sems.at[0]))
        blocks.append(pltpu.make_async_copy(sums, c_vmem, sems.at[0]))
        tags[0].start()
        for m, (k, offset) in enumerate(firsts_at):

            @pl.when(which == m)
            def _():
                for s in range(slots):
                    pltpu.make_async_copy(arrays[k].at[offset + s, *tag], a_cells.at[s], cell_sems.at[0]).start()
                for s in range(slots):
                    pltpu.make_async_copy(arrays[k].at[offset + s, body], a_vmem.at[s], sems.at[0]).start()

        blocks[0].start()
        blocks[-1].start()
        for copy in tags + blocks:
            copy.wait()
        b_cell = b_cells[0, 0].astype(jnp.int32)
        for s in range(slots):
            kept = kept_cells(a_cells[s, 0, 0].astype(jnp.int32), b_cell, where_ref, slots)

            @pl.when(functools.reduce(jnp.logical_or, kept))
            def _():
                value = dot_split(a_vmem[s], b_vmem[...])
                for c in range(slots):

                    @pl.when(kept[c])
                    def _():
                        c_vmem[c] += value
                        give = pltpu.make_async_copy(c_vmem.at[c], sums.at[c], sems.at[1])
                        give.start()
                        give.wait()


def add_products(plan, where, firsts, seconds, sums=None):
    slots = where.shape[0]
    rows, columns = seconds[0].shape
    rows -= PAD
    arrays = list({id(x): x for x, _ in firsts}.values())
    firsts_at = [([id(y) for y in arrays].index(id(x)), offset) for x, offset in firsts]
    smem = pl.BlockSpec(memory_space=pltpu.SMEM)
    hbm = pl.BlockSpec(memory_space=pltpu.HBM)
    blocks = [*arrays, *seconds]
    block = pltpu.VMEM((rows, columns), jnp.float32)
    pair = pltpu.VMEM((slots, rows, columns), jnp.float32)
    if sums is None:
        body = functools.partial(multiply, firsts_at=firsts_at, n_arrays=len(arrays), n_second=len(seconds))
        scratch = [block, block, pltpu.SMEM((len(firsts), slots, PAD, 128), jnp.float32)]
        scratch += [pltpu.SMEM((len(seconds), PAD, 128), jnp.float32)]
    else:
        body = functools.partial(multiply_last, firsts_at=firsts_at, n_arrays=len(arrays), n_second=len(seconds))
        scratch = [pair, block, pair, pltpu.SMEM((slots, PAD, 128), jnp.float32), pltpu.SMEM((PAD, 128), jnp.float32)]
        blocks.append(sums)
    return pl.pallas_call(
        body,
        out_shape=jax.ShapeDtypeStruct((slots, rows, columns), jnp.float32),
        in_specs=[smem] * 2 + [hbm] * len(blocks),
        out_specs=pl.BlockSpec(memory_space=pltpu.VMEM) if sums is None else hbm,
        scratch_shapes=scratch + [pltpu.SemaphoreType.DMA((1,)), pltpu.SemaphoreType.DMA((2,))],
        input_output_aliases={} if sums is None else {1 + len(blocks): 0},
        cost_estimate=pl.CostEstimate(
            flops=12 * len(seconds) * rows * columns * columns,
            bytes_accessed=4 * rows * columns * (slots + 2 * len(seconds)),
            transcendentals=0,
        ),
        compiler_params=pltpu.CompilerParams(vmem_limit_bytes=60 * 1024 * 1024),
    )(plan, where, *blocks)


def both_cores(a, a_chip, where, n):
    here = jnp.concatenate([a, a_chip])
    swap = lambda x: lax.ppermute(x, "row", [(p, p ^ 1) for p in range(n)])
    return here, lax.cond(where[0] >= 0, swap, jnp.zeros_like, here)


def by_four(a, a_cells, b, b_cells, where, n):
    parts = list(tagged(b, b_cells))
    slots = range(len(parts))
    j, i = np.meshgrid(np.arange(n), np.arange(n), indexing="ij")
    down_tiles, up_tiles = origins(DOWN, n), origins(UP, n)
    moved = [(part, np.tile(np.arange(n), (n, 1))) for part in parts]
    a, parts[0] = lax.optimization_barrier((a, parts[0]))
    a = tagged_together(a, a_cells)
    a_chip = lax.ppermute(a, "row", [(p, p ^ 2) for p in range(n)])
    down, up = list(parts), list(parts)
    last_tiles = [down_tiles[-1], up_tiles[-1]] * len(parts)
    all_tiles = [t for _, t in moved] + [t for k in range(len(DOWN) - 1) for _ in slots for t in (down_tiles[k], up_tiles[k])]
    plan = [np.where((t >= 0) & ((t - i - j) % n < STEPS), t ^ j, -1) for t in all_tiles + last_tiles]
    n_last = 2
    place = lax.axis_index("row"), lax.axis_index("col")
    plans = [jnp.asarray(np.stack(x, -1), jnp.int32)[place] for x in (plan[:-n_last], plan[-n_last:])]
    for stage in range(len(DOWN) - 1):
        for s in slots:
            if (stage, s) == (1, slots[-1]):
                up[s], plans = lax.optimization_barrier((up[s], plans))
            down[s], up[s] = move(down[s], DOWN[stage], n), move(up[s], UP[stage], n)
            moved += [(down[s], down_tiles[stage]), (up[s], up_tiles[stage])]
    for s in slots:
        down[s], up[s] = move(down[s], DOWN[-1], n), move(up[s], UP[-1], n)
        moved += [(down[s], down_tiles[-1]), (up[s], up_tiles[-1])]
    here, there = both_cores(a, a_chip, where, n)
    firsts = [(here, 0), (there, 0), (here, len(parts)), (there, len(parts))]
    blocks = [x for x, _ in moved]
    sums = add_products(plans[0], where, firsts, blocks[:-n_last])
    return add_products(plans[1], where, firsts, blocks[-n_last:], sums)


def by_any(a, a_cells, b, b_cells, where, n):
    a, parts = tagged_together(a, a_cells), tagged(b, b_cells)
    firsts, seconds, plan = [], [], []
    here = [(j, i) for j in range(n) for i in range(n)]
    for step in range(STEPS):
        from_row = [(((i + j + step) % n) * n + i, j * n + i) for j, i in here]
        from_col = [(j * n + (i + j + step) % n, j * n + i) for j, i in here]
        firsts.append((lax.ppermute(a, AXES, from_row), 0))
        seconds += [lax.ppermute(part, AXES, from_col) for part in parts]
        plan += [step for _ in parts]
    return add_products(jnp.asarray(plan, jnp.int32), where, firsts, seconds)


def on_device(a_blocks, first_factor_cell_index, b_blocks, second_factor_cell_index, c_where):
    n = lax.axis_size("row")
    blocks = (a_blocks, first_factor_cell_index, b_blocks, second_factor_cell_index, c_where)
    return (by_four if n == 4 else by_any)(*(x[0, 0] for x in blocks), n)[None, None]


def solution(mesh):
    return jax.shard_map(
        on_device,
        mesh=mesh,
        in_specs=(
            P(("groups", "col"), "row", None, None, None),
            P(("groups", "col"), "row", None),
            P(("groups", "col"), "row", None, None, None),
            P(("groups", "col"), "row", None),
            P(("groups", "col"), "row", None),
        ),
        out_specs=P(("groups", "col"), "row", None, None, None),
        check_vma=False,
    )
```

time: 179 us -> 80.6 us (0.45)
  the two profiles are of different devices: /device:TPU:0 before, /device:TPU:24 now
where the time goes in v2:
time: 80.6 us; the launch traced here: 79.1 us
  waiting for transfers between devices  32.9 us (41%)
  starting transfers between devices  23.9 us (30%)
  Pallas kernels  16.9 us (21%)
  local copies, waits for them, and re-layouts  3.21 us (4%)
  other arithmetic  1.8 us (2%)
    ppermute x12, waiting for transfers between devices, move(): lax.ppermute(block, AXES, [(j * n + s, j * n + t) for j, s, t in flows])  28.2 us
    ppermute x12, starting transfers between devices, move(): lax.ppermute(block, AXES, [(j * n + s, j * n + t) for j, s, t in flows])  22.3 us
    pallas_call x2, Pallas kernels, add_products(): pl.pallas_call(body, out_shape=jax.ShapeDtypeStruct((slots, rows, columns...  10.8 us
    ppermute x1, waiting for transfers between devices, both_cores(): swap = lambda x: lax.ppermute(x, 'row', [(p, p ^ 1) for p in range(n)])  4.72 us
    pallas_call x1, Pallas kernels, tagged_together(): pl.pallas_call(tag_all_kernel, out_shape=jax.ShapeDtypeStruct((slots, row...  3.13 us
    pallas_call x1, Pallas kernels, tagged(): pl.pallas_call(tag_kernel, out_shape=[jax.ShapeDtypeStruct((rows + PAD, c...  2.96 us
    squeeze x2, local copies, waits for them, and re-layouts, by_four(): jnp.asarray(np.stack(x, -1), jnp.int32)[place]  2.37 us
    concatenate x1, other arithmetic, both_cores(): here = jnp.concatenate([a, a_chip])  1.8 us
  transfers between devices with their start and end apart: 14, of which 6 were waited for; matrix products, arithmetic and copies ran while one was open for 5% of the time, Pallas kernels for 15%

profile of v2, /device:TPU:24, one launch (start us, length us, event | category | flops | bytes accessed | tf_op | source)
XLA Modules:
  0.0 79.1 jit_solution(7748189062715107481)
XLA Ops:
  0.0 3.0 %shard_map.73 = (f32[392,384]{1,0:T(8,128)}, f32[392,384]{1,0:T(8,128)}) custom-call(s32[2]{0:T(128)} %bitcast.14, f32[2,384,384]{2,1,0:T(8,128)} %bitcast.12), custom_call_target="tpu_custom_call" | custom-call | tf_op jit(solution)/shard_map/pallas_call | solution.py:58
  3.0 2.5 %collective-permute-start.8 = (f32[392,384]{1,0:T(8,128)}, f32[392,384]{1,0:T(8,128)S(1)}, u32[]{:S(2)}, u32[]{:S(2)}) collective-permute-start(f32[392,384]{1,0:T(8,128)} %get-tuple-element.22.refs_2_), channel_id=1, source_target_pairs={{1,0},{2,1},{3,2},{5,4},{6,5},{7,6},{13,12},{14,13},{15,14},{10,8}... | collective-permute-start | bytes 1806344 | tf_op jit(solution)/shard_map/ppermute | solution.py:41
  5.5 1.3 %collective-permute-start.9 = (f32[392,384]{1,0:T(8,128)}, f32[392,384]{1,0:T(8,128)}, u32[]{:S(2)}, u32[]{:S(2)}) collective-permute-start(f32[392,384]{1,0:T(8,128)} %get-tuple-element.22.refs_2_), channel_id=1, source_target_pairs={{0,1},{1,3},{4,5},{5,6},{6,7},{8,9},{9,10},{10,11},{12,13},{13,14}... | collective-permute-start | bytes 1806344 | tf_op jit(solution)/shard_map/ppermute | solution.py:41
  6.8 0.0 copy-start.1
  6.8 3.1 %shard_map.74 = f32[2,392,384]{2,1,0:T(8,128)} custom-call(s32[2]{0:T(128)} %bitcast.18, f32[2,384,384]{2,1,0:T(8,128)} %bitcast.13), custom_call_target="tpu_custom_call" | custom-call | tf_op jit(solution)/shard_map/pallas_call | solution.py:79
  10.0 1.6 %collective-permute-start.2 = (f32[2,392,384]{2,1,0:T(8,128)}, f32[2,392,384]{2,1,0:T(8,128)}, u32[]{:S(2)}, u32[]{:S(2)}) collective-permute-start(f32[2,392,384]{2,1,0:T(8,128)} %shard_map.74), channel_id=1, source_target_pairs={{0,8},{4,12},{8,0},{12,4},{1,9},{5,13},{9,1},{13,5},{2,10},{6,14},... | collective-permute-start | bytes 3612680 | tf_op jit(solution)/shard_map/ppermute | solution.py:259
  11.5 1.3 %collective-permute-start.1 = (f32[392,384]{1,0:T(8,128)S(1)}, f32[392,384]{1,0:T(8,128)}, u32[]{:S(2)}, u32[]{:S(2)}) collective-permute-start(f32[392,384]{1,0:T(8,128)S(1)} %copy-done.2), channel_id=1, source_target_pairs={{0,1},{1,3},{4,5},{5,6},{6,7},{8,9},{9,10},{10,11},{12,13},{13,14}... | collective-permute-start | bytes 1806344 | tf_op jit(solution)/shard_map/ppermute | solution.py:41
  12.8 5.6 %collective-permute-start.3 = (f32[392,384]{1,0:T(8,128)S(1)}, f32[392,384]{1,0:T(8,128)}, u32[]{:S(2)}, u32[]{:S(2)}) collective-permute-start(f32[392,384]{1,0:T(8,128)S(1)} %copy-done.2), channel_id=1, source_target_pairs={{1,0},{2,1},{3,2},{5,4},{6,5},{7,6},{13,12},{14,13},{15,14},{10,8}... | collective-permute-start | bytes 1806344 | tf_op jit(solution)/shard_map/ppermute | solution.py:41
  18.4 1.4 %collective-permute-done.8.refs_4_ = f32[392,384]{1,0:T(8,128)S(1)} collective-permute-done((f32[392,384]{1,0:T(8,128)}, f32[392,384]{1,0:T(8,128)S(1)}, u32[]{:S(2)}, u32[]{:S(2)}) %collective-permute-start.8) | collective-permute-done | bytes 602144 | tf_op jit(solution)/shard_map/ppermute | solution.py:41
  19.8 1.5 %collective-permute-start.10 = (f32[392,384]{1,0:T(8,128)S(1)}, f32[392,384]{1,0:T(8,128)}, u32[]{:S(2)}, u32[]{:S(2)}) collective-permute-start(f32[392,384]{1,0:T(8,128)S(1)} %collective-permute-done.8.refs_4_), channel_id=1, source_target_pairs={{1,0},{2,1},{5,4},{6,5},{10,9},{14,12},{17,16},{18,17},{21,20},{22... | collective-permute-start | bytes 1806344 | tf_op jit(solution)/shard_map/ppermute | solution.py:41
  21.3 3.9 %collective-permute-done.9.refs_5_ = f32[392,384]{1,0:T(8,128)} collective-permute-done((f32[392,384]{1,0:T(8,128)}, f32[392,384]{1,0:T(8,128)}, u32[]{:S(2)}, u32[]{:S(2)}) %collective-permute-start.9) | collective-permute-done | bytes 602144 | tf_op jit(solution)/shard_map/ppermute | solution.py:41
  25.2 1.5 %collective-permute-start.11 = (f32[392,384]{1,0:T(8,128)}, f32[392,384]{1,0:T(8,128)}, u32[]{:S(2)}, u32[]{:S(2)}) collective-permute-start(f32[392,384]{1,0:T(8,128)} %collective-permute-done.9.refs_5_), channel_id=1, source_target_pairs={{1,2},{5,6},{6,7},{9,10},{10,11},{13,15},{17,18},{21,22},{22,23},{... | collective-permute-start | bytes 1806344 | tf_op jit(solution)/shard_map/ppermute | solution.py:41
  26.7 1.2 %dynamic-slice_bitcast_fusion.plan_ref = s32[2]{0:T(128)} fusion(s32[4,4,2]{2,1,0:T(4,128)} %constant.20.clone, s32[]{:T(128)S(6)} %select_n.8, s32[]{:T(128)S(6)} %select_n.9), kind=kLoop, calls=%fused_computation.1 | loop fusion | bytes 24 | tf_op jit(solution)/shard_map/squeeze | solution.py:266
  27.9 1.2 %dynamic-slice_bitcast_fusion.1.plan_ref = s32[12]{0:T(128)} fusion(s32[4,4,12]{2,1,0:T(4,128)} %constant.19.clone, s32[]{:T(128)S(6)} %select_n.8, s32[]{:T(128)S(6)} %select_n.9), kind=kLoop, calls=%fused_computation.2 | loop fusion | bytes 104 | tf_op jit(solution)/shard_map/squeeze | solution.py:266
  29.0 9.0 %collective-permute-done.1.refs_7_ = f32[392,384]{1,0:T(8,128)} collective-permute-done((f32[392,384]{1,0:T(8,128)S(1)}, f32[392,384]{1,0:T(8,128)}, u32[]{:S(2)}, u32[]{:S(2)}) %collective-permute-start.1) | collective-permute-done | bytes 602144 | tf_op jit(solution)/shard_map/ppermute | solution.py:41
  38.1 1.5 %collective-permute-start.6 = (f32[392,384]{1,0:T(8,128)}, f32[392,384]{1,0:T(8,128)}, u32[]{:S(2)}, u32[]{:S(2)}) collective-permute-start(f32[392,384]{1,0:T(8,128)} %collective-permute-done.1.refs_7_), channel_id=1, source_target_pairs={{1,2},{5,6},{6,7},{9,10},{10,11},{13,15},{17,18},{21,22},{22,23},{... | collective-permute-start | bytes 1806344 | tf_op jit(solution)/shard_map/ppermute | solution.py:41
  39.5 0.0 collective-permute-done.3.refs_6_
  39.6 1.5 %collective-permute-start.4 = (f32[392,384]{1,0:T(8,128)}, f32[392,384]{1,0:T(8,128)}, u32[]{:S(2)}, u32[]{:S(2)}) collective-permute-start(f32[392,384]{1,0:T(8,128)} %collective-permute-done.3.refs_6_), channel_id=1, source_target_pairs={{1,0},{2,1},{5,4},{6,5},{10,9},{14,12},{17,16},{18,17},{21,20},{22... | collective-permute-start | bytes 1806344 | tf_op jit(solution)/shard_map/ppermute | solution.py:41
  41.0 1.6 %collective-permute-start.12 = (f32[392,384]{1,0:T(8,128)}, f32[392,384]{1,0:T(8,128)}, u32[]{:S(2)}, u32[]{:S(2)}) collective-permute-start(f32[392,384]{1,0:T(8,128)} %collective-permute-done.10.refs_8_), channel_id=1, source_target_pairs={{5,4},{9,8},{21,20},{25,24}} | collective-permute-start | bytes 1806344 | tf_op jit(solution)/shard_map/ppermute | solution.py:41
  42.6 0.0 collective-permute-done.11.refs_9_
  42.6 1.3 %collective-permute-start.13 = (f32[392,384]{1,0:T(8,128)}, f32[392,384]{1,0:T(8,128)}, u32[]{:S(2)}, u32[]{:S(2)}) collective-permute-start(f32[392,384]{1,0:T(8,128)} %collective-permute-done.11.refs_9_), channel_id=1, source_target_pairs={{2,3},{6,7},{18,19},{22,23}} | collective-permute-start | bytes 1806344 | tf_op jit(solution)/shard_map/ppermute | solution.py:41
  44.0 1.8 %pad_maximum_fusion.refs_0_ = f32[4,392,384]{2,1,0:T(8,128)S(1)} fusion(f32[2,392,384]{2,1,0:T(8,128)} %collective-permute-done.2, f32[2,392,384]{2,1,0:T(8,128)} %shard_map.74), kind=kLoop, calls=%fused_computation | loop fusion | flops 602112 | bytes 4816896 | tf_op jit(solution)/shard_map/concatenate | solution.py:246
  45.8 4.8 %conditional.1 = (f32[4,392,384]{2,1,0:T(8,128)}) conditional(s32[]{:T(128)} %bitcast.7, () %tuple.15, f32[4,392,384]{2,1,0:T(8,128)S(1)} %pad_maximum_fusion.refs_0_), branch_computations={%region_0.0_spmd, %region_1.0_spmd} | conditional | bytes 9633840 | solution.py:248
  45.8 0.1 collective-permute-start
  45.9 4.7 %collective-permute-done = f32[4,392,384]{2,1,0:T(8,128)} collective-permute-done((f32[4,392,384]{2,1,0:T(8,128)S(1)}, f32[4,392,384]{2,1,0:T(8,128)}, u32[]{:S(2)}, u32[]{:S(2)}) %collective-permute-start) | collective-permute-done | bytes 2408480 | tf_op jit(solution)/shard_map/cond/branch_1_fun/ppermute | solution.py:247
  50.6 1.3 %collective-permute-start.7 = (f32[392,384]{1,0:T(8,128)}, f32[392,384]{1,0:T(8,128)S(1)}, u32[]{:S(2)}, u32[]{:S(2)}) collective-permute-start(f32[392,384]{1,0:T(8,128)} %collective-permute-done.6.refs_11_), channel_id=1, source_target_pairs={{2,3},{6,7},{18,19},{22,23}} | collective-permute-start | bytes 1806344 | tf_op jit(solution)/shard_map/ppermute | solution.py:41
  51.9 1.5 %collective-permute-start.5 = (f32[392,384]{1,0:T(8,128)}, f32[392,384]{1,0:T(8,128)}, u32[]{:S(2)}, u32[]{:S(2)}) collective-permute-start(f32[392,384]{1,0:T(8,128)} %collective-permute-done.4.refs_10_), channel_id=1, source_target_pairs={{5,4},{9,8},{21,20},{25,24}} | collective-permute-start | bytes 1806344 | tf_op jit(solution)/shard_map/ppermute | solution.py:41
  53.4 8.5 %collective-permute-done.13.refs_13_ = f32[392,384]{1,0:T(8,128)} collective-permute-done((f32[392,384]{1,0:T(8,128)}, f32[392,384]{1,0:T(8,128)}, u32[]{:S(2)}, u32[]{:S(2)}) %collective-permute-start.13) | collective-permute-done | bytes 602144 | tf_op jit(solution)/shard_map/ppermute | solution.py:41
  61.9 8.4 %shard_map.75.refs_4_ = f32[2,384,384]{2,1,0:T(8,128)} custom-call(s32[12]{0:T(128)} %dynamic-slice_bitcast_fusion.1.plan_ref, s32[2]{0:T(128)} %bitcast.15, f32[4,392,384]{2,1,0:T(8,128)S(1)} %pad_maximum_fusion.refs_0_, f32[4,392,384]{2,1,0:T(8,128)} %get-tuple-element.23.refs_1_, f32[392,384]{1,0:T(8,128)} %get-tuple-element.22.refs_2_, ...), custom_call_target="tpu_custom_call" | custom-call | flops 8153726976 | bytes 15335424 | tf_op jit(solution)/shard_map/pallas_call | solution.py:229
  70.3 5.4 %collective-permute-done.7.refs_3_ = f32[392,384]{1,0:T(8,128)S(1)} collective-permute-done((f32[392,384]{1,0:T(8,128)}, f32[392,384]{1,0:T(8,128)S(1)}, u32[]{:S(2)}, u32[]{:S(2)}) %collective-permute-start.7) | collective-permute-done | bytes 602144 | tf_op jit(solution)/shard_map/ppermute | solution.py:41
  75.7 0.8 %copy-done = f32[392,384]{1,0:T(8,128)} copy-done((f32[392,384]{1,0:T(8,128)}, f32[392,384]{1,0:T(8,128)S(1)}, u32[]{:S(2)}) %copy-start) | copy-done | bytes 602136
  76.5 2.4 %shard_map.76 = f32[2,384,384]{2,1,0:T(8,128)} custom-call(s32[2]{0:T(128)} %dynamic-slice_bitcast_fusion.plan_ref, s32[2]{0:T(128)} %bitcast.16, f32[4,392,384]{2,1,0:T(8,128)S(1)} %pad_maximum_fusion.refs_0_, f32[4,392,384]{2,1,0:T(8,128)} %get-tuple-element.23.refs_1_, f32[392,384]{1,0:T(8,128)} %collective-permute-done.5.refs_2_, ...), custom_call_target="tpu_custom_call", output_to_operand_aliasing={{}: (6, {})} | custom-call | flops 1358954496 | bytes 3538944 | tf_op jit(solution)/shard_map/pallas_call | solution.py:229
  (12 shorter events, 0.0 us)
Async XLA Ops:
  3.0 8.5 %copy-start.2 = (f32[392,384]{1,0:T(8,128)S(1)}, f32[392,384]{1,0:T(8,128)}, u32[]{:S(2)}) copy-start(f32[392,384]{1,0:T(8,128)} %get-tuple-element.16.refs_3_) | copy-start | bytes 1806340
  3.0 16.8 %collective-permute-start.8 = (f32[392,384]{1,0:T(8,128)}, f32[392,384]{1,0:T(8,128)S(1)}, u32[]{:S(2)}, u32[]{:S(2)}) collective-permute-start(f32[392,384]{1,0:T(8,128)} %get-tuple-element.22.refs_2_), channel_id=1, source_target_pairs={{1,0},{2,1},{3,2},{5,4},{6,5},{7,6},{13,12},{14,13},{15,14},{10,8}... | collective-permute-start | bytes 1806344 | tf_op jit(solution)/shard_map/ppermute | solution.py:41
  5.5 19.6 %collective-permute-start.9 = (f32[392,384]{1,0:T(8,128)}, f32[392,384]{1,0:T(8,128)}, u32[]{:S(2)}, u32[]{:S(2)}) collective-permute-start(f32[392,384]{1,0:T(8,128)} %get-tuple-element.22.refs_2_), channel_id=1, source_target_pairs={{0,1},{1,3},{4,5},{5,6},{6,7},{8,9},{9,10},{10,11},{12,13},{13,14}... | collective-permute-start | bytes 1806344 | tf_op jit(solution)/shard_map/ppermute | solution.py:41
  6.8 37.1 %copy-start.1 = (s32[1,1,2]{2,1,0:T(1,128)S(1)}, s32[1,1,2]{2,1,0:T(1,128)}, u32[]{:S(2)}) copy-start(s32[1,1,2]{2,1,0:T(1,128)} %param.13) | copy-start | bytes 28
  10.0 34.0 %collective-permute-start.2 = (f32[2,392,384]{2,1,0:T(8,128)}, f32[2,392,384]{2,1,0:T(8,128)}, u32[]{:S(2)}, u32[]{:S(2)}) collective-permute-start(f32[2,392,384]{2,1,0:T(8,128)} %shard_map.74), channel_id=1, source_target_pairs={{0,8},{4,12},{8,0},{12,4},{1,9},{5,13},{9,1},{13,5},{2,10},{6,14},... | collective-permute-start | bytes 3612680 | tf_op jit(solution)/shard_map/ppermute | solution.py:259
  11.5 26.5 %collective-permute-start.1 = (f32[392,384]{1,0:T(8,128)S(1)}, f32[392,384]{1,0:T(8,128)}, u32[]{:S(2)}, u32[]{:S(2)}) collective-permute-start(f32[392,384]{1,0:T(8,128)S(1)} %copy-done.2), channel_id=1, source_target_pairs={{0,1},{1,3},{4,5},{5,6},{6,7},{8,9},{9,10},{10,11},{12,13},{13,14}... | collective-permute-start | bytes 1806344 | tf_op jit(solution)/shard_map/ppermute | solution.py:41
  12.8 26.7 %collective-permute-start.3 = (f32[392,384]{1,0:T(8,128)S(1)}, f32[392,384]{1,0:T(8,128)}, u32[]{:S(2)}, u32[]{:S(2)}) collective-permute-start(f32[392,384]{1,0:T(8,128)S(1)} %copy-done.2), channel_id=1, source_target_pairs={{1,0},{2,1},{3,2},{5,4},{6,5},{7,6},{13,12},{14,13},{15,14},{10,8}... | collective-permute-start | bytes 1806344 | tf_op jit(solution)/shard_map/ppermute | solution.py:41
  19.8 24.2 %copy-start.3 = (f32[392,384]{1,0:T(8,128)}, f32[392,384]{1,0:T(8,128)S(1)}, u32[]{:S(2)}) copy-start(f32[392,384]{1,0:T(8,128)S(1)} %collective-permute-done.8.refs_4_) | copy-start | bytes 1806340
  19.8 21.3 %collective-permute-start.10 = (f32[392,384]{1,0:T(8,128)S(1)}, f32[392,384]{1,0:T(8,128)}, u32[]{:S(2)}, u32[]{:S(2)}) collective-permute-start(f32[392,384]{1,0:T(8,128)S(1)} %collective-permute-done.8.refs_4_), channel_id=1, source_target_pairs={{1,0},{2,1},{5,4},{6,5},{10,9},{14,12},{17,16},{18,17},{21,20},{22... | collective-permute-start | bytes 1806344 | tf_op jit(solution)/shard_map/ppermute | solution.py:41
  25.2 17.5 %collective-permute-start.11 = (f32[392,384]{1,0:T(8,128)}, f32[392,384]{1,0:T(8,128)}, u32[]{:S(2)}, u32[]{:S(2)}) collective-permute-start(f32[392,384]{1,0:T(8,128)} %collective-permute-done.9.refs_5_), channel_id=1, source_target_pairs={{1,2},{5,6},{6,7},{9,10},{10,11},{13,15},{17,18},{21,22},{22,23},{... | collective-permute-start | bytes 1806344 | tf_op jit(solution)/shard_map/ppermute | solution.py:41
  38.1 12.5 %collective-permute-start.6 = (f32[392,384]{1,0:T(8,128)}, f32[392,384]{1,0:T(8,128)}, u32[]{:S(2)}, u32[]{:S(2)}) collective-permute-start(f32[392,384]{1,0:T(8,128)} %collective-permute-done.1.refs_7_), channel_id=1, source_target_pairs={{1,2},{5,6},{6,7},{9,10},{10,11},{13,15},{17,18},{21,22},{22,23},{... | collective-permute-start | bytes 1806344 | tf_op jit(solution)/shard_map/ppermute | solution.py:41
  39.6 12.3 %collective-permute-start.4 = (f32[392,384]{1,0:T(8,128)}, f32[392,384]{1,0:T(8,128)}, u32[]{:S(2)}, u32[]{:S(2)}) collective-permute-start(f32[392,384]{1,0:T(8,128)} %collective-permute-done.3.refs_6_), channel_id=1, source_target_pairs={{1,0},{2,1},{5,4},{6,5},{10,9},{14,12},{17,16},{18,17},{21,20},{22... | collective-permute-start | bytes 1806344 | tf_op jit(solution)/shard_map/ppermute | solution.py:41
  41.0 12.4 %collective-permute-start.12 = (f32[392,384]{1,0:T(8,128)}, f32[392,384]{1,0:T(8,128)}, u32[]{:S(2)}, u32[]{:S(2)}) collective-permute-start(f32[392,384]{1,0:T(8,128)} %collective-permute-done.10.refs_8_), channel_id=1, source_target_pairs={{5,4},{9,8},{21,20},{25,24}} | collective-permute-start | bytes 1806344 | tf_op jit(solution)/shard_map/ppermute | solution.py:41
  42.6 19.3 %collective-permute-start.13 = (f32[392,384]{1,0:T(8,128)}, f32[392,384]{1,0:T(8,128)}, u32[]{:S(2)}, u32[]{:S(2)}) collective-permute-start(f32[392,384]{1,0:T(8,128)} %collective-permute-done.11.refs_9_), channel_id=1, source_target_pairs={{2,3},{6,7},{18,19},{22,23}} | collective-permute-start | bytes 1806344 | tf_op jit(solution)/shard_map/ppermute | solution.py:41
  45.8 4.8 %collective-permute-start = (f32[4,392,384]{2,1,0:T(8,128)S(1)}, f32[4,392,384]{2,1,0:T(8,128)}, u32[]{:S(2)}, u32[]{:S(2)}) collective-permute-start(f32[4,392,384]{2,1,0:T(8,128)S(1)} %param.1), channel_id=1, source_target_pairs={{0,4},{4,0},{8,12},{12,8},{1,5},{5,1},{9,13},{13,9},{2,6},{6,2},{1... | collective-permute-start | bytes 7225352 | tf_op jit(solution)/shard_map/cond/branch_1_fun/ppermute | solution.py:247
  50.6 25.1 %collective-permute-start.7 = (f32[392,384]{1,0:T(8,128)}, f32[392,384]{1,0:T(8,128)S(1)}, u32[]{:S(2)}, u32[]{:S(2)}) collective-permute-start(f32[392,384]{1,0:T(8,128)} %collective-permute-done.6.refs_11_), channel_id=1, source_target_pairs={{2,3},{6,7},{18,19},{22,23}} | collective-permute-start | bytes 1806344 | tf_op jit(solution)/shard_map/ppermute | solution.py:41
  51.9 23.8 %collective-permute-start.5 = (f32[392,384]{1,0:T(8,128)}, f32[392,384]{1,0:T(8,128)}, u32[]{:S(2)}, u32[]{:S(2)}) collective-permute-start(f32[392,384]{1,0:T(8,128)} %collective-permute-done.4.refs_10_), channel_id=1, source_target_pairs={{5,4},{9,8},{21,20},{25,24}} | collective-permute-start | bytes 1806344 | tf_op jit(solution)/shard_map/ppermute | solution.py:41
  75.7 0.8 %copy-start = (f32[392,384]{1,0:T(8,128)}, f32[392,384]{1,0:T(8,128)S(1)}, u32[]{:S(2)}) copy-start(f32[392,384]{1,0:T(8,128)S(1)} %collective-permute-done.7.refs_3_) | copy-start | bytes 1806340

commit v3 on v2

--- a/solution.py
+++ b/solution.py
@@ -41,48 +41,37 @@
     return lax.ppermute(block, AXES, [(j * n + s, j * n + t) for j, s, t in flows])
 
 
-def tag_kernel(cell_ref, in_ref, *rest):
-    slots, rows, columns = in_ref.shape
-    outs, sems = rest[:slots], rest[slots]
-    copies = [pltpu.make_async_copy(in_ref.at[s], outs[s].at[pl.ds(0, rows)], sems.at[s]) for s in range(slots)]
+def tag_kernel(cells_ref, blocks_ref, *rest, apart):
+    slots, rows, columns = blocks_ref.shape
+    outs, (cells, sems, cells_sem) = rest[:-3], rest[-3:]
+    outs = outs if apart else [outs[0].at[s] for s in range(slots)]
+    copies = [pltpu.make_async_copy(blocks_ref.at[s], outs[s].at[pl.ds(0, rows)], sems.at[s]) for s in range(slots)]
+    fetch = pltpu.make_async_copy(cells_ref, cells, cells_sem.at[0])
+    fetch.start()
     for copy in copies:
         copy.start()
+    fetch.wait()
     for s in range(slots):
-        outs[s][pl.ds(rows, PAD)] = jnp.full((PAD, columns), cell_ref[s].astype(jnp.float32))
+        outs[s][pl.ds(rows, PAD)] = jnp.full((PAD, columns), cells[s].astype(jnp.float32))
     for copy in copies:
         copy.wait()
 
 
-def tagged(blocks, cells):
+def tagged(blocks, cells, apart):
     slots, rows, columns = blocks.shape
+    hbm = pl.BlockSpec(memory_space=pltpu.HBM)
+    shapes = [(rows + PAD, columns)] * slots if apart else [(slots, rows + PAD, columns)]
     return pl.pallas_call(
-        tag_kernel,
-        out_shape=[jax.ShapeDtypeStruct((rows + PAD, columns), blocks.dtype)] * slots,
-        in_specs=[pl.BlockSpec(memory_space=pltpu.SMEM), pl.BlockSpec(memory_space=pltpu.HBM)],
-        out_specs=[pl.BlockSpec(memory_space=pltpu.VMEM)] * slots,
-        scratch_shapes=[pltpu.SemaphoreType.DMA((slots,))],
-        compiler_params=pltpu.CompilerParams(vmem_limit_bytes=62 * 1024 * 1024),
-    )(cells, blocks)
-
-
-def tag_all_kernel(cell_ref, in_ref, out_ref, sems):
-    slots, rows, columns = in_ref.shape
-    copy = pltpu.make_async_copy(in_ref, out_ref.at[:, pl.ds(0, rows)], sems.at[0])
-    copy.start()
-    for s in range(slots):
-        out_ref[s, pl.ds(rows, PAD)] = jnp.full((PAD, columns), cell_ref[s].astype(jnp.float32))
-    copy.wait()
-
-
-def tagged_together(blocks, cells):
-    slots, rows, columns = blocks.shape
-    return pl.pallas_call(
-        tag_all_kernel,
-        out_shape=jax.ShapeDtypeStruct((slots, rows + PAD, columns), blocks.dtype),
-        in_specs=[pl.BlockSpec(memory_space=pltpu.SMEM), pl.BlockSpec(memory_space=pltpu.HBM)],
-        out_specs=pl.BlockSpec(memory_space=pltpu.VMEM),
-        scratch_shapes=[pltpu.SemaphoreType.DMA((1,))],
-        compiler_params=pltpu.CompilerParams(vmem_limit_bytes=62 * 1024 * 1024),
+        functools.partial(tag_kernel, apart=apart),
+        out_shape=[jax.ShapeDtypeStruct(shape, blocks.dtype) for shape in shapes],
+        in_specs=[hbm, hbm],
+        out_specs=[pl.BlockSpec(memory_space=pltpu.VMEM)] * len(shapes),
+        scratch_shapes=[
+            pltpu.SMEM((slots,), jnp.int32),
+            pltpu.SemaphoreType.DMA((slots,)),
+            pltpu.SemaphoreType.DMA((1,)),
+        ],
+        compiler_params=pltpu.CompilerParams(vmem_limit_bytes=60 * 1024 * 1024),
     )(cells, blocks)
 
 
@@ -226,6 +215,7 @@
         body = functools.partial(multiply_last, firsts_at=firsts_at, n_arrays=len(arrays), n_second=len(seconds))
         scratch = [pair, block, pair, pltpu.SMEM((slots, PAD, 128), jnp.float32), pltpu.SMEM((PAD, 128), jnp.float32)]
         blocks.append(sums)
+    hbm = hbm if sums is None else pl.BlockSpec(memory_space=pl.ANY)
     return pl.pallas_call(
         body,
         out_shape=jax.ShapeDtypeStruct((slots, rows, columns), jnp.float32),
@@ -238,7 +228,7 @@
             bytes_accessed=4 * rows * columns * (slots + 2 * len(seconds)),
             transcendentals=0,
         ),
-        compiler_params=pltpu.CompilerParams(vmem_limit_bytes=60 * 1024 * 1024),
+        compiler_params=pltpu.CompilerParams(vmem_limit_bytes=(60 if sums is None else 8) * 1024 * 1024),
     )(plan, where, *blocks)
 
 
@@ -249,13 +239,13 @@
 
 
 def by_four(a, a_cells, b, b_cells, where, n):
-    parts = list(tagged(b, b_cells))
+    parts = list(tagged(b, b_cells, True))
     slots = range(len(parts))
     j, i = np.meshgrid(np.arange(n), np.arange(n), indexing="ij")
     down_tiles, up_tiles = origins(DOWN, n), origins(UP, n)
     moved = [(part, np.tile(np.arange(n), (n, 1))) for part in parts]
     a, parts[0] = lax.optimization_barrier((a, parts[0]))
-    a = tagged_together(a, a_cells)
+    (a,) = tagged(a, a_cells, False)
     a_chip = lax.ppermute(a, "row", [(p, p ^ 2) for p in range(n)])
     down, up = list(parts), list(parts)
     last_tiles = [down_tiles[-1], up_tiles[-1]] * len(parts)
@@ -281,7 +271,7 @@
 
 
 def by_any(a, a_cells, b, b_cells, where, n):
-    a, parts = tagged_together(a, a_cells), tagged(b, b_cells)
+    (a,), parts = tagged(a, a_cells, False), tagged(b, b_cells, True)
     firsts, seconds, plan = [], [], []
     here = [(j, i) for j in range(n) for i in range(n)]
     for step in range(STEPS):

time: 80.6 us -> 78.9 us (0.979)
  waiting for transfers between devices: 32.9 us -> 38.8 us
  Pallas kernels: 16.9 us -> 11.3 us
  local copies, waits for them, and re-layouts: 3.21 us -> 1.97 us
    ppermute x12, waiting for transfers between devices: 28.2 us -> 34.1 us  [move(): lax.ppermute(block, AXES, [(j * n + s, j * n + t) for j, s, t in flows])]
    pallas_call x2, Pallas kernels: 10.8 us -> 6.69 us  [add_products(): pl.pallas_call(body, out_shape=jax.ShapeDtypeStruct((slots, rows, columns...]
    pallas_call x2, Pallas kernels: 6.08 us -> 4.61 us  [tagged(): pl.pallas_call(functools.partial(tag_kernel, apart=apart), out_shape=[jax...]
    unnamed x8 -> x10, local copies, waits for them, and re-layouts: 0.84 us -> 0.02 us
  transfers between devices with their start and end apart: 14 -> 14, of which waited for: 6 -> 6; matrix products, arithmetic and copies ran while one was open for 5% -> 5% of each run, Pallas kernels for 15% -> 9%
where the time goes in v3:
time: 78.9 us; the launch traced here: 77.4 us
  waiting for transfers between devices  38.8 us (49%)
  starting transfers between devices  23.2 us (29%)
  Pallas kernels  11.3 us (14%)
  local copies, waits for them, and re-layouts  1.97 us (2%)
  other arithmetic  1.8 us (2%)
    ppermute x12, waiting for transfers between devices, move(): lax.ppermute(block, AXES, [(j * n + s, j * n + t) for j, s, t in flows])  34.1 us
    ppermute x12, starting transfers between devices, move(): lax.ppermute(block, AXES, [(j * n + s, j * n + t) for j, s, t in flows])  21.5 us
    pallas_call x2, Pallas kernels, add_products(): pl.pallas_call(body, out_shape=jax.ShapeDtypeStruct((slots, rows, columns...  6.69 us
    ppermute x1, waiting for transfers between devices, both_cores(): swap = lambda x: lax.ppermute(x, 'row', [(p, p ^ 1) for p in range(n)])  4.72 us
    pallas_call x2, Pallas kernels, tagged(): pl.pallas_call(functools.partial(tag_kernel, apart=apart), out_shape=[jax...  4.61 us
    squeeze x2, local copies, waits for them, and re-layouts, by_four(): jnp.asarray(np.stack(x, -1), jnp.int32)[place]  1.95 us
    concatenate x1, other arithmetic, both_cores(): here = jnp.concatenate([a, a_chip])  1.8 us
  transfers between devices with their start and end apart: 14, of which 6 were waited for; matrix products, arithmetic and copies ran while one was open for 5% of the time, Pallas kernels for 9%

profile of v3, /device:TPU:24, one launch (start us, length us, event | category | flops | bytes accessed | tf_op | source)
XLA Modules:
  0.0 77.4 jit_solution(14654299029077828802)
XLA Ops:
  0.0 2.3 %shard_map.73 = (f32[392,384]{1,0:T(8,128)}, f32[392,384]{1,0:T(8,128)}) custom-call(s32[2]{0:T(128)} %bitcast.17, f32[2,384,384]{2,1,0:T(8,128)} %bitcast.15), custom_call_target="tpu_custom_call" | custom-call | tf_op jit(solution)/shard_map/pallas_call | solution.py:64
  2.3 2.5 %collective-permute-start.8 = (f32[392,384]{1,0:T(8,128)}, f32[392,384]{1,0:T(8,128)S(1)}, u32[]{:S(2)}, u32[]{:S(2)}) collective-permute-start(f32[392,384]{1,0:T(8,128)} %get-tuple-element.22.refs_2_), channel_id=1, source_target_pairs={{1,0},{2,1},{3,2},{5,4},{6,5},{7,6},{13,12},{14,13},{15,14},{10,8}... | collective-permute-start | bytes 1806344 | tf_op jit(solution)/shard_map/ppermute | solution.py:41
  4.8 1.3 %collective-permute-start.9 = (f32[392,384]{1,0:T(8,128)}, f32[392,384]{1,0:T(8,128)S(1)}, u32[]{:S(2)}, u32[]{:S(2)}) collective-permute-start(f32[392,384]{1,0:T(8,128)} %get-tuple-element.22.refs_2_), channel_id=1, source_target_pairs={{0,1},{1,3},{4,5},{5,6},{6,7},{8,9},{9,10},{10,11},{12,13},{13,14}... | collective-permute-start | bytes 1806344 | tf_op jit(solution)/shard_map/ppermute | solution.py:41
  6.1 0.0 copy-start
  6.2 2.3 %shard_map.74 = f32[2,392,384]{2,1,0:T(8,128)} custom-call(s32[2]{0:T(128)} %bitcast.18, f32[2,384,384]{2,1,0:T(8,128)} %bitcast.16), custom_call_target="tpu_custom_call" | custom-call | tf_op jit(solution)/shard_map/pallas_call | solution.py:64
  8.5 1.6 %collective-permute-start.2 = (f32[2,392,384]{2,1,0:T(8,128)}, f32[2,392,384]{2,1,0:T(8,128)}, u32[]{:S(2)}, u32[]{:S(2)}) collective-permute-start(f32[2,392,384]{2,1,0:T(8,128)} %shard_map.74), channel_id=1, source_target_pairs={{0,8},{4,12},{8,0},{12,4},{1,9},{5,13},{9,1},{13,5},{2,10},{6,14},... | collective-permute-start | bytes 3612680 | tf_op jit(solution)/shard_map/ppermute | solution.py:249
  10.0 1.3 %collective-permute-start.1 = (f32[392,384]{1,0:T(8,128)S(1)}, f32[392,384]{1,0:T(8,128)}, u32[]{:S(2)}, u32[]{:S(2)}) collective-permute-start(f32[392,384]{1,0:T(8,128)S(1)} %copy-done.2), channel_id=1, source_target_pairs={{0,1},{1,3},{4,5},{5,6},{6,7},{8,9},{9,10},{10,11},{12,13},{13,14}... | collective-permute-start | bytes 1806344 | tf_op jit(solution)/shard_map/ppermute | solution.py:41
  11.3 5.6 %collective-permute-start.3 = (f32[392,384]{1,0:T(8,128)S(1)}, f32[392,384]{1,0:T(8,128)}, u32[]{:S(2)}, u32[]{:S(2)}) collective-permute-start(f32[392,384]{1,0:T(8,128)S(1)} %copy-done.2), channel_id=1, source_target_pairs={{1,0},{2,1},{3,2},{5,4},{6,5},{7,6},{13,12},{14,13},{15,14},{10,8}... | collective-permute-start | bytes 1806344 | tf_op jit(solution)/shard_map/ppermute | solution.py:41
  16.9 2.2 %collective-permute-done.8.refs_4_ = f32[392,384]{1,0:T(8,128)S(1)} collective-permute-done((f32[392,384]{1,0:T(8,128)}, f32[392,384]{1,0:T(8,128)S(1)}, u32[]{:S(2)}, u32[]{:S(2)}) %collective-permute-start.8) | collective-permute-done | bytes 602144 | tf_op jit(solution)/shard_map/ppermute | solution.py:41
  19.1 1.5 %collective-permute-start.10 = (f32[392,384]{1,0:T(8,128)S(1)}, f32[392,384]{1,0:T(8,128)}, u32[]{:S(2)}, u32[]{:S(2)}) collective-permute-start(f32[392,384]{1,0:T(8,128)S(1)} %collective-permute-done.8.refs_4_), channel_id=1, source_target_pairs={{1,0},{2,1},{5,4},{6,5},{10,9},{14,12},{17,16},{18,17},{21,20},{22... | collective-permute-start | bytes 1806344 | tf_op jit(solution)/shard_map/ppermute | solution.py:41
  20.6 3.8 %collective-permute-done.9.refs_5_ = f32[392,384]{1,0:T(8,128)S(1)} collective-permute-done((f32[392,384]{1,0:T(8,128)}, f32[392,384]{1,0:T(8,128)S(1)}, u32[]{:S(2)}, u32[]{:S(2)}) %collective-permute-start.9) | collective-permute-done | bytes 602144 | tf_op jit(solution)/shard_map/ppermute | solution.py:41
  24.4 1.6 %collective-permute-start.11 = (f32[392,384]{1,0:T(8,128)S(1)}, f32[392,384]{1,0:T(8,128)}, u32[]{:S(2)}, u32[]{:S(2)}) collective-permute-start(f32[392,384]{1,0:T(8,128)S(1)} %collective-permute-done.9.refs_5_), channel_id=1, source_target_pairs={{1,2},{5,6},{6,7},{9,10},{10,11},{13,15},{17,18},{21,22},{22,23},{... | collective-permute-start | bytes 1806344 | tf_op jit(solution)/shard_map/ppermute | solution.py:41
  25.9 0.7 dynamic-slice_bitcast_fusion.plan_ref
  26.6 1.3 %dynamic-slice_bitcast_fusion.1.plan_ref = s32[12]{0:T(128)} fusion(s32[4,4,12]{2,1,0:T(4,128)} %constant.19.clone, s32[]{:T(128)S(6)} %select_n.8, s32[]{:T(128)S(6)} %select_n.9), kind=kLoop, calls=%fused_computation.2 | loop fusion | bytes 104 | tf_op jit(solution)/shard_map/squeeze | solution.py:256
  27.9 9.5 %collective-permute-done.1.refs_7_ = f32[392,384]{1,0:T(8,128)} collective-permute-done((f32[392,384]{1,0:T(8,128)S(1)}, f32[392,384]{1,0:T(8,128)}, u32[]{:S(2)}, u32[]{:S(2)}) %collective-permute-start.1) | collective-permute-done | bytes 602144 | tf_op jit(solution)/shard_map/ppermute | solution.py:41
  37.4 1.5 %collective-permute-start.6 = (f32[392,384]{1,0:T(8,128)}, f32[392,384]{1,0:T(8,128)}, u32[]{:S(2)}, u32[]{:S(2)}) collective-permute-start(f32[392,384]{1,0:T(8,128)} %collective-permute-done.1.refs_7_), channel_id=1, source_target_pairs={{1,2},{5,6},{6,7},{9,10},{10,11},{13,15},{17,18},{21,22},{22,23},{... | collective-permute-start | bytes 1806344 | tf_op jit(solution)/shard_map/ppermute | solution.py:41
  38.9 0.0 collective-permute-done.3.refs_6_
  38.9 1.5 %collective-permute-start.4 = (f32[392,384]{1,0:T(8,128)}, f32[392,384]{1,0:T(8,128)}, u32[]{:S(2)}, u32[]{:S(2)}) collective-permute-start(f32[392,384]{1,0:T(8,128)} %collective-permute-done.3.refs_6_), channel_id=1, source_target_pairs={{1,0},{2,1},{5,4},{6,5},{10,9},{14,12},{17,16},{18,17},{21,20},{22... | collective-permute-start | bytes 1806344 | tf_op jit(solution)/shard_map/ppermute | solution.py:41
  40.4 0.0 collective-permute-done.10.refs_8_
  40.4 1.6 %collective-permute-start.12 = (f32[392,384]{1,0:T(8,128)}, f32[392,384]{1,0:T(8,128)}, u32[]{:S(2)}, u32[]{:S(2)}) collective-permute-start(f32[392,384]{1,0:T(8,128)} %collective-permute-done.10.refs_8_), channel_id=1, source_target_pairs={{5,4},{9,8},{21,20},{25,24}} | collective-permute-start | bytes 1806344 | tf_op jit(solution)/shard_map/ppermute | solution.py:41
  41.9 1.3 %collective-permute-start.13 = (f32[392,384]{1,0:T(8,128)}, f32[392,384]{1,0:T(8,128)}, u32[]{:S(2)}, u32[]{:S(2)}) collective-permute-start(f32[392,384]{1,0:T(8,128)} %collective-permute-done.11.refs_9_), channel_id=1, source_target_pairs={{2,3},{6,7},{18,19},{22,23}} | collective-permute-start | bytes 1806344 | tf_op jit(solution)/shard_map/ppermute | solution.py:41
  43.3 1.8 %pad_maximum_fusion.refs_0_ = f32[4,392,384]{2,1,0:T(8,128)S(1)} fusion(f32[2,392,384]{2,1,0:T(8,128)} %collective-permute-done.2, f32[2,392,384]{2,1,0:T(8,128)} %shard_map.74), kind=kLoop, calls=%fused_computation | loop fusion | flops 602112 | bytes 4816896 | tf_op jit(solution)/shard_map/concatenate | solution.py:236
  45.1 4.8 %conditional.1 = (f32[4,392,384]{2,1,0:T(8,128)}) conditional(s32[]{:T(128)} %bitcast.7, () %tuple.15, f32[4,392,384]{2,1,0:T(8,128)S(1)} %pad_maximum_fusion.refs_0_), branch_computations={%region_0.0_spmd, %region_1.0_spmd} | conditional | bytes 9633840 | solution.py:238
  45.1 0.1 collective-permute-start
  45.2 4.7 %collective-permute-done = f32[4,392,384]{2,1,0:T(8,128)} collective-permute-done((f32[4,392,384]{2,1,0:T(8,128)S(1)}, f32[4,392,384]{2,1,0:T(8,128)}, u32[]{:S(2)}, u32[]{:S(2)}) %collective-permute-start) | collective-permute-done | bytes 2408480 | tf_op jit(solution)/shard_map/cond/branch_1_fun/ppermute | solution.py:237
  49.9 1.3 %collective-permute-start.7 = (f32[392,384]{1,0:T(8,128)}, f32[392,384]{1,0:T(8,128)S(1)}, u32[]{:S(2)}, u32[]{:S(2)}) collective-permute-start(f32[392,384]{1,0:T(8,128)} %collective-permute-done.6.refs_11_), channel_id=1, source_target_pairs={{2,3},{6,7},{18,19},{22,23}} | collective-permute-start | bytes 1806344 | tf_op jit(solution)/shard_map/ppermute | solution.py:41
  51.2 0.0 collective-permute-done.4.refs_10_
  51.2 0.7 collective-permute-start.5
  52.0 9.3 %collective-permute-done.13.refs_13_ = f32[392,384]{1,0:T(8,128)} collective-permute-done((f32[392,384]{1,0:T(8,128)}, f32[392,384]{1,0:T(8,128)}, u32[]{:S(2)}, u32[]{:S(2)}) %collective-permute-start.13) | collective-permute-done | bytes 602144 | tf_op jit(solution)/shard_map/ppermute | solution.py:41
  61.3 4.5 %shard_map.75.refs_4_ = f32[2,384,384]{2,1,0:T(8,128)} custom-call(s32[12]{0:T(128)} %dynamic-slice_bitcast_fusion.1.plan_ref, s32[2]{0:T(128)} %bitcast.12, f32[4,392,384]{2,1,0:T(8,128)S(1)} %pad_maximum_fusion.refs_0_, f32[4,392,384]{2,1,0:T(8,128)} %get-tuple-element.23.refs_1_, f32[392,384]{1,0:T(8,128)} %get-tuple-element.22.refs_2_, ...), custom_call_target="tpu_custom_call" | custom-call | flops 8153726976 | bytes 15335424 | tf_op jit(solution)/shard_map/pallas_call | solution.py:219
  65.7 9.3 %collective-permute-done.7.refs_3_ = f32[392,384]{1,0:T(8,128)S(1)} collective-permute-done((f32[392,384]{1,0:T(8,128)}, f32[392,384]{1,0:T(8,128)S(1)}, u32[]{:S(2)}, u32[]{:S(2)}) %collective-permute-start.7) | collective-permute-done | bytes 602144 | tf_op jit(solution)/shard_map/ppermute | solution.py:41
  75.0 2.2 %shard_map.76 = f32[2,384,384]{2,1,0:T(8,128)} custom-call(s32[2]{0:T(128)S(1)} %dynamic-slice_bitcast_fusion.plan_ref, s32[2]{0:T(128)S(1)} %bitcast.14, f32[4,392,384]{2,1,0:T(8,128)S(1)} %pad_maximum_fusion.refs_0_, f32[4,392,384]{2,1,0:T(8,128)} %get-tuple-element.23.refs_1_, ...), custom_call_target="tpu_custom_call", output_to_operand_aliasing={{}: (6, {})} | custom-call | flops 1358954496 | bytes 3538944 | tf_op jit(solution)/shard_map/pallas_call | solution.py:219
  (14 shorter events, 0.0 us)
Async XLA Ops:
  2.3 7.7 %copy-start.2 = (f32[392,384]{1,0:T(8,128)S(1)}, f32[392,384]{1,0:T(8,128)}, u32[]{:S(2)}) copy-start(f32[392,384]{1,0:T(8,128)} %get-tuple-element.16.refs_3_) | copy-start | bytes 1806340
  2.3 16.8 %collective-permute-start.8 = (f32[392,384]{1,0:T(8,128)}, f32[392,384]{1,0:T(8,128)S(1)}, u32[]{:S(2)}, u32[]{:S(2)}) collective-permute-start(f32[392,384]{1,0:T(8,128)} %get-tuple-element.22.refs_2_), channel_id=1, source_target_pairs={{1,0},{2,1},{3,2},{5,4},{6,5},{7,6},{13,12},{14,13},{15,14},{10,8}... | collective-permute-start | bytes 1806344 | tf_op jit(solution)/shard_map/ppermute | solution.py:41
  4.8 19.5 %collective-permute-start.9 = (f32[392,384]{1,0:T(8,128)}, f32[392,384]{1,0:T(8,128)S(1)}, u32[]{:S(2)}, u32[]{:S(2)}) collective-permute-start(f32[392,384]{1,0:T(8,128)} %get-tuple-element.22.refs_2_), channel_id=1, source_target_pairs={{0,1},{1,3},{4,5},{5,6},{6,7},{8,9},{9,10},{10,11},{12,13},{13,14}... | collective-permute-start | bytes 1806344 | tf_op jit(solution)/shard_map/ppermute | solution.py:41
  6.1 37.1 %copy-start = (s32[1,1,2]{2,1,0:T(1,128)S(1)}, s32[1,1,2]{2,1,0:T(1,128)}, u32[]{:S(2)}) copy-start(s32[1,1,2]{2,1,0:T(1,128)} %param.13) | copy-start | bytes 28
  8.5 34.8 %collective-permute-start.2 = (f32[2,392,384]{2,1,0:T(8,128)}, f32[2,392,384]{2,1,0:T(8,128)}, u32[]{:S(2)}, u32[]{:S(2)}) collective-permute-start(f32[2,392,384]{2,1,0:T(8,128)} %shard_map.74), channel_id=1, source_target_pairs={{0,8},{4,12},{8,0},{12,4},{1,9},{5,13},{9,1},{13,5},{2,10},{6,14},... | collective-permute-start | bytes 3612680 | tf_op jit(solution)/shard_map/ppermute | solution.py:249
  10.0 27.3 %collective-permute-start.1 = (f32[392,384]{1,0:T(8,128)S(1)}, f32[392,384]{1,0:T(8,128)}, u32[]{:S(2)}, u32[]{:S(2)}) collective-permute-start(f32[392,384]{1,0:T(8,128)S(1)} %copy-done.2), channel_id=1, source_target_pairs={{0,1},{1,3},{4,5},{5,6},{6,7},{8,9},{9,10},{10,11},{12,13},{13,14}... | collective-permute-start | bytes 1806344 | tf_op jit(solution)/shard_map/ppermute | solution.py:41
  11.3 27.6 %collective-permute-start.3 = (f32[392,384]{1,0:T(8,128)S(1)}, f32[392,384]{1,0:T(8,128)}, u32[]{:S(2)}, u32[]{:S(2)}) collective-permute-start(f32[392,384]{1,0:T(8,128)S(1)} %copy-done.2), channel_id=1, source_target_pairs={{1,0},{2,1},{3,2},{5,4},{6,5},{7,6},{13,12},{14,13},{15,14},{10,8}... | collective-permute-start | bytes 1806344 | tf_op jit(solution)/shard_map/ppermute | solution.py:41
  19.1 24.2 %copy-start.3 = (f32[392,384]{1,0:T(8,128)}, f32[392,384]{1,0:T(8,128)S(1)}, u32[]{:S(2)}) copy-start(f32[392,384]{1,0:T(8,128)S(1)} %collective-permute-done.8.refs_4_) | copy-start | bytes 1806340
  19.1 21.3 %collective-permute-start.10 = (f32[392,384]{1,0:T(8,128)S(1)}, f32[392,384]{1,0:T(8,128)}, u32[]{:S(2)}, u32[]{:S(2)}) collective-permute-start(f32[392,384]{1,0:T(8,128)S(1)} %collective-permute-done.8.refs_4_), channel_id=1, source_target_pairs={{1,0},{2,1},{5,4},{6,5},{10,9},{14,12},{17,16},{18,17},{21,20},{22... | collective-permute-start | bytes 1806344 | tf_op jit(solution)/shard_map/ppermute | solution.py:41
  24.4 18.9 %copy-start.4 = (f32[392,384]{1,0:T(8,128)}, f32[392,384]{1,0:T(8,128)S(1)}, u32[]{:S(2)}) copy-start(f32[392,384]{1,0:T(8,128)S(1)} %collective-permute-done.9.refs_5_) | copy-start | bytes 1806340
  24.4 17.6 %collective-permute-start.11 = (f32[392,384]{1,0:T(8,128)S(1)}, f32[392,384]{1,0:T(8,128)}, u32[]{:S(2)}, u32[]{:S(2)}) collective-permute-start(f32[392,384]{1,0:T(8,128)S(1)} %collective-permute-done.9.refs_5_), channel_id=1, source_target_pairs={{1,2},{5,6},{6,7},{9,10},{10,11},{13,15},{17,18},{21,22},{22,23},{... | collective-permute-start | bytes 1806344 | tf_op jit(solution)/shard_map/ppermute | solution.py:41
  37.4 12.5 %collective-permute-start.6 = (f32[392,384]{1,0:T(8,128)}, f32[392,384]{1,0:T(8,128)}, u32[]{:S(2)}, u32[]{:S(2)}) collective-permute-start(f32[392,384]{1,0:T(8,128)} %collective-permute-done.1.refs_7_), channel_id=1, source_target_pairs={{1,2},{5,6},{6,7},{9,10},{10,11},{13,15},{17,18},{21,22},{22,23},{... | collective-permute-start | bytes 1806344 | tf_op jit(solution)/shard_map/ppermute | solution.py:41
  38.9 12.3 %collective-permute-start.4 = (f32[392,384]{1,0:T(8,128)}, f32[392,384]{1,0:T(8,128)}, u32[]{:S(2)}, u32[]{:S(2)}) collective-permute-start(f32[392,384]{1,0:T(8,128)} %collective-permute-done.3.refs_6_), channel_id=1, source_target_pairs={{1,0},{2,1},{5,4},{6,5},{10,9},{14,12},{17,16},{18,17},{21,20},{22... | collective-permute-start | bytes 1806344 | tf_op jit(solution)/shard_map/ppermute | solution.py:41
  40.4 11.6 %collective-permute-start.12 = (f32[392,384]{1,0:T(8,128)}, f32[392,384]{1,0:T(8,128)}, u32[]{:S(2)}, u32[]{:S(2)}) collective-permute-start(f32[392,384]{1,0:T(8,128)} %collective-permute-done.10.refs_8_), channel_id=1, source_target_pairs={{5,4},{9,8},{21,20},{25,24}} | collective-permute-start | bytes 1806344 | tf_op jit(solution)/shard_map/ppermute | solution.py:41
  41.9 19.3 %collective-permute-start.13 = (f32[392,384]{1,0:T(8,128)}, f32[392,384]{1,0:T(8,128)}, u32[]{:S(2)}, u32[]{:S(2)}) collective-permute-start(f32[392,384]{1,0:T(8,128)} %collective-permute-done.11.refs_9_), channel_id=1, source_target_pairs={{2,3},{6,7},{18,19},{22,23}} | collective-permute-start | bytes 1806344 | tf_op jit(solution)/shard_map/ppermute | solution.py:41
  45.1 4.8 %collective-permute-start = (f32[4,392,384]{2,1,0:T(8,128)S(1)}, f32[4,392,384]{2,1,0:T(8,128)}, u32[]{:S(2)}, u32[]{:S(2)}) collective-permute-start(f32[4,392,384]{2,1,0:T(8,128)S(1)} %param.1), channel_id=1, source_target_pairs={{0,4},{4,0},{8,12},{12,8},{1,5},{5,1},{9,13},{13,9},{2,6},{6,2},{1... | collective-permute-start | bytes 7225352 | tf_op jit(solution)/shard_map/cond/branch_1_fun/ppermute | solution.py:237
  49.9 25.1 %collective-permute-start.7 = (f32[392,384]{1,0:T(8,128)}, f32[392,384]{1,0:T(8,128)S(1)}, u32[]{:S(2)}, u32[]{:S(2)}) collective-permute-start(f32[392,384]{1,0:T(8,128)} %collective-permute-done.6.refs_11_), channel_id=1, source_target_pairs={{2,3},{6,7},{18,19},{22,23}} | collective-permute-start | bytes 1806344 | tf_op jit(solution)/shard_map/ppermute | solution.py:41
  51.2 23.8 %collective-permute-start.5 = (f32[392,384]{1,0:T(8,128)}, f32[392,384]{1,0:T(8,128)S(1)}, u32[]{:S(2)}, u32[]{:S(2)}) collective-permute-start(f32[392,384]{1,0:T(8,128)} %collective-permute-done.4.refs_10_), channel_id=1, source_target_pairs={{5,4},{9,8},{21,20},{25,24}} | collective-permute-start | bytes 1806344 | tf_op jit(solution)/shard_map/ppermute | solution.py:41
  61.2 13.8 %copy-start.1 = (s32[1,1,2]{2,1,0:T(1,128)S(1)}, s32[1,1,2]{2,1,0:T(1,128)}, u32[]{:S(2)}) copy-start(s32[1,1,2]{2,1,0:T(1,128)} %param.13) | copy-start | bytes 28

commit v4 on v3

v4 whole, which is shorter than its diff:
```python
import functools

import jax
import jax.numpy as jnp
import numpy as np
from jax import lax
from jax.experimental import pallas as pl
from jax.experimental.pallas import tpu as pltpu
from jax.sharding import PartitionSpec as P

TILE = 7
STEPS = 3
PAD = 8
LANES = 128
LATE = 8
AXES = ("row", "col")

DOWN = (
    [(j, s, s - 1) for j in (0, 1, 3) for s in (1, 2, 3)] + [(2, 2, 0), (2, 3, 2)],
    [(0, 1, 0), (0, 2, 1), (1, 1, 0), (1, 2, 1), (2, 2, 1), (3, 2, 0)],
    [(1, 1, 0), (2, 1, 0)],
)
UP = (
    [(0, 0, 1), (0, 1, 3)] + [(j, s, s + 1) for j in (1, 2, 3) for s in (0, 1, 2)],
    [(0, 1, 2), (1, 1, 2), (1, 2, 3), (2, 1, 2), (2, 2, 3), (3, 1, 3)],
    [(0, 2, 3), (1, 2, 3)],
)


def origins(stages, n):
    held = np.tile(np.arange(n), (n, 1))
    out = []
    for flows in stages:
        got = np.full((n, n), -1)
        for j, source, target in flows:
            got[j, target] = held[j, source]
        held = got
        out.append(got)
    return out


def move(block, flows, n):
    return lax.ppermute(block, AXES, [(j * n + s, j * n + t) for j, s, t in flows])


def tag_kernel(cells_ref, blocks_ref, *rest, apart):
    slots, rows, columns = blocks_ref.shape
    outs, (cells, sems, cells_sem) = rest[:-3], rest[-3:]
    blocks = outs if apart else [outs[0].at[s] for s in range(slots)]
    copies = [pltpu.make_async_copy(blocks_ref.at[s], blocks[s].at[pl.ds(0, rows)], sems.at[s]) for s in range(slots)]
    fetch = pltpu.make_async_copy(cells_ref, cells, cells_sem.at[0])
    fetch.start()
    for copy in copies:
        copy.start()
    fetch.wait()
    group = lax.broadcasted_iota(jnp.int32, (PAD, columns), 1) // LANES
    foot = sum(jnp.where(group == s, cells[s], 0) for s in range(slots)).astype(jnp.float32)
    for block in blocks[:1] if apart else blocks:
        block[pl.ds(rows, PAD)] = foot
    for copy in copies:
        copy.wait()


def tag_twice_kernel(cells_ref, blocks_ref, out_ref, wide_ref, both, cells, sems):
    slots, rows, columns = blocks_ref.shape
    copy = pltpu.make_async_copy(blocks_ref, both.at[:, pl.ds(0, rows)], sems.at[0])
    fetch = pltpu.make_async_copy(cells_ref, cells, sems.at[1])
    fetch.start()
    copy.start()
    fetch.wait()
    group = lax.broadcasted_iota(jnp.int32, (PAD, columns), 1) // LANES
    foot = sum(jnp.where(group == s, cells[s], 0) for s in range(slots)).astype(jnp.float32)
    for s in range(slots):
        both[s, pl.ds(rows, PAD)] = foot
    copy.wait()
    copies = [
        pltpu.make_async_copy(both, out_ref, sems.at[0]),
        pltpu.make_async_copy(both, wide_ref.at[pl.ds(0, slots)], sems.at[1]),
    ]
    for copy in copies:
        copy.start()
    for copy in copies:
        copy.wait()


def tagged_twice(blocks, cells):
    slots, rows, columns = blocks.shape
    hbm = pl.BlockSpec(memory_space=pltpu.HBM)
    shapes = [(slots, rows + PAD, columns), (2 * slots, rows + PAD, columns)]
    return pl.pallas_call(
        tag_twice_kernel,
        out_shape=[jax.ShapeDtypeStruct(shape, blocks.dtype) for shape in shapes],
        in_specs=[hbm, hbm],
        out_specs=[hbm] * 2,
        scratch_shapes=[
            pltpu.VMEM(shapes[0], jnp.float32),
            pltpu.SMEM((slots,), jnp.int32),
            pltpu.SemaphoreType.DMA((2,)),
        ],
        compiler_params=pltpu.CompilerParams(vmem_limit_bytes=60 * 1024 * 1024),
    )(cells, blocks)


def tagged(blocks, cells, apart):
    slots, rows, columns = blocks.shape
    hbm = pl.BlockSpec(memory_space=pltpu.HBM)
    shapes = [(rows + PAD, columns)] + [(rows, columns)] * (slots - 1) if apart else [(slots, rows + PAD, columns)]
    return pl.pallas_call(
        functools.partial(tag_kernel, apart=apart),
        out_shape=[jax.ShapeDtypeStruct(shape, blocks.dtype) for shape in shapes],
        in_specs=[hbm, hbm],
        out_specs=[pl.BlockSpec(memory_space=pltpu.VMEM)] * len(shapes),
        scratch_shapes=[
            pltpu.SMEM((slots,), jnp.int32),
            pltpu.SemaphoreType.DMA((slots,)),
            pltpu.SemaphoreType.DMA((1,)),
        ],
        compiler_params=pltpu.CompilerParams(vmem_limit_bytes=60 * 1024 * 1024),
    )(cells, blocks)


def dot_split(a, b):
    a_high, b_high = a.astype(jnp.bfloat16), b.astype(jnp.bfloat16)
    a_low = (a - a_high.astype(jnp.float32)).astype(jnp.bfloat16)
    b_low = (b - b_high.astype(jnp.float32)).astype(jnp.bfloat16)
    dot = functools.partial(jnp.dot, preferred_element_type=jnp.float32)
    return dot(a_high, b_high) + (dot(a_high, b_low) + dot(a_low, b_high))


def row_and_column(cell):
    row = lax.shift_right_logical(cell * 37, 8)
    return row, cell - row * TILE


def kept_cells(a_place, b_place, where_places):
    (a_row, a_column), (b_row, b_column) = a_place, b_place
    matching = a_column == b_row
    return [matching & (a_row == row) & (b_column == column) for row, column in where_places]


def multiply(plan_hbm, where_hbm, *refs, firsts_at, n_arrays, n_flows, n_late):
    arrays, refs = refs[:n_arrays], refs[n_arrays:]
    out_ref, late_ref, a_vmem, b_vmem, tags, row, cells, hits, plan_ref, where_ref, cell_sems, sems = refs[-12:]
    seconds = refs[:-12]
    slots, rows, columns = out_ref.shape
    body, foot = pl.ds(0, rows), pl.ds(rows, PAD)
    blocks_of = [slots] * (n_flows - n_late) + [1] * n_late
    begins = [sum(blocks_of[:f]) for f in range(n_flows)]

    lanes = pl.ds(0, LANES * slots)
    sources = [arrays[k].at[offset, foot, lanes] for k, offset in firsts_at]
    sources += [seconds[n].at[foot, lanes] for n in begins]
    copies = [pltpu.make_async_copy(x, tags.at[n], cell_sems.at[0]) for n, x in enumerate(sources)]
    copies.append(pltpu.make_async_copy(plan_hbm, plan_ref, cell_sems.at[0]))
    copies.append(pltpu.make_async_copy(where_hbm, where_ref, cell_sems.at[0]))
    for copy in copies:
        copy.start()
    out_ref[...] = jnp.zeros_like(out_ref)
    for copy in copies:
        copy.wait()
    lane = lax.broadcasted_iota(jnp.int32, (PAD, LANES), 1)
    packed = jnp.zeros((PAD, LANES), jnp.float32)
    for n in range(len(sources)):
        for s in range(slots):
            packed = jnp.where(lane == slots * n + s, tags[n, :, pl.ds(LANES * s, LANES)], packed)
    row[...] = packed.astype(jnp.int32)
    copy = pltpu.make_async_copy(row, cells, cell_sems.at[0])
    copy.start()
    copy.wait()

    where_places = [row_and_column(where_ref[c]) for c in range(slots)]
    for n in range(LATE):
        late_ref[n] = 0
    count = jnp.int32(0)
    for f in range(n_flows):
        which = plan_ref[f]
        k = sum(jnp.where(which == m, array, 0) for m, (array, _) in enumerate(firsts_at))
        offset = sum(jnp.where(which == m, offset, 0) for m, (_, offset) in enumerate(firsts_at))
        for s in range(slots):
            b_place = row_and_column(cells[0, slots * (len(firsts_at) + f) + s])
            for first_slot in range(slots):
                a_place = row_and_column(cells[0, slots * jnp.maximum(which, 0) + first_slot])
                kept = [jnp.where(x, 1 << c, 0) for c, x in enumerate(kept_cells(a_place, b_place, where_places))]
                hit = jnp.where(which >= 0, sum(kept), 0)
                here = s < blocks_of[f]

                @pl.when(hit > 0)
                def _(f=f, s=s, k=k, offset=offset, first_slot=first_slot, hit=hit, count=count, here=here):
                    if here:
                        for n, x in enumerate((begins[f] + s, k, offset + first_slot, hit)):
                            hits[4 * count + n] = x
                    else:
                        for n, x in ((0, f - (n_flows - n_late)), (1, k), (2, offset), (3 + first_slot, hit)):
                            late_ref[n] = x

                count = count + jnp.where(hit > 0, int(here), 0)

    def fetch(n, slot):
        entry, k, block = (hits[4 * n + x] for x in range(3))
        for e, second in enumerate(seconds):

            @pl.when(entry == e)
            def _():
                pltpu.make_async_copy(second.at[body], b_vmem.at[slot], sems.at[slot]).start()

        for m, array in enumerate(arrays):

            @pl.when(k == m)
            def _():
                pltpu.make_async_copy(array.at[block, body], a_vmem.at[slot], sems.at[slot]).start()

    @pl.when(count > 0)
    def _():
        fetch(0, 0)

    def one_hit(n, carry):
        slot = n % 2

        @pl.when(n + 1 < count)
        def _():
            fetch(n + 1, 1 - slot)

        pltpu.make_async_copy(seconds[0].at[body], b_vmem.at[slot], sems.at[slot]).wait()
        pltpu.make_async_copy(arrays[0].at[0, body], a_vmem.at[slot], sems.at[slot]).wait()
        value = dot_split(a_vmem[slot], b_vmem[slot])
        for c in range(slots):

            @pl.when((hits[4 * n + 3] >> c) & 1 == 1)
            def _():
                out_ref[c] += value

        return carry

    lax.fori_loop(0, count, one_hit, 0)


def multiply_late(late_ref, *refs, n_arrays, n_second):
    arrays, seconds = refs[:n_arrays], refs[n_arrays : n_arrays + n_second]
    sums, a_vmem, b_vmem, c_vmem, sems = refs[-5:]
    slots = sums.shape[0]
    flow, k, offset = (late_ref[n] for n in range(3))
    hits = [late_ref[3 + s] for s in range(slots)]
    touched = functools.reduce(jnp.bitwise_or, hits)

    @pl.when(touched > 0)
    def _():
        copies = []
        for f, second in enumerate(seconds):
            copies.append((flow == f, pltpu.make_async_copy(second, b_vmem, sems.at[0])))
        for s in range(slots):
            for m, array in enumerate(arrays):
                source = array.at[offset + s, pl.ds(0, a_vmem.shape[1])]
                copies.append(((hits[s] > 0) & (k == m), pltpu.make_async_copy(source, a_vmem.at[s], sems.at[1 + s])))
        takes = [pltpu.make_async_copy(sums.at[c], c_vmem.at[c], sems.at[1 + slots]) for c in range(slots)]
        copies += [((touched >> c) & 1 == 1, take) for c, take in enumerate(takes)]
        for wanted, copy in copies:
            pl.when(wanted)(copy.start)
        for wanted, copy in copies:
            pl.when(wanted)(copy.wait)

        def one_slot(s, carry):
            hit = sum(jnp.where(s == t, hits[t], 0) for t in range(slots))

            @pl.when(hit > 0)
            def _():
                value = dot_split(a_vmem[s], b_vmem[...])
                for c in range(slots):

                    @pl.when((hit >> c) & 1 == 1)
                    def _():
                        c_vmem[c] += value

            return carry

        lax.fori_loop(0, slots, one_slot, 0)
        gives = [pltpu.make_async_copy(c_vmem.at[c], sums.at[c], sems.at[1 + slots]) for c in range(slots)]
        for c, give in enumerate(gives):
            pl.when((touched >> c) & 1 == 1)(give.start)
        for c, give in enumerate(gives):
            pl.when((touched >> c) & 1 == 1)(give.wait)


def arrays_of(firsts):
    arrays = list({id(x): x for x, _ in firsts}.values())
    return arrays, [([id(y) for y in arrays].index(id(x)), offset) for x, offset in firsts]


def add_products(plan, where, firsts, flows, n_late):
    slots, rows, columns = where.shape[0], *flows[0][-1].shape
    arrays, firsts_at = arrays_of(firsts)
    seconds = [x for flow in flows for x in flow]
    smem, hbm = pl.BlockSpec(memory_space=pltpu.SMEM), pl.BlockSpec(memory_space=pltpu.HBM)
    both = pltpu.VMEM((2, rows, columns), jnp.float32)
    return pl.pallas_call(
        functools.partial(
            multiply, firsts_at=firsts_at, n_arrays=len(arrays), n_flows=len(flows), n_late=n_late
        ),
        out_shape=[
            jax.ShapeDtypeStruct((slots, rows, columns), jnp.float32),
            jax.ShapeDtypeStruct((LATE,), jnp.int32),
        ],
        in_specs=[hbm] * (2 + len(arrays) + len(seconds)),
        out_specs=[pl.BlockSpec(memory_space=pltpu.VMEM), smem],
        scratch_shapes=[
            both,
            both,
            pltpu.VMEM((len(firsts) + len(flows), PAD, LANES * slots), jnp.float32),
            pltpu.VMEM((PAD, LANES), jnp.int32),
            pltpu.SMEM((PAD, LANES), jnp.int32),
            pltpu.SMEM((4 * slots * slots * len(flows),), jnp.int32),
            pltpu.SMEM(plan.shape, jnp.int32),
            pltpu.SMEM(where.shape, jnp.int32),
            pltpu.SemaphoreType.DMA((1,)),
            pltpu.SemaphoreType.DMA((2,)),
        ],
        cost_estimate=pl.CostEstimate(
            flops=12 * len(seconds) * rows * columns * columns,
            bytes_accessed=4 * rows * columns * (slots + 2 * len(seconds)),
            transcendentals=0,
        ),
        compiler_params=pltpu.CompilerParams(vmem_limit_bytes=60 * 1024 * 1024),
    )(plan, where, *arrays, *seconds)


def add_late_products(late, firsts, seconds, sums):
    slots, rows, columns = sums.shape
    arrays, _ = arrays_of(firsts)
    where_it_is = pl.BlockSpec(memory_space=pl.ANY)
    blocks = [*arrays, *seconds, sums]
    pair = pltpu.VMEM((slots, rows, columns), jnp.float32)
    return pl.pallas_call(
        functools.partial(multiply_late, n_arrays=len(arrays), n_second=len(seconds)),
        out_shape=jax.ShapeDtypeStruct((slots, rows, columns), jnp.float32),
        in_specs=[pl.BlockSpec(memory_space=pltpu.SMEM)] + [where_it_is] * len(blocks),
        out_specs=where_it_is,
        scratch_shapes=[
            pair,
            pltpu.VMEM((rows, columns), jnp.float32),
            pair,
            pltpu.SemaphoreType.DMA((slots + 2,)),
        ],
        input_output_aliases={len(blocks): 0},
        cost_estimate=pl.CostEstimate(
            flops=12 * len(seconds) * rows * columns * columns,
            bytes_accessed=4 * rows * columns * (slots + 2 * len(seconds)),
            transcendentals=0,
        ),
        compiler_params=pltpu.CompilerParams(vmem_limit_bytes=8 * 1024 * 1024),
    )(late, *blocks)


def both_cores(wide, a_chip, where, n):
    here = lax.dynamic_update_slice(wide, a_chip, (a_chip.shape[0], 0, 0))
    swap = lambda x: lax.ppermute(x, "row", [(p, p ^ 1) for p in range(n)])
    return here, lax.cond(where[0] >= 0, swap, jnp.zeros_like, here)


def by_four(a, a_cells, b, b_cells, where, n):
    parts = list(tagged(b, b_cells, True))
    slots = range(len(parts))
    last = slots[-1]
    j, i = np.meshgrid(np.arange(n), np.arange(n), indexing="ij")
    a, parts[0] = lax.optimization_barrier((a, parts[0]))
    a, wide = tagged_twice(a, a_cells)
    a_chip = lax.ppermute(a, "row", [(p, p ^ 2) for p in range(n)])

    tiles = [np.tile(np.arange(n), (n, 1))]
    for down_tiles, up_tiles in zip(origins(DOWN, n), origins(UP, n)):
        tiles += [down_tiles, up_tiles]
    plan = [np.where((tile >= 0) & ((tile - i - j) % n < STEPS), tile ^ j, -1) for tile in tiles]
    assert not np.any((plan[-2] >= 0) & (plan[-1] >= 0))
    plan = jnp.asarray(np.stack(plan, -1), jnp.int32)[lax.axis_index("row"), lax.axis_index("col")]

    flows = [parts]
    down, up = list(parts), list(parts)
    for stage in range(len(DOWN)):
        for s in slots:
            if (stage, s) == (1, last):
                up[s], plan = lax.optimization_barrier((up[s], plan))
            down[s], up[s] = move(down[s], DOWN[stage], n), move(up[s], UP[stage], n)
        flows += [list(down), list(up)]
    here, there = both_cores(wide, a_chip, where, n)
    firsts = [(here, 0), (there, 0), (here, len(parts)), (there, len(parts))]
    late_blocks = [flow.pop() for flow in flows[-2:]]
    sums, late = add_products(plan, where, firsts, flows, 2)
    return add_late_products(late, firsts, late_blocks, sums)


def by_any(a, a_cells, b, b_cells, where, n):
    (a,), parts = tagged(a, a_cells, False), tagged(b, b_cells, True)
    firsts, flows = [], []
    here = [(j, i) for j in range(n) for i in range(n)]
    for step in range(STEPS):
        from_row = [(((i + j + step) % n) * n + i, j * n + i) for j, i in here]
        from_col = [(j * n + (i + j + step) % n, j * n + i) for j, i in here]
        firsts.append((lax.ppermute(a, AXES, from_row), 0))
        flows.append([lax.ppermute(part, AXES, from_col) for part in parts])
    return add_products(jnp.arange(STEPS, dtype=jnp.int32), where, firsts, flows, 0)[0]


def on_device(a_blocks, first_factor_cell_index, b_blocks, second_factor_cell_index, c_where):
    n = lax.axis_size("row")
    blocks = (a_blocks, first_factor_cell_index, b_blocks, second_factor_cell_index, c_where)
    return (by_four if n == 4 else by_any)(*(x[0, 0] for x in blocks), n)[None, None]


def solution(mesh):
    return jax.shard_map(
        on_device,
        mesh=mesh,
        in_specs=(
            P(("groups", "col"), "row", None, None, None),
            P(("groups", "col"), "row", None),
            P(("groups", "col"), "row", None, None, None),
            P(("groups", "col"), "row", None),
            P(("groups", "col"), "row", None),
        ),
        out_specs=P(("groups", "col"), "row", None, None, None),
        check_vma=False,
    )
```

time: 78.9 us -> 76 us (0.963)
  waiting for transfers between devices: 38.8 us -> 34.5 us
  starting transfers between devices: 23.2 us -> 25.9 us
  other arithmetic: 1.8 us -> 0 us
  local copies, waits for them, and re-layouts: 1.97 us -> 2.98 us
  Pallas kernels: 11.3 us -> 10.5 us
    ppermute x12, waiting for transfers between devices: 34.1 us -> 30 us  [move(): lax.ppermute(block, AXES, [(j * n + s, j * n + t) for j, s, t in flows])]
    ppermute x1, starting transfers between devices: 0.07 us -> 3.86 us  [both_cores(): swap = lambda x: lax.ppermute(x, 'row', [(p, p ^ 1) for p in range(n)])]
    pallas_call x2 -> x1, Pallas kernels: 4.61 us -> 2.31 us  [tagged(): pl.pallas_call(functools.partial(tag_kernel, apart=apart), out_shape=[jax...]
    concatenate x1 -> x0, other arithmetic: 1.8 us -> none  [both_cores(): here = jnp.concatenate([a, a_chip])]
    pallas_call x2 -> x3, Pallas kernels: 6.69 us -> 8.16 us  [the longest x1 4.88 us: add_products(): pl.pallas_call(functools.partial(multiply, firsts_at=firsts_at, n_arrays=...]
    dynamic_update_slice x0 -> x1, local copies, waits for them, and re-layouts: none -> 1.1 us  [both_cores(): here = lax.dynamic_update_slice(wide, a_chip, (a_chip.shape[0], 0, 0))]
    ppermute x12, starting transfers between devices: 21.5 us -> 20.5 us  [move(): lax.ppermute(block, AXES, [(j * n + s, j * n + t) for j, s, t in flows])]
    squeeze x2 -> x1, local copies, waits for them, and re-layouts: 1.95 us -> 1.2 us  [by_four(): jnp.asarray(np.stack(plan, -1), jnp.int32)]
  transfers between devices with their start and end apart: 14 -> 14, of which waited for: 6 -> 6; matrix products, arithmetic and copies ran while one was open for 5% -> 3% of each run, Pallas kernels for 9% -> 10%
where the time goes in v4:
time: 76 us; the launch traced here: 74.6 us
  waiting for transfers between devices  34.5 us (45%)
  starting transfers between devices  25.9 us (34%)
  Pallas kernels  10.5 us (14%)
  local copies, waits for them, and re-layouts  2.98 us (4%)
  between operations  0.77 us (1%)
    ppermute x12, waiting for transfers between devices, move(): lax.ppermute(block, AXES, [(j * n + s, j * n + t) for j, s, t in flows])  30 us
    ppermute x12, starting transfers between devices, move(): lax.ppermute(block, AXES, [(j * n + s, j * n + t) for j, s, t in flows])  20.5 us
    pallas_call x1, Pallas kernels, add_products(): pl.pallas_call(functools.partial(multiply, firsts_at=firsts_at, n_arrays=...  4.88 us
    ppermute x1, waiting for transfers between devices, both_cores(): swap = lambda x: lax.ppermute(x, 'row', [(p, p ^ 1) for p in range(n)])  4.57 us
    ppermute x1, starting transfers between devices, both_cores(): swap = lambda x: lax.ppermute(x, 'row', [(p, p ^ 1) for p in range(n)])  3.86 us
    pallas_call x1, Pallas kernels, tagged_twice(): pl.pallas_call(tag_twice_kernel, out_shape=[jax.ShapeDtypeStruct(shape, b...  2.7 us
    pallas_call x1, Pallas kernels, tagged(): pl.pallas_call(functools.partial(tag_kernel, apart=apart), out_shape=[jax...  2.31 us
    ppermute x1, starting transfers between devices, by_four(): a_chip = lax.ppermute(a, 'row', [(p, p ^ 2) for p in range(n)])  1.56 us
  transfers between devices with their start and end apart: 14, of which 6 were waited for; matrix products, arithmetic and copies ran while one was open for 3% of the time, Pallas kernels for 10%

profile of v4, /device:TPU:24, one launch (start us, length us, event | category | flops | bytes accessed | tf_op | source)
XLA Modules:
  0.0 74.6 jit_solution(5626714100049601003)
XLA Ops:
  0.0 2.3 %shard_map.64 = (f32[392,384]{1,0:T(8,128)}, f32[384,384]{1,0:T(8,128)}) custom-call(s32[2]{0:T(128)} %bitcast.12, f32[2,384,384]{2,1,0:T(8,128)} %bitcast.10), custom_call_target="tpu_custom_call" | custom-call | tf_op jit(solution)/shard_map/pallas_call | solution.py:108
  2.3 2.4 %collective-permute-start.3 = (f32[392,384]{1,0:T(8,128)}, f32[392,384]{1,0:T(8,128)S(1)}, u32[]{:S(2)}, u32[]{:S(2)}) collective-permute-start(f32[392,384]{1,0:T(8,128)} %get-tuple-element.25.refs_2_), channel_id=1, source_target_pairs={{1,0},{2,1},{3,2},{5,4},{6,5},{7,6},{13,12},{14,13},{15,14},{10,8}... | collective-permute-start | bytes 1806344 | tf_op jit(solution)/shard_map/ppermute | solution.py:43
  4.7 1.3 %collective-permute-start.5 = (f32[392,384]{1,0:T(8,128)}, f32[392,384]{1,0:T(8,128)S(1)}, u32[]{:S(2)}, u32[]{:S(2)}) collective-permute-start(f32[392,384]{1,0:T(8,128)} %get-tuple-element.25.refs_2_), channel_id=1, source_target_pairs={{0,1},{1,3},{4,5},{5,6},{6,7},{8,9},{9,10},{10,11},{12,13},{13,14}... | collective-permute-start | bytes 1806344 | tf_op jit(solution)/shard_map/ppermute | solution.py:43
  6.0 2.7 %shard_map.65 = (f32[2,392,384]{2,1,0:T(8,128)}, f32[4,392,384]{2,1,0:T(8,128)}) custom-call(s32[2]{0:T(128)} %bitcast.13, f32[2,384,384]{2,1,0:T(8,128)} %bitcast.11), custom_call_target="tpu_custom_call" | custom-call | tf_op jit(solution)/shard_map/pallas_call | solution.py:90
  8.7 1.6 %collective-permute-start.2 = (f32[2,392,384]{2,1,0:T(8,128)}, f32[2,392,384]{2,1,0:T(8,128)S(1)}, u32[]{:S(2)}, u32[]{:S(2)}) collective-permute-start(f32[2,392,384]{2,1,0:T(8,128)} %get-tuple-element.24), channel_id=1, source_target_pairs={{0,8},{4,12},{8,0},{12,4},{1,9},{5,13},{9,1},{13,5},{2,10},{6,14},... | collective-permute-start | bytes 3612680 | tf_op jit(solution)/shard_map/ppermute | solution.py:365
  10.3 1.3 %collective-permute-start.1 = (f32[384,384]{1,0:T(8,128)}, f32[384,384]{1,0:T(8,128)S(1)}, u32[]{:S(2)}, u32[]{:S(2)}) collective-permute-start(f32[384,384]{1,0:T(8,128)} %get-tuple-element.19.refs_3_), channel_id=1, source_target_pairs={{0,1},{1,3},{4,5},{5,6},{6,7},{8,9},{9,10},{10,11},{12,13},{13,14}... | collective-permute-start | bytes 1769480 | tf_op jit(solution)/shard_map/ppermute | solution.py:43
  11.6 4.8 %collective-permute-start.4 = (f32[384,384]{1,0:T(8,128)}, f32[384,384]{1,0:T(8,128)}, u32[]{:S(2)}, u32[]{:S(2)}) collective-permute-start(f32[384,384]{1,0:T(8,128)} %get-tuple-element.19.refs_3_), channel_id=1, source_target_pairs={{1,0},{2,1},{3,2},{5,4},{6,5},{7,6},{13,12},{14,13},{15,14},{10,8}... | collective-permute-start | bytes 1769480 | tf_op jit(solution)/shard_map/ppermute | solution.py:43
  16.3 2.6 %collective-permute-done.3.refs_4_ = f32[392,384]{1,0:T(8,128)S(1)} collective-permute-done((f32[392,384]{1,0:T(8,128)}, f32[392,384]{1,0:T(8,128)S(1)}, u32[]{:S(2)}, u32[]{:S(2)}) %collective-permute-start.3) | collective-permute-done | bytes 602144 | tf_op jit(solution)/shard_map/ppermute | solution.py:43
  19.0 1.5 %collective-permute-start.6 = (f32[392,384]{1,0:T(8,128)S(1)}, f32[392,384]{1,0:T(8,128)}, u32[]{:S(2)}, u32[]{:S(2)}) collective-permute-start(f32[392,384]{1,0:T(8,128)S(1)} %collective-permute-done.3.refs_4_), channel_id=1, source_target_pairs={{1,0},{2,1},{5,4},{6,5},{10,9},{14,12},{17,16},{18,17},{21,20},{22... | collective-permute-start | bytes 1806344 | tf_op jit(solution)/shard_map/ppermute | solution.py:43
  20.4 3.8 %collective-permute-done.5.refs_6_ = f32[392,384]{1,0:T(8,128)S(1)} collective-permute-done((f32[392,384]{1,0:T(8,128)}, f32[392,384]{1,0:T(8,128)S(1)}, u32[]{:S(2)}, u32[]{:S(2)}) %collective-permute-start.5) | collective-permute-done | bytes 602144 | tf_op jit(solution)/shard_map/ppermute | solution.py:43
  24.3 1.5 %collective-permute-start.8 = (f32[392,384]{1,0:T(8,128)S(1)}, f32[392,384]{1,0:T(8,128)}, u32[]{:S(2)}, u32[]{:S(2)}) collective-permute-start(f32[392,384]{1,0:T(8,128)S(1)} %collective-permute-done.5.refs_6_), channel_id=1, source_target_pairs={{1,2},{5,6},{6,7},{9,10},{10,11},{13,15},{17,18},{21,22},{22,23},{... | collective-permute-start | bytes 1806344 | tf_op jit(solution)/shard_map/ppermute | solution.py:43
  25.8 1.2 %dynamic-slice_bitcast_fusion.plan_hbm = s32[7]{0:T(128)} fusion(s32[4,4,7]{2,1,0:T(4,128)} %constant.19.clone, s32[]{:T(128)S(6)} %select_n.6, s32[]{:T(128)S(6)} %select_n.7), kind=kLoop, calls=%fused_computation.1 | loop fusion | bytes 64 | tf_op jit(solution)/shard_map/squeeze | solution.py:372
  27.0 9.9 %collective-permute-done.1.refs_7_ = f32[384,384]{1,0:T(8,128)S(1)} collective-permute-done((f32[384,384]{1,0:T(8,128)}, f32[384,384]{1,0:T(8,128)S(1)}, u32[]{:S(2)}, u32[]{:S(2)}) %collective-permute-start.1) | collective-permute-done | bytes 589856 | tf_op jit(solution)/shard_map/ppermute | solution.py:43
  36.9 1.5 %collective-permute-start.9 = (f32[384,384]{1,0:T(8,128)S(1)}, f32[384,384]{1,0:T(8,128)}, u32[]{:S(2)}, u32[]{:S(2)}) collective-permute-start(f32[384,384]{1,0:T(8,128)S(1)} %collective-permute-done.1.refs_7_), channel_id=1, source_target_pairs={{1,2},{5,6},{6,7},{9,10},{10,11},{13,15},{17,18},{21,22},{22,23},{... | collective-permute-start | bytes 1769480 | tf_op jit(solution)/shard_map/ppermute | solution.py:43
  38.4 0.0 collective-permute-done.4.refs_5_
  38.4 1.5 %collective-permute-start.7 = (f32[384,384]{1,0:T(8,128)}, f32[384,384]{1,0:T(8,128)}, u32[]{:S(2)}, u32[]{:S(2)}) collective-permute-start(f32[384,384]{1,0:T(8,128)} %collective-permute-done.4.refs_5_), channel_id=1, source_target_pairs={{1,0},{2,1},{5,4},{6,5},{10,9},{14,12},{17,16},{18,17},{21,20},{22... | collective-permute-start | bytes 1769480 | tf_op jit(solution)/shard_map/ppermute | solution.py:43
  39.9 1.5 %collective-permute-start.10 = (f32[392,384]{1,0:T(8,128)}, f32[392,384]{1,0:T(8,128)}, u32[]{:S(2)}, u32[]{:S(2)}) collective-permute-start(f32[392,384]{1,0:T(8,128)} %collective-permute-done.6.refs_8_), channel_id=1, source_target_pairs={{5,4},{9,8},{21,20},{25,24}} | collective-permute-start | bytes 1806344 | tf_op jit(solution)/shard_map/ppermute | solution.py:43
  41.4 1.3 %collective-permute-start.11 = (f32[392,384]{1,0:T(8,128)}, f32[392,384]{1,0:T(8,128)}, u32[]{:S(2)}, u32[]{:S(2)}) collective-permute-start(f32[392,384]{1,0:T(8,128)} %collective-permute-done.8.refs_10_), channel_id=1, source_target_pairs={{2,3},{6,7},{18,19},{22,23}} | collective-permute-start | bytes 1806344 | tf_op jit(solution)/shard_map/ppermute | solution.py:43
  43.3 0.0 collective-permute-done.9.refs_11_
  43.3 1.3 %collective-permute-start.13 = (f32[384,384]{1,0:T(8,128)}, f32[384,384]{1,0:T(8,128)S(1)}, u32[]{:S(2)}, u32[]{:S(2)}) collective-permute-start(f32[384,384]{1,0:T(8,128)} %collective-permute-done.9.refs_11_), channel_id=1, source_target_pairs={{2,3},{6,7},{18,19},{22,23}} | collective-permute-start | bytes 1769480 | tf_op jit(solution)/shard_map/ppermute | solution.py:43
  44.7 0.7 collective-permute-start.12
  45.4 1.1 %constant_dynamic-update-slice_fusion.refs_0_ = f32[4,392,384]{2,1,0:T(8,128)} fusion(f32[4,392,384]{2,1,0:T(8,128)} %get-tuple-element.23, f32[2,392,384]{2,1,0:T(8,128)S(1)} %collective-permute-done.2), kind=kLoop, calls=%fused_computation | loop fusion | bytes 2408448 | tf_op jit(solution)/shard_map/dynamic_update_slice | solution.py:353
  46.5 8.4 %conditional.1 = (f32[4,392,384]{2,1,0:T(8,128)}) conditional(s32[]{:T(128)} %bitcast.6, () %tuple.15, f32[4,392,384]{2,1,0:T(8,128)} %constant_dynamic-update-slice_fusion.refs_0_), branch_computations={%region_0.0_spmd, %region_1.0_spmd} | conditional | bytes 9633840 | solution.py:355
  46.5 3.9 %collective-permute-start = (f32[4,392,384]{2,1,0:T(8,128)}, f32[4,392,384]{2,1,0:T(8,128)}, u32[]{:S(2)}, u32[]{:S(2)}) collective-permute-start(f32[4,392,384]{2,1,0:T(8,128)} %param.1), channel_id=1, source_target_pairs={{0,4},{4,0},{8,12},{12,8},{1,5},{5,1},{9,13},{13,9},{2,6},{6,2},{1... | collective-permute-start | bytes 7225352 | tf_op jit(solution)/shard_map/cond/branch_1_fun/ppermute | solution.py:354
  50.3 4.6 %collective-permute-done = f32[4,392,384]{2,1,0:T(8,128)} collective-permute-done((f32[4,392,384]{2,1,0:T(8,128)}, f32[4,392,384]{2,1,0:T(8,128)}, u32[]{:S(2)}, u32[]{:S(2)}) %collective-permute-start) | collective-permute-done | bytes 2408480 | tf_op jit(solution)/shard_map/cond/branch_1_fun/ppermute | solution.py:354
  54.9 0.0 collective-permute-done.10.refs_12_
  54.9 6.1 %collective-permute-done.11.refs_13_ = f32[392,384]{1,0:T(8,128)} collective-permute-done((f32[392,384]{1,0:T(8,128)}, f32[392,384]{1,0:T(8,128)}, u32[]{:S(2)}, u32[]{:S(2)}) %collective-permute-start.11) | collective-permute-done | bytes 602144 | tf_op jit(solution)/shard_map/ppermute | solution.py:43
  61.1 4.9 %shard_map.66 = (f32[2,384,384]{2,1,0:T(8,128)}, s32[8]{0:T(128)}) custom-call(s32[7]{0:T(128)} %dynamic-slice_bitcast_fusion.plan_hbm, s32[2]{0:T(128)} %bitcast.15, f32[4,392,384]{2,1,0:T(8,128)} %constant_dynamic-update-slice_fusion.refs_0_, f32[4,392,384]{2,1,0:T(8,128)} %get-tuple-element.29.refs_1_, f32[392,384]{1,0:T(8,128)} %get-tuple-element.25.refs_2_, ...), custom_call_target="tpu_custom_call" | custom-call | flops 8153726976 | bytes 15335424 | tf_op jit(solution)/shard_map/pallas_call | solution.py:294
  65.9 7.5 %collective-permute-done.13.refs_3_ = f32[384,384]{1,0:T(8,128)S(1)} collective-permute-done((f32[384,384]{1,0:T(8,128)}, f32[384,384]{1,0:T(8,128)S(1)}, u32[]{:S(2)}, u32[]{:S(2)}) %collective-permute-start.13) | collective-permute-done | bytes 589856 | tf_op jit(solution)/shard_map/ppermute | solution.py:43
  73.4 0.0 collective-permute-done.12.refs_2_
  73.4 0.7 copy-done
  74.1 0.6 shard_map.67
  (11 shorter events, 0.0 us)
Async XLA Ops:
  2.3 16.7 %collective-permute-start.3 = (f32[392,384]{1,0:T(8,128)}, f32[392,384]{1,0:T(8,128)S(1)}, u32[]{:S(2)}, u32[]{:S(2)}) collective-permute-start(f32[392,384]{1,0:T(8,128)} %get-tuple-element.25.refs_2_), channel_id=1, source_target_pairs={{1,0},{2,1},{3,2},{5,4},{6,5},{7,6},{13,12},{14,13},{15,14},{10,8}... | collective-permute-start | bytes 1806344 | tf_op jit(solution)/shard_map/ppermute | solution.py:43
  4.7 19.5 %collective-permute-start.5 = (f32[392,384]{1,0:T(8,128)}, f32[392,384]{1,0:T(8,128)S(1)}, u32[]{:S(2)}, u32[]{:S(2)}) collective-permute-start(f32[392,384]{1,0:T(8,128)} %get-tuple-element.25.refs_2_), channel_id=1, source_target_pairs={{0,1},{1,3},{4,5},{5,6},{6,7},{8,9},{9,10},{10,11},{12,13},{13,14}... | collective-permute-start | bytes 1806344 | tf_op jit(solution)/shard_map/ppermute | solution.py:43
  8.7 36.6 %collective-permute-start.2 = (f32[2,392,384]{2,1,0:T(8,128)}, f32[2,392,384]{2,1,0:T(8,128)S(1)}, u32[]{:S(2)}, u32[]{:S(2)}) collective-permute-start(f32[2,392,384]{2,1,0:T(8,128)} %get-tuple-element.24), channel_id=1, source_target_pairs={{0,8},{4,12},{8,0},{12,4},{1,9},{5,13},{9,1},{13,5},{2,10},{6,14},... | collective-permute-start | bytes 3612680 | tf_op jit(solution)/shard_map/ppermute | solution.py:365
  10.3 26.6 %collective-permute-start.1 = (f32[384,384]{1,0:T(8,128)}, f32[384,384]{1,0:T(8,128)S(1)}, u32[]{:S(2)}, u32[]{:S(2)}) collective-permute-start(f32[384,384]{1,0:T(8,128)} %get-tuple-element.19.refs_3_), channel_id=1, source_target_pairs={{0,1},{1,3},{4,5},{5,6},{6,7},{8,9},{9,10},{10,11},{12,13},{13,14}... | collective-permute-start | bytes 1769480 | tf_op jit(solution)/shard_map/ppermute | solution.py:43
  11.6 26.8 %collective-permute-start.4 = (f32[384,384]{1,0:T(8,128)}, f32[384,384]{1,0:T(8,128)}, u32[]{:S(2)}, u32[]{:S(2)}) collective-permute-start(f32[384,384]{1,0:T(8,128)} %get-tuple-element.19.refs_3_), channel_id=1, source_target_pairs={{1,0},{2,1},{3,2},{5,4},{6,5},{7,6},{13,12},{14,13},{15,14},{10,8}... | collective-permute-start | bytes 1769480 | tf_op jit(solution)/shard_map/ppermute | solution.py:43
  19.0 27.5 %copy-start.1 = (f32[392,384]{1,0:T(8,128)}, f32[392,384]{1,0:T(8,128)S(1)}, u32[]{:S(2)}) copy-start(f32[392,384]{1,0:T(8,128)S(1)} %collective-permute-done.3.refs_4_) | copy-start | bytes 1806340
  19.0 20.9 %collective-permute-start.6 = (f32[392,384]{1,0:T(8,128)S(1)}, f32[392,384]{1,0:T(8,128)}, u32[]{:S(2)}, u32[]{:S(2)}) collective-permute-start(f32[392,384]{1,0:T(8,128)S(1)} %collective-permute-done.3.refs_4_), channel_id=1, source_target_pairs={{1,0},{2,1},{5,4},{6,5},{10,9},{14,12},{17,16},{18,17},{21,20},{22... | collective-permute-start | bytes 1806344 | tf_op jit(solution)/shard_map/ppermute | solution.py:43
  24.3 19.1 %copy-start.2 = (f32[392,384]{1,0:T(8,128)}, f32[392,384]{1,0:T(8,128)S(1)}, u32[]{:S(2)}) copy-start(f32[392,384]{1,0:T(8,128)S(1)} %collective-permute-done.5.refs_6_) | copy-start | bytes 1806340
  24.3 17.1 %collective-permute-start.8 = (f32[392,384]{1,0:T(8,128)S(1)}, f32[392,384]{1,0:T(8,128)}, u32[]{:S(2)}, u32[]{:S(2)}) collective-permute-start(f32[392,384]{1,0:T(8,128)S(1)} %collective-permute-done.5.refs_6_), channel_id=1, source_target_pairs={{1,2},{5,6},{6,7},{9,10},{10,11},{13,15},{17,18},{21,22},{22,23},{... | collective-permute-start | bytes 1806344 | tf_op jit(solution)/shard_map/ppermute | solution.py:43
  36.9 7.7 %copy-start.3 = (f32[384,384]{1,0:T(8,128)}, f32[384,384]{1,0:T(8,128)S(1)}, u32[]{:S(2)}) copy-start(f32[384,384]{1,0:T(8,128)S(1)} %collective-permute-done.1.refs_7_) | copy-start | bytes 1769476
  36.9 6.4 %collective-permute-start.9 = (f32[384,384]{1,0:T(8,128)S(1)}, f32[384,384]{1,0:T(8,128)}, u32[]{:S(2)}, u32[]{:S(2)}) collective-permute-start(f32[384,384]{1,0:T(8,128)S(1)} %collective-permute-done.1.refs_7_), channel_id=1, source_target_pairs={{1,2},{5,6},{6,7},{9,10},{10,11},{13,15},{17,18},{21,22},{22,23},{... | collective-permute-start | bytes 1769480 | tf_op jit(solution)/shard_map/ppermute | solution.py:43
  38.4 6.3 %collective-permute-start.7 = (f32[384,384]{1,0:T(8,128)}, f32[384,384]{1,0:T(8,128)}, u32[]{:S(2)}, u32[]{:S(2)}) collective-permute-start(f32[384,384]{1,0:T(8,128)} %collective-permute-done.4.refs_5_), channel_id=1, source_target_pairs={{1,0},{2,1},{5,4},{6,5},{10,9},{14,12},{17,16},{18,17},{21,20},{22... | collective-permute-start | bytes 1769480 | tf_op jit(solution)/shard_map/ppermute | solution.py:43
  39.9 15.1 %collective-permute-start.10 = (f32[392,384]{1,0:T(8,128)}, f32[392,384]{1,0:T(8,128)}, u32[]{:S(2)}, u32[]{:S(2)}) collective-permute-start(f32[392,384]{1,0:T(8,128)} %collective-permute-done.6.refs_8_), channel_id=1, source_target_pairs={{5,4},{9,8},{21,20},{25,24}} | collective-permute-start | bytes 1806344 | tf_op jit(solution)/shard_map/ppermute | solution.py:43
  41.4 19.7 %collective-permute-start.11 = (f32[392,384]{1,0:T(8,128)}, f32[392,384]{1,0:T(8,128)}, u32[]{:S(2)}, u32[]{:S(2)}) collective-permute-start(f32[392,384]{1,0:T(8,128)} %collective-permute-done.8.refs_10_), channel_id=1, source_target_pairs={{2,3},{6,7},{18,19},{22,23}} | collective-permute-start | bytes 1806344 | tf_op jit(solution)/shard_map/ppermute | solution.py:43
  43.3 30.1 %collective-permute-start.13 = (f32[384,384]{1,0:T(8,128)}, f32[384,384]{1,0:T(8,128)S(1)}, u32[]{:S(2)}, u32[]{:S(2)}) collective-permute-start(f32[384,384]{1,0:T(8,128)} %collective-permute-done.9.refs_11_), channel_id=1, source_target_pairs={{2,3},{6,7},{18,19},{22,23}} | collective-permute-start | bytes 1769480 | tf_op jit(solution)/shard_map/ppermute | solution.py:43
  44.7 28.7 %collective-permute-start.12 = (f32[384,384]{1,0:T(8,128)}, f32[384,384]{1,0:T(8,128)S(1)}, u32[]{:S(2)}, u32[]{:S(2)}) collective-permute-start(f32[384,384]{1,0:T(8,128)} %collective-permute-done.7.refs_9_), channel_id=1, source_target_pairs={{5,4},{9,8},{21,20},{25,24}} | collective-permute-start | bytes 1769480 | tf_op jit(solution)/shard_map/ppermute | solution.py:43
  46.5 8.4 %collective-permute-start = (f32[4,392,384]{2,1,0:T(8,128)}, f32[4,392,384]{2,1,0:T(8,128)}, u32[]{:S(2)}, u32[]{:S(2)}) collective-permute-start(f32[4,392,384]{2,1,0:T(8,128)} %param.1), channel_id=1, source_target_pairs={{0,4},{4,0},{8,12},{12,8},{1,5},{5,1},{9,13},{13,9},{2,6},{6,2},{1... | collective-permute-start | bytes 7225352 | tf_op jit(solution)/shard_map/cond/branch_1_fun/ppermute | solution.py:354
  73.4 0.7 copy-start

commit v5 on v4

--- a/solution.py
+++ b/solution.py
@@ -318,7 +318,7 @@
             bytes_accessed=4 * rows * columns * (slots + 2 * len(seconds)),
             transcendentals=0,
         ),
-        compiler_params=pltpu.CompilerParams(vmem_limit_bytes=60 * 1024 * 1024),
+        compiler_params=pltpu.CompilerParams(vmem_limit_bytes=53 * 1024 * 1024),
     )(plan, where, *arrays, *seconds)
 
 

time: 76 us -> 75.7 us (level)
  the two profiles are of different devices: /device:TPU:24 before, /device:TPU:0 now
where the time goes in v5:
time: 75.7 us; the launch traced here: 75.3 us
  waiting for transfers between devices  36.9 us (49%)
  starting transfers between devices  24.3 us (32%)
  Pallas kernels  11.4 us (15%)
  local copies, waits for them, and re-layouts  1.8 us (2%)
  between operations  0.83 us (1%)
    ppermute x12, waiting for transfers between devices, move(): lax.ppermute(block, AXES, [(j * n + s, j * n + t) for j, s, t in flows])  32 us
    ppermute x12, starting transfers between devices, move(): lax.ppermute(block, AXES, [(j * n + s, j * n + t) for j, s, t in flows])  24 us
    pallas_call x1, Pallas kernels, add_products(): pl.pallas_call(functools.partial(multiply, firsts_at=firsts_at, n_arrays=...  5.79 us
    ppermute x1, waiting for transfers between devices, both_cores(): swap = lambda x: lax.ppermute(x, 'row', [(p, p ^ 1) for p in range(n)])  4.94 us
    pallas_call x1, Pallas kernels, tagged_twice(): pl.pallas_call(tag_twice_kernel, out_shape=[jax.ShapeDtypeStruct(shape, b...  2.7 us
    pallas_call x1, Pallas kernels, tagged(): pl.pallas_call(functools.partial(tag_kernel, apart=apart), out_shape=[jax...  2.28 us
  transfers between devices with their start and end apart: 14, of which 7 were waited for; matrix products, arithmetic and copies ran while one was open for 2% of the time, Pallas kernels for 11%

profile of v5, /device:TPU:0, one launch (start us, length us, event | category | flops | bytes accessed | tf_op | source)
XLA Modules:
  0.0 75.3 jit_solution(11525220618536018621)
XLA Ops:
  0.0 2.3 %shard_map.64 = (f32[392,384]{1,0:T(8,128)}, f32[384,384]{1,0:T(8,128)}) custom-call(s32[2]{0:T(128)} %bitcast.14, f32[2,384,384]{2,1,0:T(8,128)} %bitcast.12), custom_call_target="tpu_custom_call" | custom-call | tf_op jit(solution)/shard_map/pallas_call | solution.py:108
  2.3 1.3 %collective-permute-start.3 = (f32[392,384]{1,0:T(8,128)}, f32[392,384]{1,0:T(8,128)S(1)}, u32[]{:S(2)}, u32[]{:S(2)}) collective-permute-start(f32[392,384]{1,0:T(8,128)} %get-tuple-element.25.refs_2_), channel_id=1, source_target_pairs={{1,0},{2,1},{3,2},{5,4},{6,5},{7,6},{13,12},{14,13},{15,14},{10,8}... | collective-permute-start | bytes 1806344 | tf_op jit(solution)/shard_map/ppermute | solution.py:43
  3.6 5.6 %collective-permute-start.5 = (f32[392,384]{1,0:T(8,128)}, f32[392,384]{1,0:T(8,128)S(1)}, u32[]{:S(2)}, u32[]{:S(2)}) collective-permute-start(f32[392,384]{1,0:T(8,128)} %get-tuple-element.25.refs_2_), channel_id=1, source_target_pairs={{0,1},{1,3},{4,5},{5,6},{6,7},{8,9},{9,10},{10,11},{12,13},{13,14}... | collective-permute-start | bytes 1806344 | tf_op jit(solution)/shard_map/ppermute | solution.py:43
  9.2 2.7 %shard_map.65 = (f32[2,392,384]{2,1,0:T(8,128)}, f32[4,392,384]{2,1,0:T(8,128)}) custom-call(s32[2]{0:T(128)} %bitcast.15, f32[2,384,384]{2,1,0:T(8,128)} %bitcast.13), custom_call_target="tpu_custom_call" | custom-call | tf_op jit(solution)/shard_map/pallas_call | solution.py:90
  11.9 0.3 collective-permute-start.2
  12.2 5.8 %collective-permute-start.1 = (f32[384,384]{1,0:T(8,128)}, f32[384,384]{1,0:T(8,128)}, u32[]{:S(2)}, u32[]{:S(2)}) collective-permute-start(f32[384,384]{1,0:T(8,128)} %get-tuple-element.19.refs_3_), channel_id=1, source_target_pairs={{0,1},{1,3},{4,5},{5,6},{6,7},{8,9},{9,10},{10,11},{12,13},{13,14}... | collective-permute-start | bytes 1769480 | tf_op jit(solution)/shard_map/ppermute | solution.py:43
  18.0 1.3 %collective-permute-start.4 = (f32[384,384]{1,0:T(8,128)}, f32[384,384]{1,0:T(8,128)}, u32[]{:S(2)}, u32[]{:S(2)}) collective-permute-start(f32[384,384]{1,0:T(8,128)} %get-tuple-element.19.refs_3_), channel_id=1, source_target_pairs={{1,0},{2,1},{3,2},{5,4},{6,5},{7,6},{13,12},{14,13},{15,14},{10,8}... | collective-permute-start | bytes 1769480 | tf_op jit(solution)/shard_map/ppermute | solution.py:43
  19.3 1.7 %collective-permute-done.3.refs_4_ = f32[392,384]{1,0:T(8,128)S(1)} collective-permute-done((f32[392,384]{1,0:T(8,128)}, f32[392,384]{1,0:T(8,128)S(1)}, u32[]{:S(2)}, u32[]{:S(2)}) %collective-permute-start.3) | collective-permute-done | bytes 602144 | tf_op jit(solution)/shard_map/ppermute | solution.py:43
  21.0 1.3 %collective-permute-start.6 = (f32[392,384]{1,0:T(8,128)S(1)}, f32[392,384]{1,0:T(8,128)}, u32[]{:S(2)}, u32[]{:S(2)}) collective-permute-start(f32[392,384]{1,0:T(8,128)S(1)} %collective-permute-done.3.refs_4_), channel_id=1, source_target_pairs={{1,0},{2,1},{5,4},{6,5},{10,9},{14,12},{17,16},{18,17},{21,20},{22... | collective-permute-start | bytes 1806344 | tf_op jit(solution)/shard_map/ppermute | solution.py:43
  22.3 1.1 %collective-permute-done.5.refs_6_ = f32[392,384]{1,0:T(8,128)S(1)} collective-permute-done((f32[392,384]{1,0:T(8,128)}, f32[392,384]{1,0:T(8,128)S(1)}, u32[]{:S(2)}, u32[]{:S(2)}) %collective-permute-start.5) | collective-permute-done | bytes 602144 | tf_op jit(solution)/shard_map/ppermute | solution.py:43
  23.4 1.5 %collective-permute-start.8 = (f32[392,384]{1,0:T(8,128)S(1)}, f32[392,384]{1,0:T(8,128)}, u32[]{:S(2)}, u32[]{:S(2)}) collective-permute-start(f32[392,384]{1,0:T(8,128)S(1)} %collective-permute-done.5.refs_6_), channel_id=1, source_target_pairs={{1,2},{5,6},{6,7},{9,10},{10,11},{13,15},{17,18},{21,22},{22,23},{... | collective-permute-start | bytes 1806344 | tf_op jit(solution)/shard_map/ppermute | solution.py:43
  24.9 0.7 dynamic-slice_bitcast_fusion.plan_hbm
  25.6 9.3 %collective-permute-done.1.refs_7_ = f32[384,384]{1,0:T(8,128)} collective-permute-done((f32[384,384]{1,0:T(8,128)}, f32[384,384]{1,0:T(8,128)}, u32[]{:S(2)}, u32[]{:S(2)}) %collective-permute-start.1) | collective-permute-done | bytes 589856 | tf_op jit(solution)/shard_map/ppermute | solution.py:43
  34.9 1.5 %collective-permute-start.9 = (f32[384,384]{1,0:T(8,128)}, f32[384,384]{1,0:T(8,128)}, u32[]{:S(2)}, u32[]{:S(2)}) collective-permute-start(f32[384,384]{1,0:T(8,128)} %collective-permute-done.1.refs_7_), channel_id=1, source_target_pairs={{1,2},{5,6},{6,7},{9,10},{10,11},{13,15},{17,18},{21,22},{22,23},{... | collective-permute-start | bytes 1769480 | tf_op jit(solution)/shard_map/ppermute | solution.py:43
  36.4 0.1 collective-permute-done.4.refs_5_
  36.5 1.3 %collective-permute-start.7 = (f32[384,384]{1,0:T(8,128)}, f32[384,384]{1,0:T(8,128)}, u32[]{:S(2)}, u32[]{:S(2)}) collective-permute-start(f32[384,384]{1,0:T(8,128)} %collective-permute-done.4.refs_5_), channel_id=1, source_target_pairs={{1,0},{2,1},{5,4},{6,5},{10,9},{14,12},{17,16},{18,17},{21,20},{22... | collective-permute-start | bytes 1769480 | tf_op jit(solution)/shard_map/ppermute | solution.py:43
  37.8 11.6 %collective-permute-done.6.refs_8_ = f32[392,384]{1,0:T(8,128)} collective-permute-done((f32[392,384]{1,0:T(8,128)S(1)}, f32[392,384]{1,0:T(8,128)}, u32[]{:S(2)}, u32[]{:S(2)}) %collective-permute-start.6) | collective-permute-done | bytes 602144 | tf_op jit(solution)/shard_map/ppermute | solution.py:43
  49.4 1.6 %collective-permute-start.10 = (f32[392,384]{1,0:T(8,128)}, f32[392,384]{1,0:T(8,128)}, u32[]{:S(2)}, u32[]{:S(2)}) collective-permute-start(f32[392,384]{1,0:T(8,128)} %collective-permute-done.6.refs_8_), channel_id=1, source_target_pairs={{5,4},{9,8},{21,20},{25,24}} | collective-permute-start | bytes 1806344 | tf_op jit(solution)/shard_map/ppermute | solution.py:43
  51.0 1.6 %collective-permute-start.11 = (f32[392,384]{1,0:T(8,128)}, f32[392,384]{1,0:T(8,128)}, u32[]{:S(2)}, u32[]{:S(2)}) collective-permute-start(f32[392,384]{1,0:T(8,128)} %collective-permute-done.8.refs_10_), channel_id=1, source_target_pairs={{2,3},{6,7},{18,19},{22,23}} | collective-permute-start | bytes 1806344 | tf_op jit(solution)/shard_map/ppermute | solution.py:43
  53.2 0.0 collective-permute-done.9.refs_11_
  53.2 0.7 collective-permute-start.13
  53.9 8.1 %collective-permute-done.7.refs_9_ = f32[384,384]{1,0:T(8,128)} collective-permute-done((f32[384,384]{1,0:T(8,128)}, f32[384,384]{1,0:T(8,128)}, u32[]{:S(2)}, u32[]{:S(2)}) %collective-permute-start.7) | collective-permute-done | bytes 589856 | tf_op jit(solution)/shard_map/ppermute | solution.py:43
  62.0 0.7 collective-permute-start.12
  62.8 0.0 copy-start
  62.8 0.0 copy-start.1
  62.8 1.1 %constant_dynamic-update-slice_fusion.refs_0_ = f32[4,392,384]{2,1,0:T(8,128)} fusion(f32[4,392,384]{2,1,0:T(8,128)} %get-tuple-element.23, f32[2,392,384]{2,1,0:T(8,128)S(1)} %collective-permute-done.2), kind=kLoop, calls=%fused_computation | loop fusion | bytes 2408448 | tf_op jit(solution)/shard_map/dynamic_update_slice | solution.py:353
  63.9 4.9 %conditional.1 = (f32[4,392,384]{2,1,0:T(8,128)}) conditional(s32[]{:T(128)} %bitcast.6, () %tuple.15, f32[4,392,384]{2,1,0:T(8,128)} %constant_dynamic-update-slice_fusion.refs_0_), branch_computations={%region_0.0_spmd, %region_1.0_spmd} | conditional | bytes 9633840 | solution.py:355
  63.9 0.0 collective-permute-start
  63.9 4.9 %collective-permute-done = f32[4,392,384]{2,1,0:T(8,128)} collective-permute-done((f32[4,392,384]{2,1,0:T(8,128)}, f32[4,392,384]{2,1,0:T(8,128)}, u32[]{:S(2)}, u32[]{:S(2)}) %collective-permute-start) | collective-permute-done | bytes 2408480 | tf_op jit(solution)/shard_map/cond/branch_1_fun/ppermute | solution.py:354
  68.8 0.0 collective-permute-done.10.refs_12_
  68.9 5.8 %shard_map.66 = (f32[2,384,384]{2,1,0:T(8,128)}, s32[8]{0:T(128)S(1)}) custom-call(s32[7]{0:T(128)S(1)} %dynamic-slice_bitcast_fusion.plan_hbm, s32[2]{0:T(128)S(1)} %bitcast.11, f32[4,392,384]{2,1,0:T(8,128)} %constant_dynamic-update-slice_fusion.refs_0_, f32[4,392,384]{2,1,0:T(8,128)} %get-tuple-element.29.refs_1_, f32[392,384]{1,0:T(8,128)} %get-tuple-element.25.refs_2_, ...), custom_call_target="tpu_custom_call" | custom-call | flops 8153726976 | bytes 15335424 | tf_op jit(solution)/shard_map/pallas_call | solution.py:294
  74.7 0.6 shard_map.67
  (13 shorter events, 0.0 us)
Async XLA Ops:
  2.3 18.7 %collective-permute-start.3 = (f32[392,384]{1,0:T(8,128)}, f32[392,384]{1,0:T(8,128)S(1)}, u32[]{:S(2)}, u32[]{:S(2)}) collective-permute-start(f32[392,384]{1,0:T(8,128)} %get-tuple-element.25.refs_2_), channel_id=1, source_target_pairs={{1,0},{2,1},{3,2},{5,4},{6,5},{7,6},{13,12},{14,13},{15,14},{10,8}... | collective-permute-start | bytes 1806344 | tf_op jit(solution)/shard_map/ppermute | solution.py:43
  3.6 19.9 %collective-permute-start.5 = (f32[392,384]{1,0:T(8,128)}, f32[392,384]{1,0:T(8,128)S(1)}, u32[]{:S(2)}, u32[]{:S(2)}) collective-permute-start(f32[392,384]{1,0:T(8,128)} %get-tuple-element.25.refs_2_), channel_id=1, source_target_pairs={{0,1},{1,3},{4,5},{5,6},{6,7},{8,9},{9,10},{10,11},{12,13},{13,14}... | collective-permute-start | bytes 1806344 | tf_op jit(solution)/shard_map/ppermute | solution.py:43
  11.9 50.8 %collective-permute-start.2 = (f32[2,392,384]{2,1,0:T(8,128)}, f32[2,392,384]{2,1,0:T(8,128)S(1)}, u32[]{:S(2)}, u32[]{:S(2)}) collective-permute-start(f32[2,392,384]{2,1,0:T(8,128)} %get-tuple-element.24), channel_id=1, source_target_pairs={{0,8},{4,12},{8,0},{12,4},{1,9},{5,13},{9,1},{13,5},{2,10},{6,14},... | collective-permute-start | bytes 3612680 | tf_op jit(solution)/shard_map/ppermute | solution.py:365
  12.2 22.7 %collective-permute-start.1 = (f32[384,384]{1,0:T(8,128)}, f32[384,384]{1,0:T(8,128)}, u32[]{:S(2)}, u32[]{:S(2)}) collective-permute-start(f32[384,384]{1,0:T(8,128)} %get-tuple-element.19.refs_3_), channel_id=1, source_target_pairs={{0,1},{1,3},{4,5},{5,6},{6,7},{8,9},{9,10},{10,11},{12,13},{13,14}... | collective-permute-start | bytes 1769480 | tf_op jit(solution)/shard_map/ppermute | solution.py:43
  18.0 18.5 %collective-permute-start.4 = (f32[384,384]{1,0:T(8,128)}, f32[384,384]{1,0:T(8,128)}, u32[]{:S(2)}, u32[]{:S(2)}) collective-permute-start(f32[384,384]{1,0:T(8,128)} %get-tuple-element.19.refs_3_), channel_id=1, source_target_pairs={{1,0},{2,1},{3,2},{5,4},{6,5},{7,6},{13,12},{14,13},{15,14},{10,8}... | collective-permute-start | bytes 1769480 | tf_op jit(solution)/shard_map/ppermute | solution.py:43
  21.0 32.2 %copy-start.3 = (f32[392,384]{1,0:T(8,128)}, f32[392,384]{1,0:T(8,128)S(1)}, u32[]{:S(2)}) copy-start(f32[392,384]{1,0:T(8,128)S(1)} %collective-permute-done.3.refs_4_) | copy-start | bytes 1806340
  21.0 28.4 %collective-permute-start.6 = (f32[392,384]{1,0:T(8,128)S(1)}, f32[392,384]{1,0:T(8,128)}, u32[]{:S(2)}, u32[]{:S(2)}) collective-permute-start(f32[392,384]{1,0:T(8,128)S(1)} %collective-permute-done.3.refs_4_), channel_id=1, source_target_pairs={{1,0},{2,1},{5,4},{6,5},{10,9},{14,12},{17,16},{18,17},{21,20},{22... | collective-permute-start | bytes 1806344 | tf_op jit(solution)/shard_map/ppermute | solution.py:43
  23.4 30.5 %copy-start.4 = (f32[392,384]{1,0:T(8,128)}, f32[392,384]{1,0:T(8,128)S(1)}, u32[]{:S(2)}) copy-start(f32[392,384]{1,0:T(8,128)S(1)} %collective-permute-done.5.refs_6_) | copy-start | bytes 1806340
  23.4 27.5 %collective-permute-start.8 = (f32[392,384]{1,0:T(8,128)S(1)}, f32[392,384]{1,0:T(8,128)}, u32[]{:S(2)}, u32[]{:S(2)}) collective-permute-start(f32[392,384]{1,0:T(8,128)S(1)} %collective-permute-done.5.refs_6_), channel_id=1, source_target_pairs={{1,2},{5,6},{6,7},{9,10},{10,11},{13,15},{17,18},{21,22},{22,23},{... | collective-permute-start | bytes 1806344 | tf_op jit(solution)/shard_map/ppermute | solution.py:43
  34.9 18.3 %collective-permute-start.9 = (f32[384,384]{1,0:T(8,128)}, f32[384,384]{1,0:T(8,128)}, u32[]{:S(2)}, u32[]{:S(2)}) collective-permute-start(f32[384,384]{1,0:T(8,128)} %collective-permute-done.1.refs_7_), channel_id=1, source_target_pairs={{1,2},{5,6},{6,7},{9,10},{10,11},{13,15},{17,18},{21,22},{22,23},{... | collective-permute-start | bytes 1769480 | tf_op jit(solution)/shard_map/ppermute | solution.py:43
  36.5 25.5 %collective-permute-start.7 = (f32[384,384]{1,0:T(8,128)}, f32[384,384]{1,0:T(8,128)}, u32[]{:S(2)}, u32[]{:S(2)}) collective-permute-start(f32[384,384]{1,0:T(8,128)} %collective-permute-done.4.refs_5_), channel_id=1, source_target_pairs={{1,0},{2,1},{5,4},{6,5},{10,9},{14,12},{17,16},{18,17},{21,20},{22... | collective-permute-start | bytes 1769480 | tf_op jit(solution)/shard_map/ppermute | solution.py:43
  49.4 19.4 %collective-permute-start.10 = (f32[392,384]{1,0:T(8,128)}, f32[392,384]{1,0:T(8,128)}, u32[]{:S(2)}, u32[]{:S(2)}) collective-permute-start(f32[392,384]{1,0:T(8,128)} %collective-permute-done.6.refs_8_), channel_id=1, source_target_pairs={{5,4},{9,8},{21,20},{25,24}} | collective-permute-start | bytes 1806344 | tf_op jit(solution)/shard_map/ppermute | solution.py:43
  51.0 17.9 %collective-permute-start.11 = (f32[392,384]{1,0:T(8,128)}, f32[392,384]{1,0:T(8,128)}, u32[]{:S(2)}, u32[]{:S(2)}) collective-permute-start(f32[392,384]{1,0:T(8,128)} %collective-permute-done.8.refs_10_), channel_id=1, source_target_pairs={{2,3},{6,7},{18,19},{22,23}} | collective-permute-start | bytes 1806344 | tf_op jit(solution)/shard_map/ppermute | solution.py:43
  53.2 21.4 %collective-permute-start.13 = (f32[384,384]{1,0:T(8,128)}, f32[384,384]{1,0:T(8,128)S(1)}, u32[]{:S(2)}, u32[]{:S(2)}) collective-permute-start(f32[384,384]{1,0:T(8,128)} %collective-permute-done.9.refs_11_), channel_id=1, source_target_pairs={{2,3},{6,7},{18,19},{22,23}} | collective-permute-start | bytes 1769480 | tf_op jit(solution)/shard_map/ppermute | solution.py:43
  62.0 12.6 %collective-permute-start.12 = (f32[384,384]{1,0:T(8,128)}, f32[384,384]{1,0:T(8,128)S(1)}, u32[]{:S(2)}, u32[]{:S(2)}) collective-permute-start(f32[384,384]{1,0:T(8,128)} %collective-permute-done.7.refs_9_), channel_id=1, source_target_pairs={{5,4},{9,8},{21,20},{25,24}} | collective-permute-start | bytes 1769480 | tf_op jit(solution)/shard_map/ppermute | solution.py:43
  62.8 6.1 %copy-start = (f32[384,384]{1,0:T(8,128)S(1)}, f32[384,384]{1,0:T(8,128)}, u32[]{:S(2)}) copy-start(f32[384,384]{1,0:T(8,128)} %get-tuple-element.19.refs_3_) | copy-start | bytes 1769476
  62.8 6.1 %copy-start.1 = (s32[1,1,2]{2,1,0:T(1,128)S(1)}, s32[1,1,2]{2,1,0:T(1,128)}, u32[]{:S(2)}) copy-start(s32[1,1,2]{2,1,0:T(1,128)} %param.12) | copy-start | bytes 28
  63.9 4.9 %collective-permute-start = (f32[4,392,384]{2,1,0:T(8,128)}, f32[4,392,384]{2,1,0:T(8,128)}, u32[]{:S(2)}, u32[]{:S(2)}) collective-permute-start(f32[4,392,384]{2,1,0:T(8,128)} %param.1), channel_id=1, source_target_pairs={{0,4},{4,0},{8,12},{12,8},{1,5},{5,1},{9,13},{13,9},{2,6},{6,2},{1... | collective-permute-start | bytes 7225352 | tf_op jit(solution)/shard_map/cond/branch_1_fun/ppermute | solution.py:354
  68.8 5.8 %copy-start.2 = (f32[4,392,384]{2,1,0:T(8,128)S(1)}, f32[4,392,384]{2,1,0:T(8,128)}, u32[]{:S(2)}) copy-start(f32[4,392,384]{2,1,0:T(8,128)} %constant_dynamic-update-slice_fusion.refs_0_) | copy-start | bytes 7225348

commit v6 on v4

--- a/solution.py
+++ b/solution.py
@@ -234,10 +234,13 @@
     lax.fori_loop(0, count, one_hit, 0)
 
 
-def multiply_late(late_ref, *refs, n_arrays, n_second):
+def multiply_late(late_hbm, *refs, n_arrays, n_second):
     arrays, seconds = refs[:n_arrays], refs[n_arrays : n_arrays + n_second]
-    sums, a_vmem, b_vmem, c_vmem, sems = refs[-5:]
+    sums, a_vmem, b_vmem, c_vmem, late_ref, sems = refs[-6:]
     slots = sums.shape[0]
+    fetch = pltpu.make_async_copy(late_hbm, late_ref, sems.at[0])
+    fetch.start()
+    fetch.wait()
     flow, k, offset = (late_ref[n] for n in range(3))
     hits = [late_ref[3 + s] for s in range(slots)]
     touched = functools.reduce(jnp.bitwise_or, hits)
@@ -325,18 +328,19 @@
 def add_late_products(late, firsts, seconds, sums):
     slots, rows, columns = sums.shape
     arrays, _ = arrays_of(firsts)
-    where_it_is = pl.BlockSpec(memory_space=pl.ANY)
+    where_it_is = pl.BlockSpec(memory_space=pltpu.HBM)
     blocks = [*arrays, *seconds, sums]
     pair = pltpu.VMEM((slots, rows, columns), jnp.float32)
     return pl.pallas_call(
         functools.partial(multiply_late, n_arrays=len(arrays), n_second=len(seconds)),
         out_shape=jax.ShapeDtypeStruct((slots, rows, columns), jnp.float32),
-        in_specs=[pl.BlockSpec(memory_space=pltpu.SMEM)] + [where_it_is] * len(blocks),
+        in_specs=[where_it_is] * (1 + len(blocks)),
         out_specs=where_it_is,
         scratch_shapes=[
             pair,
             pltpu.VMEM((rows, columns), jnp.float32),
             pair,
+            pltpu.SMEM((LATE,), jnp.int32),
             pltpu.SemaphoreType.DMA((slots + 2,)),
         ],
         input_output_aliases={len(blocks): 0},

time: 76 us -> 78.1 us (1.028); the launches traced: 74.6 us -> 77.6 us
  Pallas kernels: 10.5 us -> 13.4 us
    pallas_call x1, Pallas kernels: 0.59 us -> 3.55 us  [add_late_products(): pl.pallas_call(functools.partial(multiply_late, n_arrays=len(arrays), n_s...]
where the time goes in v6:
time: 78.1 us; the launch traced here: 77.6 us
  waiting for transfers between devices  34.5 us (44%)
  starting transfers between devices  25.9 us (33%)
  Pallas kernels  13.4 us (17%)
  local copies, waits for them, and re-layouts  2.98 us (4%)
    ppermute x12, waiting for transfers between devices, move(): lax.ppermute(block, AXES, [(j * n + s, j * n + t) for j, s, t in flows])  30 us
    ppermute x12, starting transfers between devices, move(): lax.ppermute(block, AXES, [(j * n + s, j * n + t) for j, s, t in flows])  20.5 us
    pallas_call x1, Pallas kernels, add_products(): pl.pallas_call(functools.partial(multiply, firsts_at=firsts_at, n_arrays=...  4.88 us
    ppermute x1, waiting for transfers between devices, both_cores(): swap = lambda x: lax.ppermute(x, 'row', [(p, p ^ 1) for p in range(n)])  4.57 us
    ppermute x1, starting transfers between devices, both_cores(): swap = lambda x: lax.ppermute(x, 'row', [(p, p ^ 1) for p in range(n)])  3.86 us
    pallas_call x1, Pallas kernels, add_late_products(): pl.pallas_call(functools.partial(multiply_late, n_arrays=len(arrays), n_s...  3.55 us
    pallas_call x1, Pallas kernels, tagged_twice(): pl.pallas_call(tag_twice_kernel, out_shape=[jax.ShapeDtypeStruct(shape, b...  2.7 us
    pallas_call x1, Pallas kernels, tagged(): pl.pallas_call(functools.partial(tag_kernel, apart=apart), out_shape=[jax...  2.31 us
  transfers between devices with their start and end apart: 14, of which 6 were waited for; matrix products, arithmetic and copies ran while one was open for 3% of the time, Pallas kernels for 10%

profile of v6, /device:TPU:24, one launch (start us, length us, event | category | flops | bytes accessed | tf_op | source)
XLA Modules:
  0.0 77.6 jit_solution(6662360486731361721)
XLA Ops:
  0.0 2.3 %shard_map.64 = (f32[392,384]{1,0:T(8,128)}, f32[384,384]{1,0:T(8,128)}) custom-call(s32[2]{0:T(128)} %bitcast.12, f32[2,384,384]{2,1,0:T(8,128)} %bitcast.10), custom_call_target="tpu_custom_call" | custom-call | tf_op jit(solution)/shard_map/pallas_call | solution.py:108
  2.3 2.4 %collective-permute-start.3 = (f32[392,384]{1,0:T(8,128)}, f32[392,384]{1,0:T(8,128)S(1)}, u32[]{:S(2)}, u32[]{:S(2)}) collective-permute-start(f32[392,384]{1,0:T(8,128)} %get-tuple-element.25.refs_2_), channel_id=1, source_target_pairs={{1,0},{2,1},{3,2},{5,4},{6,5},{7,6},{13,12},{14,13},{15,14},{10,8}... | collective-permute-start | bytes 1806344 | tf_op jit(solution)/shard_map/ppermute | solution.py:43
  4.7 1.3 %collective-permute-start.5 = (f32[392,384]{1,0:T(8,128)}, f32[392,384]{1,0:T(8,128)S(1)}, u32[]{:S(2)}, u32[]{:S(2)}) collective-permute-start(f32[392,384]{1,0:T(8,128)} %get-tuple-element.25.refs_2_), channel_id=1, source_target_pairs={{0,1},{1,3},{4,5},{5,6},{6,7},{8,9},{9,10},{10,11},{12,13},{13,14}... | collective-permute-start | bytes 1806344 | tf_op jit(solution)/shard_map/ppermute | solution.py:43
  6.0 2.7 %shard_map.65 = (f32[2,392,384]{2,1,0:T(8,128)}, f32[4,392,384]{2,1,0:T(8,128)}) custom-call(s32[2]{0:T(128)} %bitcast.13, f32[2,384,384]{2,1,0:T(8,128)} %bitcast.11), custom_call_target="tpu_custom_call" | custom-call | tf_op jit(solution)/shard_map/pallas_call | solution.py:90
  8.7 1.6 %collective-permute-start.2 = (f32[2,392,384]{2,1,0:T(8,128)}, f32[2,392,384]{2,1,0:T(8,128)S(1)}, u32[]{:S(2)}, u32[]{:S(2)}) collective-permute-start(f32[2,392,384]{2,1,0:T(8,128)} %get-tuple-element.24), channel_id=1, source_target_pairs={{0,8},{4,12},{8,0},{12,4},{1,9},{5,13},{9,1},{13,5},{2,10},{6,14},... | collective-permute-start | bytes 3612680 | tf_op jit(solution)/shard_map/ppermute | solution.py:369
  10.3 1.3 %collective-permute-start.1 = (f32[384,384]{1,0:T(8,128)}, f32[384,384]{1,0:T(8,128)S(1)}, u32[]{:S(2)}, u32[]{:S(2)}) collective-permute-start(f32[384,384]{1,0:T(8,128)} %get-tuple-element.19.refs_3_), channel_id=1, source_target_pairs={{0,1},{1,3},{4,5},{5,6},{6,7},{8,9},{9,10},{10,11},{12,13},{13,14}... | collective-permute-start | bytes 1769480 | tf_op jit(solution)/shard_map/ppermute | solution.py:43
  11.6 4.8 %collective-permute-start.4 = (f32[384,384]{1,0:T(8,128)}, f32[384,384]{1,0:T(8,128)}, u32[]{:S(2)}, u32[]{:S(2)}) collective-permute-start(f32[384,384]{1,0:T(8,128)} %get-tuple-element.19.refs_3_), channel_id=1, source_target_pairs={{1,0},{2,1},{3,2},{5,4},{6,5},{7,6},{13,12},{14,13},{15,14},{10,8}... | collective-permute-start | bytes 1769480 | tf_op jit(solution)/shard_map/ppermute | solution.py:43
  16.3 2.6 %collective-permute-done.3.refs_4_ = f32[392,384]{1,0:T(8,128)S(1)} collective-permute-done((f32[392,384]{1,0:T(8,128)}, f32[392,384]{1,0:T(8,128)S(1)}, u32[]{:S(2)}, u32[]{:S(2)}) %collective-permute-start.3) | collective-permute-done | bytes 602144 | tf_op jit(solution)/shard_map/ppermute | solution.py:43
  19.0 1.5 %collective-permute-start.6 = (f32[392,384]{1,0:T(8,128)S(1)}, f32[392,384]{1,0:T(8,128)}, u32[]{:S(2)}, u32[]{:S(2)}) collective-permute-start(f32[392,384]{1,0:T(8,128)S(1)} %collective-permute-done.3.refs_4_), channel_id=1, source_target_pairs={{1,0},{2,1},{5,4},{6,5},{10,9},{14,12},{17,16},{18,17},{21,20},{22... | collective-permute-start | bytes 1806344 | tf_op jit(solution)/shard_map/ppermute | solution.py:43
  20.4 3.8 %collective-permute-done.5.refs_6_ = f32[392,384]{1,0:T(8,128)S(1)} collective-permute-done((f32[392,384]{1,0:T(8,128)}, f32[392,384]{1,0:T(8,128)S(1)}, u32[]{:S(2)}, u32[]{:S(2)}) %collective-permute-start.5) | collective-permute-done | bytes 602144 | tf_op jit(solution)/shard_map/ppermute | solution.py:43
  24.3 1.5 %collective-permute-start.8 = (f32[392,384]{1,0:T(8,128)S(1)}, f32[392,384]{1,0:T(8,128)}, u32[]{:S(2)}, u32[]{:S(2)}) collective-permute-start(f32[392,384]{1,0:T(8,128)S(1)} %collective-permute-done.5.refs_6_), channel_id=1, source_target_pairs={{1,2},{5,6},{6,7},{9,10},{10,11},{13,15},{17,18},{21,22},{22,23},{... | collective-permute-start | bytes 1806344 | tf_op jit(solution)/shard_map/ppermute | solution.py:43
  25.8 1.2 %dynamic-slice_bitcast_fusion.plan_hbm = s32[7]{0:T(128)} fusion(s32[4,4,7]{2,1,0:T(4,128)} %constant.19.clone, s32[]{:T(128)S(6)} %select_n.6, s32[]{:T(128)S(6)} %select_n.7), kind=kLoop, calls=%fused_computation.1 | loop fusion | bytes 64 | tf_op jit(solution)/shard_map/squeeze | solution.py:376
  27.0 9.9 %collective-permute-done.1.refs_7_ = f32[384,384]{1,0:T(8,128)S(1)} collective-permute-done((f32[384,384]{1,0:T(8,128)}, f32[384,384]{1,0:T(8,128)S(1)}, u32[]{:S(2)}, u32[]{:S(2)}) %collective-permute-start.1) | collective-permute-done | bytes 589856 | tf_op jit(solution)/shard_map/ppermute | solution.py:43
  36.9 1.5 %collective-permute-start.9 = (f32[384,384]{1,0:T(8,128)S(1)}, f32[384,384]{1,0:T(8,128)}, u32[]{:S(2)}, u32[]{:S(2)}) collective-permute-start(f32[384,384]{1,0:T(8,128)S(1)} %collective-permute-done.1.refs_7_), channel_id=1, source_target_pairs={{1,2},{5,6},{6,7},{9,10},{10,11},{13,15},{17,18},{21,22},{22,23},{... | collective-permute-start | bytes 1769480 | tf_op jit(solution)/shard_map/ppermute | solution.py:43
  38.4 1.5 %collective-permute-start.7 = (f32[384,384]{1,0:T(8,128)}, f32[384,384]{1,0:T(8,128)}, u32[]{:S(2)}, u32[]{:S(2)}) collective-permute-start(f32[384,384]{1,0:T(8,128)} %collective-permute-done.4.refs_5_), channel_id=1, source_target_pairs={{1,0},{2,1},{5,4},{6,5},{10,9},{14,12},{17,16},{18,17},{21,20},{22... | collective-permute-start | bytes 1769480 | tf_op jit(solution)/shard_map/ppermute | solution.py:43
  39.9 1.5 %collective-permute-start.10 = (f32[392,384]{1,0:T(8,128)}, f32[392,384]{1,0:T(8,128)}, u32[]{:S(2)}, u32[]{:S(2)}) collective-permute-start(f32[392,384]{1,0:T(8,128)} %collective-permute-done.6.refs_8_), channel_id=1, source_target_pairs={{5,4},{9,8},{21,20},{25,24}} | collective-permute-start | bytes 1806344 | tf_op jit(solution)/shard_map/ppermute | solution.py:43
  41.4 0.0 collective-permute-done.8.refs_10_
  41.4 1.3 %collective-permute-start.11 = (f32[392,384]{1,0:T(8,128)}, f32[392,384]{1,0:T(8,128)}, u32[]{:S(2)}, u32[]{:S(2)}) collective-permute-start(f32[392,384]{1,0:T(8,128)} %collective-permute-done.8.refs_10_), channel_id=1, source_target_pairs={{2,3},{6,7},{18,19},{22,23}} | collective-permute-start | bytes 1806344 | tf_op jit(solution)/shard_map/ppermute | solution.py:43
  43.3 0.0 collective-permute-done.9.refs_11_
  43.3 1.3 %collective-permute-start.13 = (f32[384,384]{1,0:T(8,128)}, f32[384,384]{1,0:T(8,128)S(1)}, u32[]{:S(2)}, u32[]{:S(2)}) collective-permute-start(f32[384,384]{1,0:T(8,128)} %collective-permute-done.9.refs_11_), channel_id=1, source_target_pairs={{2,3},{6,7},{18,19},{22,23}} | collective-permute-start | bytes 1769480 | tf_op jit(solution)/shard_map/ppermute | solution.py:43
  44.6 0.0 collective-permute-done.7.refs_9_
  44.7 0.7 collective-permute-start.12
  45.4 0.0 collective-permute-done.2
  45.4 1.1 %constant_dynamic-update-slice_fusion.refs_0_ = f32[4,392,384]{2,1,0:T(8,128)} fusion(f32[4,392,384]{2,1,0:T(8,128)} %get-tuple-element.23, f32[2,392,384]{2,1,0:T(8,128)S(1)} %collective-permute-done.2), kind=kLoop, calls=%fused_computation | loop fusion | bytes 2408448 | tf_op jit(solution)/shard_map/dynamic_update_slice | solution.py:357
  46.5 8.4 %conditional.1 = (f32[4,392,384]{2,1,0:T(8,128)}) conditional(s32[]{:T(128)} %bitcast.6, () %tuple.15, f32[4,392,384]{2,1,0:T(8,128)} %constant_dynamic-update-slice_fusion.refs_0_), branch_computations={%region_0.0_spmd, %region_1.0_spmd} | conditional | bytes 9633840 | solution.py:359
  46.5 3.9 %collective-permute-start = (f32[4,392,384]{2,1,0:T(8,128)}, f32[4,392,384]{2,1,0:T(8,128)}, u32[]{:S(2)}, u32[]{:S(2)}) collective-permute-start(f32[4,392,384]{2,1,0:T(8,128)} %param.1), channel_id=1, source_target_pairs={{0,4},{4,0},{8,12},{12,8},{1,5},{5,1},{9,13},{13,9},{2,6},{6,2},{1... | collective-permute-start | bytes 7225352 | tf_op jit(solution)/shard_map/cond/branch_1_fun/ppermute | solution.py:358
  50.3 4.6 %collective-permute-done = f32[4,392,384]{2,1,0:T(8,128)} collective-permute-done((f32[4,392,384]{2,1,0:T(8,128)}, f32[4,392,384]{2,1,0:T(8,128)}, u32[]{:S(2)}, u32[]{:S(2)}) %collective-permute-start) | collective-permute-done | bytes 2408480 | tf_op jit(solution)/shard_map/cond/branch_1_fun/ppermute | solution.py:358
  54.9 6.1 %collective-permute-done.11.refs_13_ = f32[392,384]{1,0:T(8,128)} collective-permute-done((f32[392,384]{1,0:T(8,128)}, f32[392,384]{1,0:T(8,128)}, u32[]{:S(2)}, u32[]{:S(2)}) %collective-permute-start.11) | collective-permute-done | bytes 602144 | tf_op jit(solution)/shard_map/ppermute | solution.py:43
  61.1 4.9 %shard_map.66 = (f32[2,384,384]{2,1,0:T(8,128)}, s32[8]{0:T(128)}) custom-call(s32[7]{0:T(128)} %dynamic-slice_bitcast_fusion.plan_hbm, s32[2]{0:T(128)} %bitcast.15, f32[4,392,384]{2,1,0:T(8,128)} %constant_dynamic-update-slice_fusion.refs_0_, f32[4,392,384]{2,1,0:T(8,128)} %get-tuple-element.29.refs_1_, f32[392,384]{1,0:T(8,128)} %get-tuple-element.25.refs_2_, ...), custom_call_target="tpu_custom_call" | custom-call | flops 8153726976 | bytes 15335424 | tf_op jit(solution)/shard_map/pallas_call | solution.py:297
  65.9 7.5 %collective-permute-done.13.refs_3_ = f32[384,384]{1,0:T(8,128)S(1)} collective-permute-done((f32[384,384]{1,0:T(8,128)}, f32[384,384]{1,0:T(8,128)S(1)}, u32[]{:S(2)}, u32[]{:S(2)}) %collective-permute-start.13) | collective-permute-done | bytes 589856 | tf_op jit(solution)/shard_map/ppermute | solution.py:43
  73.4 0.7 copy-done
  74.1 3.5 %shard_map.67 = f32[2,384,384]{2,1,0:T(8,128)} custom-call(s32[8]{0:T(128)S(1)} %copy-done, f32[4,392,384]{2,1,0:T(8,128)} %constant_dynamic-update-slice_fusion.refs_0_, f32[4,392,384]{2,1,0:T(8,128)} %get-tuple-element.29.refs_1_, f32[384,384]{1,0:T(8,128)S(1)} %collective-permute-done.12.refs_2_, ...), custom_call_target="tpu_custom_call", output_to_operand_aliasing={{}: (5, {})} | custom-call | flops 1358954496 | bytes 3538944 | tf_op jit(solution)/shard_map/pallas_call | solution.py:334
  (11 shorter events, 0.0 us)
Async XLA Ops:
  2.3 16.7 %collective-permute-start.3 = (f32[392,384]{1,0:T(8,128)}, f32[392,384]{1,0:T(8,128)S(1)}, u32[]{:S(2)}, u32[]{:S(2)}) collective-permute-start(f32[392,384]{1,0:T(8,128)} %get-tuple-element.25.refs_2_), channel_id=1, source_target_pairs={{1,0},{2,1},{3,2},{5,4},{6,5},{7,6},{13,12},{14,13},{15,14},{10,8}... | collective-permute-start | bytes 1806344 | tf_op jit(solution)/shard_map/ppermute | solution.py:43
  4.7 19.5 %collective-permute-start.5 = (f32[392,384]{1,0:T(8,128)}, f32[392,384]{1,0:T(8,128)S(1)}, u32[]{:S(2)}, u32[]{:S(2)}) collective-permute-start(f32[392,384]{1,0:T(8,128)} %get-tuple-element.25.refs_2_), channel_id=1, source_target_pairs={{0,1},{1,3},{4,5},{5,6},{6,7},{8,9},{9,10},{10,11},{12,13},{13,14}... | collective-permute-start | bytes 1806344 | tf_op jit(solution)/shard_map/ppermute | solution.py:43
  8.7 36.6 %collective-permute-start.2 = (f32[2,392,384]{2,1,0:T(8,128)}, f32[2,392,384]{2,1,0:T(8,128)S(1)}, u32[]{:S(2)}, u32[]{:S(2)}) collective-permute-start(f32[2,392,384]{2,1,0:T(8,128)} %get-tuple-element.24), channel_id=1, source_target_pairs={{0,8},{4,12},{8,0},{12,4},{1,9},{5,13},{9,1},{13,5},{2,10},{6,14},... | collective-permute-start | bytes 3612680 | tf_op jit(solution)/shard_map/ppermute | solution.py:369
  10.3 26.6 %collective-permute-start.1 = (f32[384,384]{1,0:T(8,128)}, f32[384,384]{1,0:T(8,128)S(1)}, u32[]{:S(2)}, u32[]{:S(2)}) collective-permute-start(f32[384,384]{1,0:T(8,128)} %get-tuple-element.19.refs_3_), channel_id=1, source_target_pairs={{0,1},{1,3},{4,5},{5,6},{6,7},{8,9},{9,10},{10,11},{12,13},{13,14}... | collective-permute-start | bytes 1769480 | tf_op jit(solution)/shard_map/ppermute | solution.py:43
  11.6 26.8 %collective-permute-start.4 = (f32[384,384]{1,0:T(8,128)}, f32[384,384]{1,0:T(8,128)}, u32[]{:S(2)}, u32[]{:S(2)}) collective-permute-start(f32[384,384]{1,0:T(8,128)} %get-tuple-element.19.refs_3_), channel_id=1, source_target_pairs={{1,0},{2,1},{3,2},{5,4},{6,5},{7,6},{13,12},{14,13},{15,14},{10,8}... | collective-permute-start | bytes 1769480 | tf_op jit(solution)/shard_map/ppermute | solution.py:43
  19.0 27.5 %copy-start.1 = (f32[392,384]{1,0:T(8,128)}, f32[392,384]{1,0:T(8,128)S(1)}, u32[]{:S(2)}) copy-start(f32[392,384]{1,0:T(8,128)S(1)} %collective-permute-done.3.refs_4_) | copy-start | bytes 1806340
  19.0 20.9 %collective-permute-start.6 = (f32[392,384]{1,0:T(8,128)S(1)}, f32[392,384]{1,0:T(8,128)}, u32[]{:S(2)}, u32[]{:S(2)}) collective-permute-start(f32[392,384]{1,0:T(8,128)S(1)} %collective-permute-done.3.refs_4_), channel_id=1, source_target_pairs={{1,0},{2,1},{5,4},{6,5},{10,9},{14,12},{17,16},{18,17},{21,20},{22... | collective-permute-start | bytes 1806344 | tf_op jit(solution)/shard_map/ppermute | solution.py:43
  24.3 19.1 %copy-start.2 = (f32[392,384]{1,0:T(8,128)}, f32[392,384]{1,0:T(8,128)S(1)}, u32[]{:S(2)}) copy-start(f32[392,384]{1,0:T(8,128)S(1)} %collective-permute-done.5.refs_6_) | copy-start | bytes 1806340
  24.3 17.1 %collective-permute-start.8 = (f32[392,384]{1,0:T(8,128)S(1)}, f32[392,384]{1,0:T(8,128)}, u32[]{:S(2)}, u32[]{:S(2)}) collective-permute-start(f32[392,384]{1,0:T(8,128)S(1)} %collective-permute-done.5.refs_6_), channel_id=1, source_target_pairs={{1,2},{5,6},{6,7},{9,10},{10,11},{13,15},{17,18},{21,22},{22,23},{... | collective-permute-start | bytes 1806344 | tf_op jit(solution)/shard_map/ppermute | solution.py:43
  36.9 7.7 %copy-start.3 = (f32[384,384]{1,0:T(8,128)}, f32[384,384]{1,0:T(8,128)S(1)}, u32[]{:S(2)}) copy-start(f32[384,384]{1,0:T(8,128)S(1)} %collective-permute-done.1.refs_7_) | copy-start | bytes 1769476
  36.9 6.4 %collective-permute-start.9 = (f32[384,384]{1,0:T(8,128)S(1)}, f32[384,384]{1,0:T(8,128)}, u32[]{:S(2)}, u32[]{:S(2)}) collective-permute-start(f32[384,384]{1,0:T(8,128)S(1)} %collective-permute-done.1.refs_7_), channel_id=1, source_target_pairs={{1,2},{5,6},{6,7},{9,10},{10,11},{13,15},{17,18},{21,22},{22,23},{... | collective-permute-start | bytes 1769480 | tf_op jit(solution)/shard_map/ppermute | solution.py:43
  38.4 6.3 %collective-permute-start.7 = (f32[384,384]{1,0:T(8,128)}, f32[384,384]{1,0:T(8,128)}, u32[]{:S(2)}, u32[]{:S(2)}) collective-permute-start(f32[384,384]{1,0:T(8,128)} %collective-permute-done.4.refs_5_), channel_id=1, source_target_pairs={{1,0},{2,1},{5,4},{6,5},{10,9},{14,12},{17,16},{18,17},{21,20},{22... | collective-permute-start | bytes 1769480 | tf_op jit(solution)/shard_map/ppermute | solution.py:43
  39.9 15.1 %collective-permute-start.10 = (f32[392,384]{1,0:T(8,128)}, f32[392,384]{1,0:T(8,128)}, u32[]{:S(2)}, u32[]{:S(2)}) collective-permute-start(f32[392,384]{1,0:T(8,128)} %collective-permute-done.6.refs_8_), channel_id=1, source_target_pairs={{5,4},{9,8},{21,20},{25,24}} | collective-permute-start | bytes 1806344 | tf_op jit(solution)/shard_map/ppermute | solution.py:43
  41.4 19.7 %collective-permute-start.11 = (f32[392,384]{1,0:T(8,128)}, f32[392,384]{1,0:T(8,128)}, u32[]{:S(2)}, u32[]{:S(2)}) collective-permute-start(f32[392,384]{1,0:T(8,128)} %collective-permute-done.8.refs_10_), channel_id=1, source_target_pairs={{2,3},{6,7},{18,19},{22,23}} | collective-permute-start | bytes 1806344 | tf_op jit(solution)/shard_map/ppermute | solution.py:43
  43.3 30.1 %collective-permute-start.13 = (f32[384,384]{1,0:T(8,128)}, f32[384,384]{1,0:T(8,128)S(1)}, u32[]{:S(2)}, u32[]{:S(2)}) collective-permute-start(f32[384,384]{1,0:T(8,128)} %collective-permute-done.9.refs_11_), channel_id=1, source_target_pairs={{2,3},{6,7},{18,19},{22,23}} | collective-permute-start | bytes 1769480 | tf_op jit(solution)/shard_map/ppermute | solution.py:43
  44.7 28.7 %collective-permute-start.12 = (f32[384,384]{1,0:T(8,128)}, f32[384,384]{1,0:T(8,128)S(1)}, u32[]{:S(2)}, u32[]{:S(2)}) collective-permute-start(f32[384,384]{1,0:T(8,128)} %collective-permute-done.7.refs_9_), channel_id=1, source_target_pairs={{5,4},{9,8},{21,20},{25,24}} | collective-permute-start | bytes 1769480 | tf_op jit(solution)/shard_map/ppermute | solution.py:43
  46.5 8.4 %collective-permute-start = (f32[4,392,384]{2,1,0:T(8,128)}, f32[4,392,384]{2,1,0:T(8,128)}, u32[]{:S(2)}, u32[]{:S(2)}) collective-permute-start(f32[4,392,384]{2,1,0:T(8,128)} %param.1), channel_id=1, source_target_pairs={{0,4},{4,0},{8,12},{12,8},{1,5},{5,1},{9,13},{13,9},{2,6},{6,2},{1... | collective-permute-start | bytes 7225352 | tf_op jit(solution)/shard_map/cond/branch_1_fun/ppermute | solution.py:358
  73.4 0.7 copy-start
